TPU v7x, 512 devices: a whole 4x8x8 slice. The times are simulated.
512 devices in a mesh: group: 16 (over x_lo, z), tile: 32 (over x_hi, y, core).
Axes of the slice: x: 4 (x_hi: 2, x_lo: 2; x = x_hi * 2 + x_lo), y: 8, z: 8, core: 2. Of those that a mesh axis runs over, the one named last changes fastest.
Arguments:
- initial_state: float32 [48, 2, 128, 384], P(None, None, 'tile'), may hold values from -3 to 3
- perturbation: float32 [16, 48, 2, 128, 384], P('group', None, None, 'tile'), may hold values from -16 to 16
- land_sea: int32 [128, 384], P('tile'), may hold values 0 or 1
- relax_level: int32 [128, 384], P('tile'), may hold values from 0 to 3
- vertical_mix: float32 [48], replicated, may hold values from 0.1 to 2
Outputs:
- adjoint_field: float32 [16, 48, 2, 128, 384], P('group', None, None, 'tile')
- gram: float32 [16, 16], P('group')
All inputs are finite; a program needn't handle non-finite values. No bound on the sum of `land_sea` on one device may be relied on, other than what follows from the above.
Results may differ from a plain program's by a relative error of at most 0.00024.
Values sent between devices are 32-bit elements; how exact they have to be, the bound alone decides.
No kernel may reach another device: no remote copies, remote signals or barrier semaphores. Data moves between devices by JAX's collectives and lax.ppermute only.
A program may use at most 64 MiB of HBM per device.

v0:
```python
import jax
import jax.numpy as jnp
from jax import lax
from jax.sharding import PartitionSpec as P

STEPS = 3


advection = 0.2
diffusion = 0.1
drag_rate = 0.3
relaxation = 0.125


def padded_2(cells, sides, width):
    for axis, dim in sides:
        count = lax.axis_size(axis)
        ends = count - 1
        head = lax.slice_in_dim(cells, 0, width, axis=dim)
        tail = lax.slice_in_dim(cells, cells.shape[dim] - width, cells.shape[dim], axis=dim)
        cells = jnp.concatenate(
            [
                lax.ppermute(tail, axis, [(i, (i + 1) % count) for i in range(ends)]),
                cells,
                lax.ppermute(head, axis, [((i + 1) % count, i) for i in range(ends)]),
            ],
            axis=dim,
        )
    return cells


def row_slope(padded):
    return 0.5 * (padded[:, :, 2:] - padded[:, :, :-2])


def laplace(padded, left, right):
    centre = padded[:, :, 1:-1]
    widened = jnp.concatenate([left, centre, right], axis=3)
    return (
        padded[:, :, 2:] + padded[:, :, :-2] + widened[..., 2:] + widened[..., :-2] - 4.0 * centre
    )


def mixing_inverse(mixing):
    nothing = jnp.zeros((1,), jnp.float32)
    upper_band = jnp.concatenate([-mixing[:-1], nothing])
    lower_band = jnp.concatenate([nothing, -mixing[:-1]])
    diagonal_band = 1.0 + mixing + jnp.concatenate([nothing, mixing[:-1]])
    identity = jnp.eye(mixing.shape[0], dtype=jnp.float32)
    return lax.linalg.tridiagonal_solve(lower_band, diagonal_band, upper_band, identity)


def column_solve(columns, inverse_mix):
    layout = columns.shape
    solved = jnp.dot(
        inverse_mix,
        columns.reshape(layout[0], -1),
        precision=lax.Precision.HIGHEST,
        preferred_element_type=jnp.float32,
    )
    return solved.reshape(layout)


def flat_rims(padded):
    blank = jnp.zeros(padded.shape[:2] + (padded.shape[2] - 2, 1), jnp.float32)
    return (padded, blank, blank)


def state_halo(field):
    return flat_rims(padded_2(field, (("tile", 2),), 1))


def tangent_halo(field):
    return flat_rims(padded_2(field, (("tile", 2),), 1))


def adjoint_halo(field):
    return flat_rims(padded_2(field, (("tile", 2),), 1))


def adjoint_step(adjoint, zonal_wind, slopes, landmask, nudging, inverse_mix, edges):
    backed = column_solve(adjoint, inverse_mix) * nudging
    back_u = backed[:, 0:1]
    back_t = backed[:, 1:2]
    stacked = jnp.concatenate([backed, zonal_wind * backed], axis=1)
    padded, left, right = edges(stacked)
    carried = row_slope(padded[:, 2:])
    spread = laplace(padded[:, :2], left[:, :2], right[:, :2])
    adj_u = (
        back_u
        - advection * back_u * slopes[:, 0:1]
        + advection * carried[:, 0:1]
        + diffusion * spread[:, 0:1]
        - drag_rate * landmask * back_u
        - advection * back_t * slopes[:, 1:2]
    )
    adj_t = back_t + advection * carried[:, 1:2] + diffusion * spread[:, 1:2]
    return jnp.concatenate([adj_u, adj_t], axis=1)


def per_device(initial_state, perturbation, land_sea, relax_level, vertical_mix):
    landmask = land_sea.astype(jnp.float32)
    nudging = 1.0 - relaxation * relax_level.astype(jnp.float32)
    select = (jnp.arange(2) == 0).astype(jnp.float32)[None, :, None, None]
    inverse_mix = mixing_inverse(vertical_mix)
    current = initial_state
    tangent = perturbation[0]
    history = []
    for position in range(STEPS):
        state_pad, state_left, state_right = state_halo(current)
        tangent_pad, tangent_left, tangent_right = tangent_halo(tangent)
        slopes = row_slope(state_pad)
        zonal_wind = current[:, 0:1]
        history.append((zonal_wind, slopes))
        if position + 1 < STEPS:
            updated = (
                current
                - advection * zonal_wind * slopes
                + diffusion * laplace(state_pad, state_left, state_right)
                - drag_rate * landmask * select * current
            )
            current = column_solve(updated * nudging, inverse_mix)
        changed = (
            tangent
            - advection * (tangent[:, 0:1] * slopes + zonal_wind * row_slope(tangent_pad))
            + diffusion * laplace(tangent_pad, tangent_left, tangent_right)
            - drag_rate * landmask * select * tangent
        )
        tangent = column_solve(changed * nudging, inverse_mix)
    adjoint = tangent
    for position in reversed(range(STEPS)):
        zonal_wind, slopes = history[position]
        adjoint = adjoint_step(
            adjoint, zonal_wind, slopes, landmask, nudging, inverse_mix, adjoint_halo
        )
    adjoint_field = adjoint[None]
    cell_count = adjoint.size * lax.axis_size("tile")
    values = lax.map(
        lambda member_row: jnp.sum(member_row * adjoint),
        lax.all_gather(adjoint_field, "group", axis=0, tiled=True),
    )
    whole_row = lax.psum(values, "tile")
    gram = whole_row[None] / cell_count
    return (adjoint_field, gram)


def solution(mesh):
    placed = (
        P(None, None, "tile", None),
        P("group", None, None, "tile", None),
        P("tile", None),
        P("tile", None),
        P(),
    )
    return jax.shard_map(
        per_device,
        mesh=mesh,
        in_specs=placed,
        out_specs=(P("group", None, None, "tile", None), P("group", None)),
        check_vma=False,
    )
```

profile of v0, /device:TPU:1, one launch (start us, length us, event | category | flops | bytes accessed | tf_op | source)
XLA Modules:
  0.0 530.2 jit_solution(14028871688670945358)
XLA Ops:
  7.2 1.2 copy.23
  8.4 8.8 %collective-permute-start = (f32[48,2,1,384]{3,0,2,1:T(8,128)S(1)}, f32[48,2,1,384]{3,0,2,1:T(8,128)S(1)}, u32[]{:S(2)}, u32[]{:S(2)}) collective-permute-start(f32[48,2,1,384]{3,0,2,1:T(8,128)S(1)} %get-tuple-element.223), channel_id=1, source_target_pairs={{1,0},{2,1},{3,2},{4,3},{5,4},{6,5},{7,6},{8,7},{9,8},{10,9},{11,1... | collective-permute-start | bytes 442376 | tf_op jit(solution)/shard_map/ppermute | solution.py:25
  17.2 1.9 collective-permute-start.1
  19.1 1.2 copy.75
  20.4 2.4 collective-permute-start.2
  22.8 3.2 collective-permute-start.3
  121.4 30.1 %fusion.146 = (f32[1,48]{1,0:T(1,128)S(1)}, f32[48]{0:T(128)S(1)}, f32[48]{0:T(128)S(1)}, f32[48]{0:T(128)S(1)}, f32[48]{0:T(128)S(1)}, /*index=5*/f32[48]{0:T(1...) fusion(f32[]{:T(128)S(6)} %div.4795, ...), kind=kLoop, calls=%fused_computation.376 | loop fusion | flops 6912 | bytes 11904 | tf_op jit(solution)/shard_map/while/body/broadcast_in_dim | solution.py:50
  151.5 22.5 %subtract_divide_fusion = (f32[1,48]{1,0:T(1,128)S(1)}, f32[1,48]{1,0:T(1,128)S(1)}, f32[1,48]{1,0:T(1,128)S(1)}, f32[1,48]{1,0:T(1,128)S(1)}, f32[1,48]{1,0:T(1...) fusion(f32[48,48]{1,0:T(8,128)S(1)} %fusion.97, ...), kind=kLoop, calls=%fused_computation.339 | loop fusion | flops 5184 | bytes 14304 | tf_op jit(solution)/shard_map/eval_jaxpr/div | solution.py:50
  175.9 4.8 multiply_subtract_fusion.4
  180.7 2.2 concatenate.166
  187.1 1.4 fusion.15
  190.9 1.9 collective-permute-start.6
  192.8 3.6 collective-permute-start.7
  196.4 1.9 collective-permute-start.4
  198.4 3.6 collective-permute-start.5
  202.9 1.2 collective-permute-done.5
  204.1 1.5 fusion.66
  208.6 1.4 fusion.29
  211.5 1.9 collective-permute-start.10
  213.4 4.4 collective-permute-start.11
  217.8 2.1 collective-permute-start.8
  219.9 3.6 collective-permute-start.9
  224.5 1.2 collective-permute-done.9
  225.7 1.5 broadcast_multiply_fusion.3
  229.2 1.1 broadcast_multiply_fusion.2
  230.4 1.9 collective-permute-start.12
  232.3 4.4 collective-permute-start.13
  236.7 2.5 collective-permute-done.12
  239.2 1.2 collective-permute-done.13
  242.5 1.9 collective-permute-start.14
  244.4 4.4 collective-permute-start.15
  248.8 2.5 collective-permute-done.14
  251.3 1.2 collective-permute-done.15
  254.6 1.9 collective-permute-start.16
  256.5 4.4 collective-permute-start.17
  260.9 2.5 collective-permute-done.16
  263.4 1.2 collective-permute-done.17
  266.1 1.3 copy.47
  268.5 144.6 %all-gather.3.cloned.1.call-done = f32[768,2,4,384]{3,0,2,1:T(8,128)} async-done(((f32[48,2,4,384]{3,0,2,1:T(8,128)}), f32[768,2,4,384]{3,0,2,1:T(8,128)}) %all-gather.3.cloned.1.call-update) | async-done | bytes 9437200 | tf_op jit(solution)/shard_map/all_gather | solution.py:140
  413.1 44.8 %while.2 = (s32[]{:T(128)}, f32[16]{0:T(128)S(1)}, f32[16,48,2,4,384]{4,1,0,3,2:T(8,128)}, f32[48,2,4,384]{3,2,1,0:T(4,128)S(1)}, s32[]{:T(128)}) while((s32[]{:T(128)}, f32[16]{0:T(128)S(1)}, f32[16,48,2,4,384]{4,1,0,3,2:T(8,128)}, f32[48,2,4,384]{3,2,1,0:T(4,128)S(1)}, s32[]{:T(128)}) %tuple.238), condition=%wide.region_2.3_spmd, body=%wide.region_0.2_spmd.sunk | while | flops 294913 | bytes 2359377 | solution.py:138
  418.7 1.1 constant_dynamic-slice_fusion.2
  421.5 1.1 constant_dynamic-slice_fusion.2
  429.9 1.1 constant_dynamic-slice_fusion.2
  438.3 1.1 constant_dynamic-slice_fusion.2
  446.7 1.1 constant_dynamic-slice_fusion.2
  449.5 1.1 constant_dynamic-slice_fusion.2
  455.1 1.1 constant_dynamic-slice_fusion.2
  457.9 65.0 %psum.7 = f32[16]{0:T(128)S(1)} all-reduce(f32[16]{0:T(128)S(1)} %get-tuple-element.58), channel_id=1, replica_groups=mesh['group'=16,'tile'=32] {'tile'}, use_global_device_ids=true, to_apply=%region_3.4 | all-reduce | flops 16 | bytes 128 | tf_op jit(solution)/shard_map/psum | solution.py:142
  (134 shorter events, 67.3 us)
Async XLA Ops:
  7.2 405.9 %all-gather.3.cloned.1.call-start = ((), (), s32[]{:S(2)}) async-start(), calls=%async_computation | async-start | bytes 10027008 | tf_op jit(solution)/shard_map/all_gather | solution.py:140
  8.4 175.2 %collective-permute-start = (f32[48,2,1,384]{3,0,2,1:T(8,128)S(1)}, f32[48,2,1,384]{3,0,2,1:T(8,128)S(1)}, u32[]{:S(2)}, u32[]{:S(2)}) collective-permute-start(f32[48,2,1,384]{3,0,2,1:T(8,128)S(1)} %get-tuple-element.223), channel_id=1, source_target_pairs={{1,0},{2,1},{3,2},{4,3},{5,4},{6,5},{7,6},{8,7},{9,8},{10,9},{11,1... | collective-permute-start | bytes 442376 | tf_op jit(solution)/shard_map/ppermute | solution.py:25
  17.2 166.4 %collective-permute-start.1 = (f32[48,2,1,384]{3,0,2,1:T(8,128)S(1)}, f32[48,2,1,384]{3,0,2,1:T(8,128)S(1)}, u32[]{:S(2)}, u32[]{:S(2)}) collective-permute-start(f32[48,2,1,384]{3,0,2,1:T(8,128)S(1)} %get-tuple-element.222), channel_id=1, source_target_pairs={{0,1},{1,2},{2,3},{3,4},{4,5},{5,6},{6,7},{7,8},{8,9},{9,10},{10,1... | collective-permute-start | bytes 442376 | tf_op jit(solution)/shard_map/ppermute | solution.py:23
  20.4 163.3 %collective-permute-start.2 = (f32[48,2,1,384]{3,0,2,1:T(8,128)S(1)}, f32[48,2,1,384]{3,0,2,1:T(8,128)S(1)}, u32[]{:S(2)}, u32[]{:S(2)}) collective-permute-start(f32[48,2,1,384]{3,0,2,1:T(8,128)S(1)} %get-tuple-element.219), channel_id=1, source_target_pairs={{1,0},{2,1},{3,2},{4,3},{5,4},{6,5},{7,6},{8,7},{9,8},{10,9},{11,1... | collective-permute-start | bytes 442376 | tf_op jit(solution)/shard_map/ppermute | solution.py:25
  22.8 160.8 %collective-permute-start.3 = (f32[48,2,1,384]{3,0,2,1:T(8,128)S(1)}, f32[48,2,1,384]{3,0,2,1:T(8,128)S(1)}, u32[]{:S(2)}, u32[]{:S(2)}) collective-permute-start(f32[48,2,1,384]{3,0,2,1:T(8,128)S(1)} %get-tuple-element.218), channel_id=1, source_target_pairs={{0,1},{1,2},{2,3},{3,4},{4,5},{5,6},{6,7},{7,8},{8,9},{9,10},{10,1... | collective-permute-start | bytes 442376 | tf_op jit(solution)/shard_map/ppermute | solution.py:23
  183.6 1.0 copy-start.1
  190.9 11.2 %collective-permute-start.6 = (f32[48,2,1,384]{3,0,2,1:T(8,128)}, f32[48,2,1,384]{3,0,2,1:T(8,128)S(1)}, u32[]{:S(2)}, u32[]{:S(2)}) collective-permute-start(f32[48,2,1,384]{3,0,2,1:T(8,128)} %get-tuple-element.217), channel_id=1, source_target_pairs={{1,0},{2,1},{3,2},{4,3},{5,4},{6,5},{7,6},{8,7},{9,8},{10,9},{11,1... | collective-permute-start | bytes 442376 | tf_op jit(solution)/shard_map/ppermute | solution.py:25
  192.8 9.3 %collective-permute-start.7 = (f32[48,2,1,384]{3,0,2,1:T(8,128)}, f32[48,2,1,384]{3,0,2,1:T(8,128)S(1)}, u32[]{:S(2)}, u32[]{:S(2)}) collective-permute-start(f32[48,2,1,384]{3,0,2,1:T(8,128)} %get-tuple-element.216), channel_id=1, source_target_pairs={{0,1},{1,2},{2,3},{3,4},{4,5},{5,6},{6,7},{7,8},{8,9},{9,10},{10,1... | collective-permute-start | bytes 442376 | tf_op jit(solution)/shard_map/ppermute | solution.py:23
  196.4 6.5 %collective-permute-start.4 = (f32[48,2,1,384]{3,0,2,1:T(8,128)S(1)}, f32[48,2,1,384]{3,0,2,1:T(8,128)S(1)}, u32[]{:S(2)}, u32[]{:S(2)}) collective-permute-start(f32[48,2,1,384]{3,0,2,1:T(8,128)S(1)} %get-tuple-element.221), channel_id=1, source_target_pairs={{1,0},{2,1},{3,2},{4,3},{5,4},{6,5},{7,6},{8,7},{9,8},{10,9},{11,1... | collective-permute-start | bytes 442376 | tf_op jit(solution)/shard_map/ppermute | solution.py:25
  198.4 5.7 %collective-permute-start.5 = (f32[48,2,1,384]{3,0,2,1:T(8,128)S(1)}, f32[48,2,1,384]{3,0,2,1:T(8,128)S(1)}, u32[]{:S(2)}, u32[]{:S(2)}) collective-permute-start(f32[48,2,1,384]{3,0,2,1:T(8,128)S(1)} %get-tuple-element.220), channel_id=1, source_target_pairs={{0,1},{1,2},{2,3},{3,4},{4,5},{5,6},{6,7},{7,8},{8,9},{9,10},{10,1... | collective-permute-start | bytes 442376 | tf_op jit(solution)/shard_map/ppermute | solution.py:23
  204.1 1.5 copy-start.2
  211.5 12.8 %collective-permute-start.10 = (f32[48,2,1,384]{3,0,2,1:T(8,128)}, f32[48,2,1,384]{3,0,2,1:T(8,128)S(1)}, u32[]{:S(2)}, u32[]{:S(2)}) collective-permute-start(f32[48,2,1,384]{3,0,2,1:T(8,128)} %get-tuple-element.215), channel_id=1, source_target_pairs={{1,0},{2,1},{3,2},{4,3},{5,4},{6,5},{7,6},{8,7},{9,8},{10,9},{11,1... | collective-permute-start | bytes 442376 | tf_op jit(solution)/shard_map/ppermute | solution.py:25
  213.4 10.9 %collective-permute-start.11 = (f32[48,2,1,384]{3,0,2,1:T(8,128)}, f32[48,2,1,384]{3,0,2,1:T(8,128)S(1)}, u32[]{:S(2)}, u32[]{:S(2)}) collective-permute-start(f32[48,2,1,384]{3,0,2,1:T(8,128)} %get-tuple-element.214), channel_id=1, source_target_pairs={{0,1},{1,2},{2,3},{3,4},{4,5},{5,6},{6,7},{7,8},{8,9},{9,10},{10,1... | collective-permute-start | bytes 442376 | tf_op jit(solution)/shard_map/ppermute | solution.py:23
  217.8 6.6 %collective-permute-start.8 = (f32[48,2,1,384]{3,0,2,1:T(8,128)S(1)}, f32[48,2,1,384]{3,0,2,1:T(8,128)S(1)}, u32[]{:S(2)}, u32[]{:S(2)}) collective-permute-start(f32[48,2,1,384]{3,0,2,1:T(8,128)S(1)} %get-tuple-element.212), channel_id=1, source_target_pairs={{1,0},{2,1},{3,2},{4,3},{5,4},{6,5},{7,6},{8,7},{9,8},{10,9},{11,1... | collective-permute-start | bytes 442376 | tf_op jit(solution)/shard_map/ppermute | solution.py:25
  219.9 5.7 %collective-permute-start.9 = (f32[48,2,1,384]{3,0,2,1:T(8,128)S(1)}, f32[48,2,1,384]{3,0,2,1:T(8,128)S(1)}, u32[]{:S(2)}, u32[]{:S(2)}) collective-permute-start(f32[48,2,1,384]{3,0,2,1:T(8,128)S(1)} %get-tuple-element.213), channel_id=1, source_target_pairs={{0,1},{1,2},{2,3},{3,4},{4,5},{5,6},{6,7},{7,8},{8,9},{9,10},{10,1... | collective-permute-start | bytes 442376 | tf_op jit(solution)/shard_map/ppermute | solution.py:23
  229.2 12.6 %copy-start = (f32[48,4,384]{2,0,1:T(8,128)S(1)}, f32[48,4,384]{2,0,1:T(8,128)}, u32[]{:S(2)}) copy-start(f32[48,4,384]{2,0,1:T(8,128)} %get-tuple-element.210) | copy-start | bytes 884740
  230.4 8.8 %collective-permute-start.12 = (f32[48,4,1,384]{3,0,2,1:T(8,128)S(1)}, f32[48,4,1,384]{3,0,2,1:T(8,128)S(1)}, u32[]{:S(2)}, u32[]{:S(2)}) collective-permute-start(f32[48,4,1,384]{3,0,2,1:T(8,128)S(1)} %get-tuple-element.198), channel_id=1, source_target_pairs={{1,0},{2,1},{3,2},{4,3},{5,4},{6,5},{7,6},{8,7},{9,8},{10,9},{11,1... | collective-permute-start | bytes 884744 | tf_op jit(solution)/shard_map/ppermute | solution.py:25
  232.3 8.0 %collective-permute-start.13 = (f32[48,4,1,384]{3,0,2,1:T(8,128)S(1)}, f32[48,4,1,384]{3,0,2,1:T(8,128)S(1)}, u32[]{:S(2)}, u32[]{:S(2)}) collective-permute-start(f32[48,4,1,384]{3,0,2,1:T(8,128)S(1)} %get-tuple-element.199), channel_id=1, source_target_pairs={{0,1},{1,2},{2,3},{3,4},{4,5},{5,6},{6,7},{7,8},{8,9},{9,10},{10,1... | collective-permute-start | bytes 884744 | tf_op jit(solution)/shard_map/ppermute | solution.py:23
  242.5 8.8 %collective-permute-start.14 = (f32[48,4,1,384]{3,0,2,1:T(8,128)S(1)}, f32[48,4,1,384]{3,0,2,1:T(8,128)S(1)}, u32[]{:S(2)}, u32[]{:S(2)}) collective-permute-start(f32[48,4,1,384]{3,0,2,1:T(8,128)S(1)} %get-tuple-element.196), channel_id=1, source_target_pairs={{1,0},{2,1},{3,2},{4,3},{5,4},{6,5},{7,6},{8,7},{9,8},{10,9},{11,1... | collective-permute-start | bytes 884744 | tf_op jit(solution)/shard_map/ppermute | solution.py:25
  244.4 8.0 %collective-permute-start.15 = (f32[48,4,1,384]{3,0,2,1:T(8,128)S(1)}, f32[48,4,1,384]{3,0,2,1:T(8,128)S(1)}, u32[]{:S(2)}, u32[]{:S(2)}) collective-permute-start(f32[48,4,1,384]{3,0,2,1:T(8,128)S(1)} %get-tuple-element.197), channel_id=1, source_target_pairs={{0,1},{1,2},{2,3},{3,4},{4,5},{5,6},{6,7},{7,8},{8,9},{9,10},{10,1... | collective-permute-start | bytes 884744 | tf_op jit(solution)/shard_map/ppermute | solution.py:23
  254.6 8.8 %collective-permute-start.16 = (f32[48,4,1,384]{3,0,2,1:T(8,128)S(1)}, f32[48,4,1,384]{3,0,2,1:T(8,128)S(1)}, u32[]{:S(2)}, u32[]{:S(2)}) collective-permute-start(f32[48,4,1,384]{3,0,2,1:T(8,128)S(1)} %get-tuple-element.194), channel_id=1, source_target_pairs={{1,0},{2,1},{3,2},{4,3},{5,4},{6,5},{7,6},{8,7},{9,8},{10,9},{11,1... | collective-permute-start | bytes 884744 | tf_op jit(solution)/shard_map/ppermute | solution.py:25
  256.5 8.0 %collective-permute-start.17 = (f32[48,4,1,384]{3,0,2,1:T(8,128)S(1)}, f32[48,4,1,384]{3,0,2,1:T(8,128)S(1)}, u32[]{:S(2)}, u32[]{:S(2)}) collective-permute-start(f32[48,4,1,384]{3,0,2,1:T(8,128)S(1)} %get-tuple-element.195), channel_id=1, source_target_pairs={{0,1},{1,2},{2,3},{3,4},{4,5},{5,6},{6,7},{7,8},{8,9},{9,10},{10,1... | collective-permute-start | bytes 884744 | tf_op jit(solution)/shard_map/ppermute | solution.py:23
Sparse Core Ops, SparseCore 0:
  266.2 146.7 all-gather.2
where the time goes:
time: 536 us; the launch traced here: 530 us
  waiting for transfers between devices  159 us (30%)
  between operations  104 us (19%)
  other arithmetic  90.6 us (17%)
  blocking collectives  65 us (12%)
  starting transfers between devices  58.4 us (11%)
  local copies, waits for them, and re-layouts  48.3 us (9%)
  matrix products  5.36 us (1%)
    all_gather x1, waiting for transfers between devices, per_device(): lax.all_gather(adjoint_field, 'group', axis=0, tiled=True)  145 us
    psum x1, blocking collectives, per_device(): whole_row = lax.psum(values, 'tile')  65 us
    ppermute x9, starting transfers between devices, padded_2(): lax.ppermute(tail, axis, [(i, (i + 1) % count) for i in range(ends)])  33.5 us
    broadcast_in_dim x3, other arithmetic, mixing_inverse(): lax.linalg.tridiagonal_solve(lower_band, diagonal_band, upper_band, ident...  31.2 us
    ppermute x9, starting transfers between devices, padded_2(): lax.ppermute(head, axis, [((i + 1) % count, i) for i in range(ends)])  24.8 us
    div x1, other arithmetic, mixing_inverse(): lax.linalg.tridiagonal_solve(lower_band, diagonal_band, upper_band, ident...  22.5 us
    dynamic_slice x16, local copies, waits for them, and re-layouts, per_device(): lax.map(lambda member_row: jnp.sum(member_row * adjoint), lax.all_gather(...  17.7 us
    reduce_sum x16, other arithmetic, per_device(): jnp.sum(member_row * adjoint)  15.2 us
  transfers between devices with their start and end apart: 19, of which 11 were waited for; matrix products, arithmetic and copies ran while one was open for 14% of the time, Pallas kernels for 0%

commit v1 on v0

v1 whole, which is shorter than its diff:
```python
import functools

import jax
import jax.numpy as jnp
from jax import lax
from jax.experimental import pallas as pl
from jax.experimental.pallas import tpu as pltpu
from jax.sharding import PartitionSpec as P

advection = 0.2
diffusion = 0.1
drag_rate = 0.3
relaxation = 0.125

VMEM_LIMIT = 24 * 2**20

ANY = pl.BlockSpec(memory_space=pl.ANY)
VMEM = pl.BlockSpec(memory_space=pltpu.VMEM)
SMEM = pl.BlockSpec(memory_space=pltpu.SMEM)


def run(kernel, out_shape, in_specs, out_specs, scratch, flops=0, nbytes=0):
    return pl.pallas_call(
        kernel,
        out_shape=out_shape,
        in_specs=in_specs,
        out_specs=out_specs,
        scratch_shapes=scratch,
        compiler_params=pltpu.CompilerParams(vmem_limit_bytes=VMEM_LIMIT),
        cost_estimate=pl.CostEstimate(flops=flops, bytes_accessed=nbytes, transcendentals=0),
    )


def f32(*shape):
    return jax.ShapeDtypeStruct(shape, jnp.float32)


def start_all(copies):
    for copy in copies:
        copy.start()


def wait_all(copies):
    for copy in copies:
        copy.wait()


def pack_rows(src, dst, sems):
    lev, fields, rows, _ = src.shape
    return [
        pltpu.make_async_copy(
            src.at[:, f, r, :], dst.at[pl.ds((f * rows + r) * lev, lev), :], sems.at[f * rows + r]
        )
        for f in range(fields)
        for r in range(rows)
    ]


def pack_state_kernel(x, land, relax, out, sems):
    copies = pack_rows(x, out, sems)
    start_all(copies)
    rows = land.shape[0]
    end = out.shape[0] - 2 * rows
    out[end : end + rows, :] = 1.0 - relaxation * relax[...].astype(jnp.float32)
    out[end + rows :, :] = drag_rate * land[...].astype(jnp.float32)
    wait_all(copies)


def pack_field_kernel(x, out, sems):
    copies = pack_rows(x, out, sems)
    start_all(copies)
    wait_all(copies)


def inverse_kernel(mix, once, twice, solved):
    lev = mix.shape[0]
    wide = solved.shape[1]
    lane = lax.broadcasted_iota(jnp.int32, (1, wide), 1)
    unit = lane % lev
    ratio = []
    before = None
    inv = None
    for l in range(lev):
        rhs = jnp.where(unit == l, 1.0, 0.0).astype(jnp.float32)
        if l == 0:
            diag = jnp.full((1, wide), 1.0 + mix[0], jnp.float32)
        else:
            m = mix[l - 1]
            diag = (1.0 + mix[l] + m) - (m * m) * inv
            rhs = rhs + m * before
        inv = 1.0 / diag
        before = rhs * inv
        solved[l : l + 1, :] = before
        ratio.append(inv)
    for l in reversed(range(lev - 1)):
        before = solved[l : l + 1, :] + mix[l] * ratio[l] * before
        solved[l : l + 1, :] = before
    single = solved[...]
    double = jnp.dot(
        single[:, :lev],
        single,
        precision=lax.Precision.HIGHEST,
        preferred_element_type=jnp.float32,
    )
    third = lax.broadcasted_iota(jnp.int32, (lev, wide), 1) >= 2 * lev
    for matrix, out in ((single, once), (double, twice)):
        head = matrix.astype(jnp.bfloat16)
        tail = matrix - head.astype(jnp.float32)
        out[...] = jnp.where(third, tail, head.astype(jnp.float32)).astype(jnp.bfloat16)


def read(buf, base, f, i, lev):
    return buf[f, pl.ds(pl.multiple_of((i - base) * lev, 8), lev), :]


def write(buf, base, f, i, lev, value):
    buf[f, pl.ds(pl.multiple_of((i - base) * lev, 8), lev), :] = value


def tiled(block, lev):
    return jnp.concatenate([block] * (lev // 8), axis=0)


def solve(matrix, first, second):
    both = jnp.concatenate([first, second], axis=1)
    head = both.astype(jnp.bfloat16)
    tail = (both - head.astype(jnp.float32)).astype(jnp.bfloat16)
    out = jnp.dot(
        matrix, jnp.concatenate([head, tail, head], axis=0), preferred_element_type=jnp.float32
    )
    half = first.shape[1]
    return out[:, :half], out[:, half:]


def beside(value, lane):
    width = value.shape[1]
    east = jnp.where(lane < width - 1, pltpu.roll(value, width - 1, 1), 0.0)
    west = jnp.where(lane > 0, pltpu.roll(value, 1, 1), 0.0)
    return east + west


def fill_factors(borders, factors):
    for j in range(3):
        for r in range(4):
            for kind in range(2):
                line = borders[j, pl.ds(4 * kind + r, 1), :]
                factors[4 * j + r, kind] = jnp.broadcast_to(line, factors.shape[2:])


def row_loop(first, last, body):
    def pair(k, carry):
        body(first + 2 * k)
        body(first + 2 * k + 1)
        return carry

    lax.fori_loop(0, (last - first) // 2, pair, 0)


def state_row(i, x, xbase, factors, matrix, out, obase, lev):
    keep, drag = factors[i + 4, 0], factors[i + 4, 1]
    near = tiled(diffusion * keep, lev)
    wind = read(x, xbase, 0, i, lev)
    lane = lax.broadcasted_iota(jnp.int32, wind.shape, 1)
    parts = []
    for f in range(2):
        centre = wind if f == 0 else read(x, xbase, f, i, lev)
        up = read(x, xbase, f, i + 1, lev)
        down = read(x, xbase, f, i - 1, lev)
        own = tiled(keep * (0.6 - drag) if f == 0 else 0.6 * keep, lev)
        around = (up + down) + beside(centre, lane) - wind * (up - down)
        parts.append(own * centre + near * around)
    for f, value in enumerate(solve(matrix, *parts)):
        write(out, obase, f, i, lev, value)


def tangent_row(i, d, dbase, x, xbase, factors, matrix, out, obase, lev, damp):
    keep, drag = factors[i + 4, 0], factors[i + 4, 1]
    near = tiled(diffusion * keep, lev)
    wind = read(x, xbase, 0, i, lev)
    du = read(d, dbase, 0, i, lev)
    lane = lax.broadcasted_iota(jnp.int32, wind.shape, 1)
    parts = []
    for f in range(2):
        centre = du if f == 0 else read(d, dbase, f, i, lev)
        up = read(d, dbase, f, i + 1, lev)
        down = read(d, dbase, f, i - 1, lev)
        slope = read(x, xbase, f, i + 1, lev) - read(x, xbase, f, i - 1, lev)
        own = tiled(keep * (0.6 - drag) if f == 0 else 0.6 * keep, lev)
        around = (up + down) + beside(centre, lane) - wind * (up - down) - du * slope
        parts.append(own * centre + near * around)
    for f, value in enumerate(solve(matrix, *parts)):
        write(out, obase, f, i, lev, value * tiled(keep, lev) if damp else value)


def adjoint_row(i, b, bbase, x, xbase, factors, lev):
    drag = factors[i + 4, 1]
    lane = lax.broadcasted_iota(jnp.int32, (lev, b.shape[2]), 1)
    more = 1.0 + read(x, xbase, 0, i + 1, lev)
    less = 1.0 - read(x, xbase, 0, i - 1, lev)
    parts = []
    sloped = 0.0
    for f in range(2):
        centre = read(b, bbase, f, i, lev)
        up = read(b, bbase, f, i + 1, lev)
        down = read(b, bbase, f, i - 1, lev)
        sloped = sloped + centre * (read(x, xbase, f, i + 1, lev) - read(x, xbase, f, i - 1, lev))
        around = more * up + less * down + beside(centre, lane)
        parts.append((centre, around))
    wind_part = tiled(0.6 - drag, lev) * parts[0][0] + diffusion * (parts[0][1] - sloped)
    heat_part = 0.6 * parts[1][0] + diffusion * parts[1][1]
    return wind_part, heat_part


def border_copies(own, left, right, buf, borders, sems, first, last, rows, lev):
    copies = []
    for j, src in enumerate((left, own, right)):
        low = max(first - rows * (j - 1), 0)
        high = min(last - rows * (j - 1), rows)
        for f in range(2):
            copies.append(
                pltpu.make_async_copy(
                    src.at[pl.ds((f * rows + low) * lev, (high - low) * lev), :],
                    buf.at[f, pl.ds((low + rows * (j - 1) - first) * lev, (high - low) * lev), :],
                    sems.at[3 * f + j],
                )
            )
        if borders is not None:
            copies.append(
                pltpu.make_async_copy(
                    src.at[pl.ds(2 * rows * lev, 2 * rows), :], borders.at[j], sems.at[6 + j]
                )
            )
    return copies


def trajectory_kernel(own, left, right, once, x1, x2, x0, borders, factors, sems, *, lev):
    copies = border_copies(own, left, right, x0, borders, sems, -4, 8, 4, lev)
    start_all(copies)
    wait_all(copies)
    fill_factors(borders, factors)
    matrix = once[...]
    row_loop(-3, 7, lambda i: state_row(i, x0, -4, factors, matrix, x1, -3, lev))
    row_loop(-2, 6, lambda i: state_row(i, x1, -3, factors, matrix, x2, -2, lev))


def forward_kernel(
    own, left, right, p_own, p_left, p_right, x1, x2, once, twice,
    low_rows, high_rows,
    x0, borders, factors, p, t1, t2, b2, x_sems, p_sems, *, lev,
):
    copies = border_copies(p_own, p_left, p_right, p, None, p_sems, -4, 8, 4, lev)
    copies += border_copies(own, left, right, x0, borders, x_sems, -4, 8, 4, lev)
    start_all(copies)
    wait_all(copies)
    fill_factors(borders, factors)
    matrix = once[...]
    square = twice[...]
    row_loop(
        -3, 7, lambda i: tangent_row(i, p, -4, x0, -4, factors, matrix, t1, -3, lev, False)
    )
    row_loop(
        -2, 6, lambda i: tangent_row(i, t1, -3, x1, -3, factors, matrix, t2, -2, lev, False)
    )
    row_loop(
        -1, 5, lambda i: tangent_row(i, t2, -2, x2, -2, factors, square, b2, -1, lev, True)
    )

    def last(out, obase, i):
        keep = tiled(factors[i + 4, 0], lev)
        parts = adjoint_row(i, b2, -1, x2, -2, factors, lev)
        for f, value in enumerate(solve(matrix, *parts)):
            write(out, obase, f, i, lev, value * keep)

    row_loop(0, 2, lambda i: last(low_rows, 0, i))
    row_loop(2, 4, lambda i: last(high_rows, 2, i))


def backward_kernel(
    own, left, right, x1, b_left, b_low, b_high, b_right, once,
    packed, field,
    x0, borders, factors, b1, b0, x_sems, b_sems, out_sems, *, lev,
):
    copies = [
        pltpu.make_async_copy(
            src, b1.at[:, pl.ds(2 * lev * k, 2 * lev), :], b_sems.at[k]
        )
        for k, src in enumerate((b_left, b_low, b_high, b_right))
    ]
    copies += border_copies(own, left, right, x0, borders, x_sems, -1, 5, 4, lev)
    start_all(copies)
    wait_all(copies)
    fill_factors(borders, factors)
    matrix = once[...]

    def middle(i):
        keep = tiled(factors[i + 4, 0], lev)
        parts = adjoint_row(i, b1, -2, x1, -3, factors, lev)
        for f, value in enumerate(solve(matrix, *parts)):
            write(b0, -1, f, i, lev, value * keep)

    row_loop(-1, 5, middle)

    outs = []
    for i in range(4):
        parts = adjoint_row(i, b0, -1, x0, -1, factors, lev)
        for f, value in enumerate(parts):
            k = 4 * f + i
            packed[k * lev : (k + 1) * lev, :] = value
            copy = pltpu.make_async_copy(
                packed.at[pl.ds(k * lev, lev), :], field.at[:, f, i, :], out_sems.at[k]
            )
            copy.start()
            outs.append(copy)
    wait_all(outs)


def per_device(initial_state, perturbation, land_sea, relax_level, vertical_mix):
    lev, fields, rows, width = initial_state.shape
    tiles = lax.axis_size("tile")
    members = lax.axis_size("group")
    high = fields * rows * lev
    dma = pltpu.SemaphoreType.DMA
    rightward = [(i, i + 1) for i in range(tiles - 1)]
    leftward = [(i + 1, i) for i in range(tiles - 1)]

    def from_left(value):
        return lax.ppermute(value, "tile", rightward)

    def from_right(value):
        return lax.ppermute(value, "tile", leftward)

    def buffer(n):
        return pltpu.VMEM((fields, n * lev, width), jnp.float32)

    state = run(
        pack_state_kernel,
        f32(high + 2 * rows, width),
        [ANY, VMEM, VMEM],
        VMEM,
        [dma((fields * rows,))],
        nbytes=2**20,
    )(initial_state, land_sea, relax_level)
    state_left, state_right = from_left(state), from_right(state)
    start = run(
        pack_field_kernel, f32(high, width), [ANY], VMEM, [dma((fields * rows,))], nbytes=2**20
    )(perturbation[0])
    start_left, start_right = from_left(start), from_right(start)

    weights = jax.ShapeDtypeStruct((lev, 3 * lev), jnp.bfloat16)
    once, twice = run(
        inverse_kernel,
        (weights, weights),
        [SMEM],
        (VMEM, VMEM),
        [pltpu.VMEM((lev, 3 * lev), jnp.float32)],
        nbytes=2**20,
    )(vertical_mix)

    borders = pltpu.VMEM((3, 2 * rows, width), jnp.float32)
    factors = pltpu.VMEM((3 * rows, 2, 8, width), jnp.float32)
    x1, x2 = run(
        functools.partial(trajectory_kernel, lev=lev),
        (f32(fields, 10 * lev, width), f32(fields, 8 * lev, width)),
        [ANY, ANY, ANY, VMEM],
        (VMEM, VMEM),
        [buffer(12), borders, factors, dma((9,))],
        nbytes=6 * 2**20,
    )(state, state_left, state_right, once)

    low_rows, high_rows = run(
        functools.partial(forward_kernel, lev=lev),
        (f32(fields, 2 * lev, width), f32(fields, 2 * lev, width)),
        [ANY] * 6 + [VMEM] * 4,
        (VMEM, VMEM),
        [buffer(12), borders, factors, buffer(12), buffer(10), buffer(8), buffer(6)]
        + [dma((9,)), dma((6,))],
        nbytes=10 * 2**20,
    )(state, state_left, state_right, start, start_left, start_right, x1, x2, once, twice)

    b_left, b_right = from_left(high_rows), from_right(low_rows)
    packed, field = run(
        functools.partial(backward_kernel, lev=lev),
        (f32(high, width), f32(lev, fields, rows, width)),
        [ANY, ANY, ANY, VMEM, ANY, ANY, ANY, ANY, VMEM],
        (VMEM, ANY),
        [buffer(6), borders, factors, buffer(8), buffer(6)]
        + [dma((9,)), dma((4,)), dma((fields * rows,))],
        nbytes=6 * 2**20,
    )(state, state_left, state_right, x1, b_left, low_rows, high_rows, b_right, once)

    share = lax.all_to_all(
        packed.reshape(members, high // members, width), "group", 0, 0, tiled=True
    )
    products = lax.dot_general(
        share,
        share,
        (((1, 2), (1, 2)), ((), ())),
        precision=lax.Precision.HIGHEST,
        preferred_element_type=jnp.float32,
    )
    row = jnp.sum(lax.all_to_all(products, "group", 0, 0, tiled=True), axis=0)
    spread = jnp.broadcast_to(row[None], (tiles, members))
    row = jnp.sum(lax.all_to_all(spread, "tile", 0, 0, tiled=True), axis=0)
    gram = row[None] / (high * width * tiles)
    return (field[None], gram)


def solution(mesh):
    placed = (
        P(None, None, "tile", None),
        P("group", None, None, "tile", None),
        P("tile", None),
        P("tile", None),
        P(),
    )
    return jax.shard_map(
        per_device,
        mesh=mesh,
        in_specs=placed,
        out_specs=(P("group", None, None, "tile", None), P("group", None)),
        check_vma=False,
    )
```

time: 536 us -> 112 us (0.21)
  waiting for transfers between devices: 159 us -> 7.92 us
  between operations: 104 us -> 0.77 us
  other arithmetic: 90.6 us -> 0.6 us
  local copies, waits for them, and re-layouts: 48.3 us -> 2.46 us
  starting transfers between devices: 58.4 us -> 22.6 us
  Pallas kernels: 0 us -> 16.7 us
  blocking collectives: 65 us -> 59.3 us
    all_gather x1 -> x0, waiting for transfers between devices: 145 us -> none  [per_device(): lax.all_gather(adjoint_field, 'group', axis=0, tiled=True)]
    psum x1 -> x0, blocking collectives: 65 us -> none  [per_device(): whole_row = lax.psum(values, 'tile')]
    all_to_all x0 -> x3, blocking collectives: none -> 59.3 us  [the longest x1 27.5 us: per_device(): row = jnp.sum(lax.all_to_all(spread, 'tile', 0, 0, tiled=True), axis=0)]
    ppermute x18 -> x6, starting transfers between devices: 58.3 us -> 22.6 us  [the longest x3 13.1 us: from_right(): return lax.ppermute(value, 'tile', leftward)]
    broadcast_in_dim x3 -> x0, other arithmetic: 31.2 us -> none  [mixing_inverse(): lax.linalg.tridiagonal_solve(lower_band, diagonal_band, upper_band, ident...]
    div x2 -> x1, other arithmetic: 23 us -> 0.52 us  [per_device(): gram = row[None] / (high * width * tiles)]
    dynamic_slice x16 -> x0, local copies, waits for them, and re-layouts: 17.7 us -> none  [per_device(): lax.map(lambda member_row: jnp.sum(member_row * adjoint), lax.all_gather(...]
    pallas_call x0 -> x6, Pallas kernels: none -> 16.7 us  [the longest x1 6.95 us: per_device(): run(functools.partial(forward_kernel, lev=lev), (f32(fields, 2 * lev, wid...]
  transfers between devices with their start and end apart: 19 -> 6, of which waited for: 11 -> 4; matrix products, arithmetic and copies ran while one was open for 14% -> 0% of each run, Pallas kernels for 0% -> 5%
where the time goes in v1:
time: 112 us; the launch traced here: 111 us
  blocking collectives  59.3 us (53%)
  starting transfers between devices  22.6 us (20%)
  Pallas kernels  16.7 us (15%)
  waiting for transfers between devices  7.92 us (7%)
  local copies, waits for them, and re-layouts  2.46 us (2%)
    all_to_all x1, blocking collectives, per_device(): row = jnp.sum(lax.all_to_all(spread, 'tile', 0, 0, tiled=True), axis=0)  27.5 us
    all_to_all x1, blocking collectives, per_device(): lax.all_to_all(packed.reshape(members, high // members, width), 'group',...  22 us
    ppermute x3, starting transfers between devices, from_right(): return lax.ppermute(value, 'tile', leftward)  13.1 us
    all_to_all x1, blocking collectives, per_device(): row = jnp.sum(lax.all_to_all(products, 'group', 0, 0, tiled=True), axis=0)  9.88 us
    ppermute x3, starting transfers between devices, from_left(): return lax.ppermute(value, 'tile', rightward)  9.44 us
    pallas_call x1, Pallas kernels, per_device(): run(functools.partial(forward_kernel, lev=lev), (f32(fields, 2 * lev, wid...  6.95 us
    ppermute x3, waiting for transfers between devices, from_right(): return lax.ppermute(value, 'tile', leftward)  4.65 us
    pallas_call x1, Pallas kernels, per_device(): run(functools.partial(trajectory_kernel, lev=lev), (f32(fields, 10 * lev,...  4.11 us
  transfers between devices with their start and end apart: 6, of which 4 were waited for; matrix products, arithmetic and copies ran while one was open for 0% of the time, Pallas kernels for 5%

profile of v1, /device:TPU:1, one launch (start us, length us, event | category | flops | bytes accessed | tf_op | source)
XLA Modules:
  0.0 111.2 jit_solution(694439944341550885)
XLA Ops:
  0.6 0.0 copy-start
  0.6 1.1 copy-done
  1.7 0.0 copy-start.2
  1.7 0.7 copy-done.2
  2.4 0.0 copy-start.3
  2.4 0.7 copy-done.3
  3.1 0.0 copy-start.1
  3.1 0.0 copy-start.4
  3.1 0.5 shard_map.68.own
  3.6 8.8 %collective-permute-start.1 = (f32[392,384]{1,0:T(8,128)S(1)}, f32[392,384]{1,0:T(8,128)S(1)}, u32[]{:S(2)}, u32[]{:S(2)}) collective-permute-start(f32[392,384]{1,0:T(8,128)S(1)} %shard_map.68.own), channel_id=1, source_target_pairs={{1,0},{2,1},{3,2},{4,3},{5,4},{6,5},{7,6},{8,7},{9,8},{10,9},{11,1... | collective-permute-start | bytes 1806344 | tf_op jit(solution)/shard_map/ppermute | solution.py:330
  12.4 1.9 %collective-permute-start = (f32[392,384]{1,0:T(8,128)S(1)}, f32[392,384]{1,0:T(8,128)S(1)}, u32[]{:S(2)}, u32[]{:S(2)}) collective-permute-start(f32[392,384]{1,0:T(8,128)S(1)} %shard_map.68.own), channel_id=1, source_target_pairs={{0,1},{1,2},{2,3},{3,4},{4,5},{5,6},{6,7},{7,8},{8,9},{9,10},{10,1... | collective-permute-start | bytes 1806344 | tf_op jit(solution)/shard_map/ppermute | solution.py:327
  14.3 0.0 copy-done.1
  14.3 0.5 shard_map.71.p_own
  14.8 2.4 %collective-permute-start.3 = (f32[384,384]{1,0:T(8,128)S(1)}, f32[384,384]{1,0:T(8,128)S(1)}, u32[]{:S(2)}, u32[]{:S(2)}) collective-permute-start(f32[384,384]{1,0:T(8,128)S(1)} %shard_map.71.p_own), channel_id=1, source_target_pairs={{1,0},{2,1},{3,2},{4,3},{5,4},{6,5},{7,6},{8,7},{9,8},{10,9},{11,1... | collective-permute-start | bytes 1769480 | tf_op jit(solution)/shard_map/ppermute | solution.py:330
  17.3 3.1 %collective-permute-start.2 = (f32[384,384]{1,0:T(8,128)S(1)}, f32[384,384]{1,0:T(8,128)S(1)}, u32[]{:S(2)}, u32[]{:S(2)}) collective-permute-start(f32[384,384]{1,0:T(8,128)S(1)} %shard_map.71.p_own), channel_id=1, source_target_pairs={{0,1},{1,2},{2,3},{3,4},{4,5},{5,6},{6,7},{7,8},{8,9},{9,10},{10,1... | collective-permute-start | bytes 1769480 | tf_op jit(solution)/shard_map/ppermute | solution.py:327
  20.4 0.0 copy-done.4
  20.4 1.2 %shard_map.69 = (bf16[48,144]{1,0:T(8,128)(2,1)S(1)}, bf16[48,144]{1,0:T(8,128)(2,1)S(1)}) custom-call(f32[48]{0:T(128)S(1)} %copy-done.4), custom_call_target="tpu_custom_call" | custom-call | bytes 1048576 | tf_op jit(solution)/shard_map/pallas_call | solution.py:350
  21.6 0.0 collective-permute-done.1.right
  21.6 0.0 collective-permute-done.left
  21.7 4.1 %shard_map.70 = (f32[2,480,384]{2,1,0:T(8,128)S(1)}, f32[2,384,384]{2,1,0:T(8,128)S(1)}) custom-call(f32[392,384]{1,0:T(8,128)S(1)} %shard_map.68.own, f32[392,384]{1,0:T(8,128)S(1)} %collective-permute-done.left, f32[392,384]{1,0:T(8,128)S(1)} %collective-permute-done.1.right, bf16[48,144]{1,0:T(8,128)(2,1)S(1)} %get-tuple-element.10.once), custom_call_target="tpu_custom_call" | custom-call | bytes 6291456 | tf_op jit(solution)/shard_map/pallas_call | solution.py:361
  25.8 0.3 collective-permute-done.3.p_right
  26.0 1.5 %collective-permute-done.2.p_left = f32[384,384]{1,0:T(8,128)S(1)} collective-permute-done((f32[384,384]{1,0:T(8,128)S(1)}, f32[384,384]{1,0:T(8,128)S(1)}, u32[]{:S(2)}, u32[]{:S(2)}) %collective-permute-start.2) | collective-permute-done | bytes 589856 | tf_op jit(solution)/shard_map/ppermute | solution.py:327
  27.6 7.0 %shard_map.72 = (f32[2,96,384]{2,1,0:T(8,128)S(1)}, f32[2,96,384]{2,1,0:T(8,128)S(1)}) custom-call(f32[392,384]{1,0:T(8,128)S(1)} %shard_map.68.own, f32[392,384]{1,0:T(8,128)S(1)} %collective-permute-done.left, f32[392,384]{1,0:T(8,128)S(1)} %collective-permute-done.1.right, f32[384,384]{1,0:T(8,128)S(1)} %shard_map.71.p_own, ...), custom_call_target="tpu_custom_call" | custom-call | bytes 10485760 | tf_op jit(solution)/shard_map/pallas_call | solution.py:370
  34.5 4.4 %collective-permute-start.4 = (f32[2,96,384]{2,1,0:T(8,128)S(1)}, f32[2,96,384]{2,1,0:T(8,128)S(1)}, u32[]{:S(2)}, u32[]{:S(2)}) collective-permute-start(f32[2,96,384]{2,1,0:T(8,128)S(1)} %get-tuple-element.14.b_high), channel_id=1, source_target_pairs={{0,1},{1,2},{2,3},{3,4},{4,5},{5,6},{6,7},{7,8},{8,9},{9,10},{10,1... | collective-permute-start | bytes 884744 | tf_op jit(solution)/shard_map/ppermute | solution.py:327
  38.9 1.9 %collective-permute-start.5 = (f32[2,96,384]{2,1,0:T(8,128)S(1)}, f32[2,96,384]{2,1,0:T(8,128)S(1)}, u32[]{:S(2)}, u32[]{:S(2)}) collective-permute-start(f32[2,96,384]{2,1,0:T(8,128)S(1)} %get-tuple-element.15.b_low), channel_id=1, source_target_pairs={{1,0},{2,1},{3,2},{4,3},{5,4},{6,5},{7,6},{8,7},{9,8},{10,9},{11,1... | collective-permute-start | bytes 884744 | tf_op jit(solution)/shard_map/ppermute | solution.py:330
  40.9 1.7 %collective-permute-done.4.b_left = f32[2,96,384]{2,1,0:T(8,128)S(1)} collective-permute-done((f32[2,96,384]{2,1,0:T(8,128)S(1)}, f32[2,96,384]{2,1,0:T(8,128)S(1)}, u32[]{:S(2)}, u32[]{:S(2)}) %collective-permute-start.4) | collective-permute-done | bytes 294944 | tf_op jit(solution)/shard_map/ppermute | solution.py:327
  42.6 4.4 %collective-permute-done.5.b_right = f32[2,96,384]{2,1,0:T(8,128)S(1)} collective-permute-done((f32[2,96,384]{2,1,0:T(8,128)S(1)}, f32[2,96,384]{2,1,0:T(8,128)S(1)}, u32[]{:S(2)}, u32[]{:S(2)}) %collective-permute-start.5) | collective-permute-done | bytes 294944 | tf_op jit(solution)/shard_map/ppermute | solution.py:330
  47.0 3.4 %shard_map.73 = (f32[384,384]{1,0:T(8,128)S(1)}, f32[48,2,4,384]{3,2,1,0:T(4,128)}) custom-call(f32[392,384]{1,0:T(8,128)S(1)} %shard_map.68.own, f32[392,384]{1,0:T(8,128)S(1)} %collective-permute-done.left, f32[392,384]{1,0:T(8,128)S(1)} %collective-permute-done.1.right, f32[2,480,384]{2,1,0:T(8,128)S(1)} %get-tuple-element.11.x1, ...), custom_call_target="tpu_custom_call" | custom-call | bytes 6291456 | tf_op jit(solution)/shard_map/pallas_call | solution.py:381
  50.4 22.0 %all_to_all.20 = f32[16,24,384]{2,1,0:T(8,128)S(1)} all-to-all(f32[16,24,384]{2,1,0:T(8,128)S(1)} %bitcast.10), channel_id=1, replica_groups=mesh['group'=16,'tile'=32] {'group'}, dimensions={0} | all-to-all | bytes 1179648 | tf_op jit(solution)/shard_map/all_to_all | solution.py:391
  72.4 0.8 fusion
  73.2 9.9 %all_to_all.21 = f32[16,1,16]{2,1,0:T(1,128)S(1)} all-to-all(f32[16,1,16]{2,1,0:T(1,128)S(1)} %bitcast.11), channel_id=1, replica_groups=mesh['group'=16,'tile'=32] {'group'}, dimensions={0} | all-to-all | bytes 2048 | tf_op jit(solution)/shard_map/all_to_all | solution.py:401
  83.2 27.5 %all_to_all.22 = f32[32,1,16]{2,1,0:T(1,128)S(1)} all-to-all(f32[32,1,16]{2,1,0:T(1,128)S(1)} %broadcast_in_dim.5), channel_id=1, replica_groups=mesh['group'=16,'tile'=32] {'tile'}, dimensions={0} | all-to-all | bytes 4096 | tf_op jit(solution)/shard_map/all_to_all | solution.py:403
  110.6 0.1 reduce_sum.19
  110.7 0.5 multiply_bitcast_fusion
  (2 shorter events, 0.0 us)
Async XLA Ops:
  0.6 1.1 copy-start
  1.7 0.7 copy-start.2
  2.4 0.7 copy-start.3
  3.1 11.2 %copy-start.1 = (f32[1,48,2,4,384]{4,3,2,1,0:T(4,128)S(1)}, f32[1,48,2,4,384]{4,3,2,1,0:T(4,128)}, u32[]{:S(2)}) copy-start(f32[1,48,2,4,384]{4,3,2,1,0:T(4,128)} %param.6) | copy-start | bytes 1769476
  3.1 17.3 %copy-start.4 = (f32[48]{0:T(128)S(1)}, f32[48]{0:T(128)}, u32[]{:S(2)}) copy-start(f32[48]{0:T(128)} %mix.1) | copy-start | bytes 580
  3.6 18.0 %collective-permute-start.1 = (f32[392,384]{1,0:T(8,128)S(1)}, f32[392,384]{1,0:T(8,128)S(1)}, u32[]{:S(2)}, u32[]{:S(2)}) collective-permute-start(f32[392,384]{1,0:T(8,128)S(1)} %shard_map.68.own), channel_id=1, source_target_pairs={{1,0},{2,1},{3,2},{4,3},{5,4},{6,5},{7,6},{8,7},{9,8},{10,9},{11,1... | collective-permute-start | bytes 1806344 | tf_op jit(solution)/shard_map/ppermute | solution.py:330
  12.4 9.3 %collective-permute-start = (f32[392,384]{1,0:T(8,128)S(1)}, f32[392,384]{1,0:T(8,128)S(1)}, u32[]{:S(2)}, u32[]{:S(2)}) collective-permute-start(f32[392,384]{1,0:T(8,128)S(1)} %shard_map.68.own), channel_id=1, source_target_pairs={{0,1},{1,2},{2,3},{3,4},{4,5},{5,6},{6,7},{7,8},{8,9},{9,10},{10,1... | collective-permute-start | bytes 1806344 | tf_op jit(solution)/shard_map/ppermute | solution.py:327
  14.8 11.2 %collective-permute-start.3 = (f32[384,384]{1,0:T(8,128)S(1)}, f32[384,384]{1,0:T(8,128)S(1)}, u32[]{:S(2)}, u32[]{:S(2)}) collective-permute-start(f32[384,384]{1,0:T(8,128)S(1)} %shard_map.71.p_own), channel_id=1, source_target_pairs={{1,0},{2,1},{3,2},{4,3},{5,4},{6,5},{7,6},{8,7},{9,8},{10,9},{11,1... | collective-permute-start | bytes 1769480 | tf_op jit(solution)/shard_map/ppermute | solution.py:330
  17.3 10.3 %collective-permute-start.2 = (f32[384,384]{1,0:T(8,128)S(1)}, f32[384,384]{1,0:T(8,128)S(1)}, u32[]{:S(2)}, u32[]{:S(2)}) collective-permute-start(f32[384,384]{1,0:T(8,128)S(1)} %shard_map.71.p_own), channel_id=1, source_target_pairs={{0,1},{1,2},{2,3},{3,4},{4,5},{5,6},{6,7},{7,8},{8,9},{9,10},{10,1... | collective-permute-start | bytes 1769480 | tf_op jit(solution)/shard_map/ppermute | solution.py:327
  34.5 8.0 %collective-permute-start.4 = (f32[2,96,384]{2,1,0:T(8,128)S(1)}, f32[2,96,384]{2,1,0:T(8,128)S(1)}, u32[]{:S(2)}, u32[]{:S(2)}) collective-permute-start(f32[2,96,384]{2,1,0:T(8,128)S(1)} %get-tuple-element.14.b_high), channel_id=1, source_target_pairs={{0,1},{1,2},{2,3},{3,4},{4,5},{5,6},{6,7},{7,8},{8,9},{9,10},{10,1... | collective-permute-start | bytes 884744 | tf_op jit(solution)/shard_map/ppermute | solution.py:327
  38.9 8.0 %collective-permute-start.5 = (f32[2,96,384]{2,1,0:T(8,128)S(1)}, f32[2,96,384]{2,1,0:T(8,128)S(1)}, u32[]{:S(2)}, u32[]{:S(2)}) collective-permute-start(f32[2,96,384]{2,1,0:T(8,128)S(1)} %get-tuple-element.15.b_low), channel_id=1, source_target_pairs={{1,0},{2,1},{3,2},{4,3},{5,4},{6,5},{7,6},{8,7},{9,8},{10,9},{11,1... | collective-permute-start | bytes 884744 | tf_op jit(solution)/shard_map/ppermute | solution.py:330

commit v2 on v1

v2 whole, which is shorter than its diff:
```python
import jax
import jax.numpy as jnp
from jax import lax
from jax.experimental import pallas as pl
from jax.experimental.pallas import tpu as pltpu
from jax.sharding import PartitionSpec as P

advection = 0.2
diffusion = 0.1
drag_rate = 0.3
relaxation = 0.125

VMEM_LIMIT = 24 * 2**20

ANY = pl.BlockSpec(memory_space=pl.ANY)
VMEM = pl.BlockSpec(memory_space=pltpu.VMEM)
SMEM = pl.BlockSpec(memory_space=pltpu.SMEM)


def run(kernel, out_shape, in_specs, out_specs, scratch, nbytes, limit=VMEM_LIMIT):
    return pl.pallas_call(
        kernel,
        out_shape=out_shape,
        in_specs=in_specs,
        out_specs=out_specs,
        scratch_shapes=scratch,
        compiler_params=pltpu.CompilerParams(vmem_limit_bytes=limit),
        cost_estimate=pl.CostEstimate(flops=0, bytes_accessed=nbytes, transcendentals=0),
    )


def f32(*shape):
    return jax.ShapeDtypeStruct(shape, jnp.float32)


def start_all(copies):
    for copy in copies:
        copy.start()


def wait_all(copies):
    for copy in copies:
        copy.wait()


def pack_rows(src, dst, sems, flipped):
    lev, fields, rows, _ = src.shape
    copies = []
    for f in range(fields):
        for r in range(rows):
            place = f * rows + jnp.where(flipped, rows - 1 - r, r)
            copies.append(
                pltpu.make_async_copy(
                    src.at[:, f, r, :],
                    dst.at[pl.ds(pl.multiple_of(place * lev, 8), lev), :],
                    sems.at[f * rows + r],
                )
            )
    return copies


def fill_lines(ints, out, flipped):
    rows = ints.shape[1]
    end = out.shape[0] - 2 * rows
    keep = 1.0 - relaxation * ints[0].astype(jnp.float32)
    drag = drag_rate * ints[1].astype(jnp.float32)
    for k, values in enumerate((keep, drag)):
        for r in range(rows):
            other = rows - 1 - r
            line = jnp.where(flipped, values[other : other + 1], values[r : r + 1])
            out[end + k * rows + r : end + k * rows + r + 1, :] = line


def pack_state_kernel(side, x, land, relax, out, sems, ints, more_sems, staged, out_sems):
    flipped = side[0] < 0.0
    loads = [
        pltpu.make_async_copy(src, ints.at[k], more_sems.at[k])
        for k, src in enumerate((relax, land))
    ]
    copies = pack_rows(x, staged, sems, flipped)
    start_all(loads)
    start_all(copies)
    wait_all(loads)
    fill_lines(ints, staged, flipped)
    lev, fields, rows, _ = x.shape
    places = [
        (f * rows + jnp.where(flipped, rows - 1 - r, r)) * lev
        for f in range(fields)
        for r in range(rows)
    ]
    pieces = [pl.ds(pl.multiple_of(place, 8), lev) for place in places]
    pieces.append(pl.ds(fields * rows * lev, 2 * rows))
    outs = [
        pltpu.make_async_copy(staged.at[piece], out.at[piece], out_sems.at[k])
        for k, piece in enumerate(pieces)
    ]
    outs[-1].start()
    for copy, onward in zip(copies, outs):
        copy.wait()
        onward.start()
    wait_all(outs)


def pack_field_kernel(side, x, out, sems):
    copies = pack_rows(x, out, sems, side[0] < 0.0)
    start_all(copies)
    wait_all(copies)


def inverse_kernel(mix, once, twice, solved):
    lev = mix.shape[0]
    wide = solved.shape[1]
    lane = lax.broadcasted_iota(jnp.int32, (1, wide), 1)
    unit = lane % lev
    ratio = []
    before = None
    inv = None
    for l in range(lev):
        rhs = jnp.where(unit == l, 1.0, 0.0).astype(jnp.float32)
        if l == 0:
            diag = jnp.full((1, wide), 1.0 + mix[0], jnp.float32)
        else:
            m = mix[l - 1]
            diag = (1.0 + mix[l] + m) - (m * m) * inv
            rhs = rhs + m * before
        inv = 1.0 / diag
        before = rhs * inv
        solved[l : l + 1, :] = before
        ratio.append(inv)
    for l in reversed(range(lev - 1)):
        before = solved[l : l + 1, :] + mix[l] * ratio[l] * before
        solved[l : l + 1, :] = before
    single = solved[...]
    double = jnp.dot(
        single[:, :lev],
        single,
        precision=lax.Precision.HIGHEST,
        preferred_element_type=jnp.float32,
    )
    third = lax.broadcasted_iota(jnp.int32, (lev, wide), 1) >= 2 * lev
    for matrix, out in ((single, once), (double, twice)):
        head = matrix.astype(jnp.bfloat16)
        tail = matrix - head.astype(jnp.float32)
        out[...] = jnp.where(third, tail, head.astype(jnp.float32)).astype(jnp.bfloat16)


class Rows:
    def __init__(self, lev, *pieces):
        self.lev = lev
        self.where = {}
        for buf, rows in pieces:
            for k, i in enumerate(rows):
                for f in range(2):
                    self.where[f, i] = (buf, (f * len(rows) + k) * lev)

    def read(self, f, i):
        buf, at = self.where[f, i]
        return buf[at : at + self.lev, :]

    def write(self, f, i, value):
        buf, at = self.where[f, i]
        buf[at : at + self.lev, :] = value


OWN = (0, 1, 2, 3)
OUTER = (-1, -2, -3, -4)
INNER = (7, 6, 5, 4)


def state_rows(own, outer, inner):
    lev = (own.shape[0] - 8) // 8
    return Rows(lev, (own, OWN), (outer, OUTER), (inner, INNER))


class Factors:
    def __init__(self, own, outer, inner):
        self.end = own.shape[0] - 8
        self.lev = self.end // 8
        self.where = {}
        for buf, rows in ((own, OWN), (outer, OUTER), (inner, INNER)):
            for k, i in enumerate(rows):
                self.where[i] = (buf, k)

    def line(self, i, kind):
        buf, k = self.where[i]
        at = self.end + 4 * kind + k
        return jnp.broadcast_to(buf[at : at + 1, :], (8, buf.shape[1]))

    def keep(self, i):
        return self.line(i, 0)

    def drag(self, i):
        return self.line(i, 1)


def tiled(block, lev):
    return jnp.concatenate([block] * (lev // 8), axis=0)


def solve(matrix, first, second):
    both = jnp.concatenate([first, second], axis=1)
    head = both.astype(jnp.bfloat16)
    tail = (both - head.astype(jnp.float32)).astype(jnp.bfloat16)
    out = jnp.dot(
        matrix, jnp.concatenate([head, tail, head], axis=0), preferred_element_type=jnp.float32
    )
    half = first.shape[1]
    return out[:, :half], out[:, half:]


def beside(value):
    lev, width = value.shape
    step = 128
    lane = lax.broadcasted_iota(jnp.int32, (lev, step), 1)
    parts = [value[:, c : c + step] for c in range(0, width, step)]
    up = [pltpu.roll(part, 1, 1) for part in parts]
    down = [pltpu.roll(part, step - 1, 1) for part in parts]
    zero = jnp.zeros_like(up[0])
    sums = []
    for k in range(len(parts)):
        west = jnp.where(lane == 0, up[k - 1] if k > 0 else zero, up[k])
        east = jnp.where(lane == step - 1, down[k + 1] if k + 1 < len(parts) else zero, down[k])
        sums.append(west + east)
    return jnp.concatenate(sums, axis=1)


def state_row(i, side, x, factors, matrix, out):
    lev = x.lev
    keep, drag = factors.keep(i), factors.drag(i)
    near = tiled(diffusion * keep, lev)
    wind = side * x.read(0, i)
    parts = []
    for f in range(2):
        centre = x.read(f, i)
        up, down = x.read(f, i + 1), x.read(f, i - 1)
        own = tiled(keep * (0.6 - drag) if f == 0 else 0.6 * keep, lev)
        around = (up + down) + beside(centre) - wind * (up - down)
        parts.append(own * centre + near * around)
    for f, value in enumerate(solve(matrix, *parts)):
        out.write(f, i, value)


def tangent_row(i, side, d, x, factors, matrix, out, damp):
    lev = x.lev
    keep, drag = factors.keep(i), factors.drag(i)
    near = tiled(diffusion * keep, lev)
    wind = side * x.read(0, i)
    du = side * d.read(0, i)
    parts = []
    for f in range(2):
        centre = d.read(f, i)
        up, down = d.read(f, i + 1), d.read(f, i - 1)
        slope = x.read(f, i + 1) - x.read(f, i - 1)
        own = tiled(keep * (0.6 - drag) if f == 0 else 0.6 * keep, lev)
        around = (up + down) + beside(centre) - wind * (up - down) - du * slope
        parts.append(own * centre + near * around)
    for f, value in enumerate(solve(matrix, *parts)):
        out.write(f, i, value * tiled(keep, lev) if damp else value)


def adjoint_row(i, side, b, x, factors):
    lev = x.lev
    drag = factors.drag(i)
    more = 1.0 + side * x.read(0, i + 1)
    less = 1.0 - side * x.read(0, i - 1)
    parts = []
    sloped = 0.0
    for f in range(2):
        centre = b.read(f, i)
        sloped = sloped + centre * (x.read(f, i + 1) - x.read(f, i - 1))
        around = more * b.read(f, i + 1) + less * b.read(f, i - 1) + beside(centre)
        parts.append((centre, around))
    wind_part = tiled(0.6 - drag, lev) * parts[0][0] + diffusion * (parts[0][1] - side * sloped)
    heat_part = 0.6 * parts[1][0] + diffusion * parts[1][1]
    return wind_part, heat_part


def adjoint_solved(i, side, b, x, factors, matrix, out):
    keep = tiled(factors.keep(i), x.lev)
    for f, value in enumerate(solve(matrix, *adjoint_row(i, side, b, x, factors))):
        out.write(f, i, value * keep)


def span(first, last):
    return tuple(range(first, last))


def trajectory_kernel(side, own, inner, outer, once, x1, x2):
    sign = side[0]
    first = state_rows(own, outer, inner)
    factors = Factors(own, outer, inner)
    lev = first.lev
    second = Rows(lev, (x1, span(-3, 7)))
    third = Rows(lev, (x2, span(-2, 6)))
    for i in span(-3, 7):
        state_row(i, sign, first, factors, once[...], second)
    for i in span(-2, 6):
        state_row(i, sign, second, factors, once[...], third)


def forward_kernel(
    side, own, inner, outer, p_own, p_inner, p_outer, x1, x2, once, twice,
    outer_rows, inner_rows,
    t1, t2, b2,
):
    sign = side[0]
    first = state_rows(own, outer, inner)
    factors = Factors(own, outer, inner)
    lev = first.lev
    second = Rows(lev, (x1, span(-3, 7)))
    third = Rows(lev, (x2, span(-2, 6)))
    start = Rows(lev, (p_own, OWN), (p_outer, OUTER), (p_inner, INNER))
    once_moved = Rows(lev, (t1, span(-3, 7)))
    twice_moved = Rows(lev, (t2, span(-2, 6)))
    back = Rows(lev, (b2, span(-1, 5)))
    out = Rows(lev, (outer_rows, (0, 1)), (inner_rows, (3, 2)))
    for i in span(-3, 7):
        tangent_row(i, sign, start, first, factors, once[...], once_moved, False)
    for i in span(-2, 6):
        tangent_row(i, sign, once_moved, second, factors, once[...], twice_moved, False)
    for i in span(-1, 5):
        tangent_row(i, sign, twice_moved, third, factors, twice[...], back, True)
    for i in OWN:
        adjoint_solved(i, sign, back, third, factors, once[...], out)


def backward_kernel(
    side, own, inner, outer, x1, outer_rows, inner_rows, b_outer, b_inner, once,
    packed, field,
    b0, sems,
):
    sign = side[0]
    first = state_rows(own, outer, inner)
    factors = Factors(own, outer, inner)
    lev = first.lev
    second = Rows(lev, (x1, span(-3, 7)))
    back = Rows(
        lev, (outer_rows, (0, 1)), (inner_rows, (3, 2)), (b_outer, (-1, -2)), (b_inner, (4, 5))
    )
    last = Rows(lev, (b0, span(-1, 5)))
    for i in span(-1, 5):
        adjoint_solved(i, sign, back, second, factors, once[...], last)
    outs = []
    for i in OWN:
        row = jnp.where(sign < 0.0, 3 - i, i)
        for f, value in enumerate(adjoint_row(i, sign, last, first, factors)):
            k = 4 * f + i
            packed[k * lev : (k + 1) * lev, :] = value
            copy = pltpu.make_async_copy(
                packed.at[pl.ds(k * lev, lev), :], field.at[:, f, row, :], sems.at[k]
            )
            copy.start()
            outs.append(copy)
    wait_all(outs)


def per_device(initial_state, perturbation, land_sea, relax_level, vertical_mix):
    lev, fields, rows, width = initial_state.shape
    tiles = lax.axis_size("tile")
    members = lax.axis_size("group")
    high = fields * rows * lev
    dma = pltpu.SemaphoreType.DMA
    side = (1 - 2 * (lax.axis_index("tile") & 1)).astype(jnp.float32)[None]
    across = [(i, i + 1) for i in range(1, tiles - 1, 2)]
    within = [(i, i + 1) for i in range(0, tiles, 2)]

    def swap(value, pairs):
        return lax.ppermute(value, "tile", pairs + [(j, i) for i, j in pairs])

    def buffer(n):
        return pltpu.VMEM((fields * n * lev, width), jnp.float32)

    state = run(
        pack_state_kernel,
        f32(high + 2 * rows, width),
        [SMEM, ANY, ANY, ANY],
        ANY,
        [
            dma((fields * rows,)),
            pltpu.VMEM((2, rows, width), jnp.int32),
            dma((2,)),
            pltpu.VMEM((high + 2 * rows, width), jnp.float32),
            dma((fields * rows + 1,)),
        ],
        2**20,
        60 * 2**20,
    )(side, initial_state, land_sea, relax_level)
    state_inner = swap(state, within)
    state_outer = swap(state, across)
    start = run(
        pack_field_kernel, f32(high, width), [SMEM, ANY], VMEM, [dma((fields * rows,))], nbytes=2**20
    )(side, perturbation[0])
    start_inner = swap(start, within)
    start_outer = swap(start, across)

    weights = jax.ShapeDtypeStruct((lev, 3 * lev), jnp.bfloat16)
    once, twice = run(
        inverse_kernel,
        (weights, weights),
        [SMEM],
        (VMEM, VMEM),
        [pltpu.VMEM((lev, 3 * lev), jnp.float32)],
        nbytes=2**20,
    )(vertical_mix)

    x1, x2 = run(
        trajectory_kernel,
        (f32(fields * 10 * lev, width), f32(fields * 8 * lev, width)),
        [SMEM] + [VMEM] * 4,
        (VMEM, VMEM),
        [],
        nbytes=6 * 2**20,
    )(side, state, state_inner, state_outer, once)

    outer_rows, inner_rows = run(
        forward_kernel,
        (f32(fields * 2 * lev, width), f32(fields * 2 * lev, width)),
        [SMEM] + [VMEM] * 10,
        (VMEM, VMEM),
        [buffer(10), buffer(8), buffer(6)],
        nbytes=10 * 2**20,
    )(side, state, state_inner, state_outer, start, start_inner, start_outer, x1, x2, once, twice)

    b_outer, b_inner = swap(outer_rows, across), swap(inner_rows, within)
    packed, field = run(
        backward_kernel,
        (f32(high, width), f32(lev, fields, rows, width)),
        [SMEM] + [VMEM] * 9,
        (VMEM, ANY),
        [buffer(6), dma((fields * rows,))],
        nbytes=6 * 2**20,
    )(side, state, state_inner, state_outer, x1, outer_rows, inner_rows, b_outer, b_inner, once)

    share = lax.all_to_all(
        packed.reshape(members, high // members, width), "group", 0, 0, tiled=True
    )
    products = lax.dot_general(
        share,
        share,
        (((1, 2), (1, 2)), ((), ())),
        precision=lax.Precision.HIGHEST,
        preferred_element_type=jnp.float32,
    )
    row = jnp.sum(lax.all_to_all(products, "group", 0, 0, tiled=True), axis=0)
    spread = jnp.broadcast_to(row[None], (tiles, members))
    row = jnp.sum(lax.all_to_all(spread, "tile", 0, 0, tiled=True), axis=0)
    gram = row[None] / (high * width * tiles)
    return (field[None], gram)


def solution(mesh):
    placed = (
        P(None, None, "tile", None),
        P("group", None, None, "tile", None),
        P("tile", None),
        P("tile", None),
        P(),
    )
    return jax.shard_map(
        per_device,
        mesh=mesh,
        in_specs=placed,
        out_specs=(P("group", None, None, "tile", None), P("group", None)),
        check_vma=False,
    )
```

time: 112 us -> 98.1 us (0.88)
  starting transfers between devices: 22.6 us -> 17.3 us
  Pallas kernels: 16.7 us -> 11.6 us
  local copies, waits for them, and re-layouts: 2.46 us -> 0.03 us
    all_to_all x1, blocking collectives: 27.5 us -> 21 us  [per_device(): row = jnp.sum(lax.all_to_all(spread, 'tile', 0, 0, tiled=True), axis=0)]
    all_to_all x1, blocking collectives: 22 us -> 27.3 us  [per_device(): lax.all_to_all(packed.reshape(members, high // members, width), 'group',...]
    ppermute x6, starting transfers between devices: 22.6 us -> 17.3 us  [swap(): return lax.ppermute(value, 'tile', pairs + [(j, i) for i, j in pairs])]
    pallas_call x5, Pallas kernels: 15.5 us -> 10.4 us  [the longest x1 3.6 us: per_device(): run(forward_kernel, (f32(fields * 2 * lev, width), f32(fields * 2 * lev,...]
    unnamed x10 -> x6, local copies, waits for them, and re-layouts: 2.45 us -> 0.01 us
  transfers between devices with their start and end apart: 6 -> 6, of which waited for: 4 -> 2; matrix products, arithmetic and copies ran while one was open for 0% -> 0% of each run, Pallas kernels for 5% -> 4%
where the time goes in v2:
time: 98.1 us; the launch traced here: 97.7 us
  blocking collectives  58.4 us (60%)
  starting transfers between devices  17.3 us (18%)
  Pallas kernels  11.6 us (12%)
  waiting for transfers between devices  8.09 us (8%)
    all_to_all x1, blocking collectives, per_device(): lax.all_to_all(packed.reshape(members, high // members, width), 'group',...  27.3 us
    all_to_all x1, blocking collectives, per_device(): row = jnp.sum(lax.all_to_all(spread, 'tile', 0, 0, tiled=True), axis=0)  21 us
    ppermute x6, starting transfers between devices, swap(): return lax.ppermute(value, 'tile', pairs + [(j, i) for i, j in pairs])  17.3 us
    all_to_all x1, blocking collectives, per_device(): row = jnp.sum(lax.all_to_all(products, 'group', 0, 0, tiled=True), axis=0)  10.1 us
    ppermute x6, waiting for transfers between devices, swap(): return lax.ppermute(value, 'tile', pairs + [(j, i) for i, j in pairs])  8.09 us
    pallas_call x1, Pallas kernels, per_device(): run(forward_kernel, (f32(fields * 2 * lev, width), f32(fields * 2 * lev,...  3.6 us
    pallas_call x1, Pallas kernels, per_device(): run(trajectory_kernel, (f32(fields * 10 * lev, width), f32(fields * 8 * l...  2.18 us
    pallas_call x1, Pallas kernels, per_device(): run(pack_state_kernel, f32(high + 2 * rows, width), [SMEM, ANY, ANY, ANY]...  2.1 us
  transfers between devices with their start and end apart: 6, of which 2 were waited for; matrix products, arithmetic and copies ran while one was open for 0% of the time, Pallas kernels for 4%

profile of v2, /device:TPU:1, one launch (start us, length us, event | category | flops | bytes accessed | tf_op | source)
XLA Modules:
  0.0 97.7 jit_solution(8509054009476547044)
XLA Ops:
  0.6 0.0 copy-start.1
  0.6 0.0 copy-start.2
  0.7 2.1 %shard_map.68.own = f32[392,384]{1,0:T(8,128)} custom-call(f32[1]{0:T(128)} %bitcast.side, f32[48,2,4,384]{3,2,1,0:T(4,128)} %x.1, s32[4,384]{1,0:T(4,128)} %land.1, s32[4,384]{1,0:T(4,128)} %relax.1), custom_call_target="tpu_custom_call" | custom-call | bytes 1048576 | tf_op jit(solution)/shard_map/pallas_call | solution.py:373
  2.8 0.0 copy-start
  2.8 4.7 %collective-permute-start.1 = (f32[392,384]{1,0:T(8,128)}, f32[392,384]{1,0:T(8,128)S(1)}, u32[]{:S(2)}, u32[]{:S(2)}) collective-permute-start(f32[392,384]{1,0:T(8,128)} %shard_map.68.own), channel_id=1, source_target_pairs={{1,2},{3,4},{5,6},{7,8},{9,10},{11,12},{13,14},{15,16},{17,18},{19... | collective-permute-start | bytes 1806344 | tf_op jit(solution)/shard_map/ppermute | solution.py:368
  7.5 4.9 %collective-permute-start = (f32[392,384]{1,0:T(8,128)}, f32[392,384]{1,0:T(8,128)S(1)}, u32[]{:S(2)}, u32[]{:S(2)}) collective-permute-start(f32[392,384]{1,0:T(8,128)} %shard_map.68.own), channel_id=1, source_target_pairs={{0,1},{2,3},{4,5},{6,7},{8,9},{10,11},{12,13},{14,15},{16,17},{18,... | collective-permute-start | bytes 1806344 | tf_op jit(solution)/shard_map/ppermute | solution.py:368
  12.4 0.0 copy-done.1
  12.4 0.5 shard_map.71.p_own
  12.9 1.9 %collective-permute-start.3 = (f32[384,384]{1,0:T(8,128)S(1)}, f32[384,384]{1,0:T(8,128)S(1)}, u32[]{:S(2)}, u32[]{:S(2)}) collective-permute-start(f32[384,384]{1,0:T(8,128)S(1)} %shard_map.71.p_own), channel_id=1, source_target_pairs={{1,2},{3,4},{5,6},{7,8},{9,10},{11,12},{13,14},{15,16},{17,18},{19... | collective-permute-start | bytes 1769480 | tf_op jit(solution)/shard_map/ppermute | solution.py:368
  14.9 1.9 %collective-permute-start.2 = (f32[384,384]{1,0:T(8,128)S(1)}, f32[384,384]{1,0:T(8,128)S(1)}, u32[]{:S(2)}, u32[]{:S(2)}) collective-permute-start(f32[384,384]{1,0:T(8,128)S(1)} %shard_map.71.p_own), channel_id=1, source_target_pairs={{0,1},{2,3},{4,5},{6,7},{8,9},{10,11},{12,13},{14,15},{16,17},{18,... | collective-permute-start | bytes 1769480 | tf_op jit(solution)/shard_map/ppermute | solution.py:368
  16.8 0.0 copy-done.2
  16.8 1.2 %shard_map.69 = (bf16[48,144]{1,0:T(8,128)(2,1)S(1)}, bf16[48,144]{1,0:T(8,128)(2,1)S(1)}) custom-call(f32[48]{0:T(128)S(1)} %copy-done.2), custom_call_target="tpu_custom_call" | custom-call | bytes 1048576 | tf_op jit(solution)/shard_map/pallas_call | solution.py:397
  18.0 0.0 collective-permute-done.1.outer
  18.0 0.0 collective-permute-done.inner
  18.0 0.0 copy-done
  18.0 2.2 %shard_map.70 = (f32[960,384]{1,0:T(8,128)S(1)}, f32[768,384]{1,0:T(8,128)S(1)}) custom-call(f32[1]{0:T(128)} %bitcast.side, f32[392,384]{1,0:T(8,128)S(1)} %copy-done, f32[392,384]{1,0:T(8,128)S(1)} %collective-permute-done.inner, f32[392,384]{1,0:T(8,128)S(1)} %collective-permute-done.1.outer, bf16[48,144]{1,0:T(8,128)(2,1)S(1)} %get-tuple-element.10.once), custom_call_target="tpu_custom_call" | custom-call | bytes 6291456 | tf_op jit(solution)/shard_map/pallas_call | solution.py:406
  20.2 3.9 %collective-permute-done.3.p_outer = f32[384,384]{1,0:T(8,128)S(1)} collective-permute-done((f32[384,384]{1,0:T(8,128)S(1)}, f32[384,384]{1,0:T(8,128)S(1)}, u32[]{:S(2)}, u32[]{:S(2)}) %collective-permute-start.3) | collective-permute-done | bytes 589856 | tf_op jit(solution)/shard_map/ppermute | solution.py:368
  24.1 0.0 collective-permute-done.2.p_inner
  24.1 3.6 %shard_map.72 = (f32[192,384]{1,0:T(8,128)S(1)}, f32[192,384]{1,0:T(8,128)S(1)}) custom-call(f32[1]{0:T(128)} %bitcast.side, f32[392,384]{1,0:T(8,128)S(1)} %copy-done, f32[392,384]{1,0:T(8,128)S(1)} %collective-permute-done.inner, f32[392,384]{1,0:T(8,128)S(1)} %collective-permute-done.1.outer, f32[384,384]{1,0:T(8,128)S(1)} %shard_map.71.p_own, ...), custom_call_target="tpu_custom_call" | custom-call | bytes 10485760 | tf_op jit(solution)/shard_map/pallas_call | solution.py:415
  27.7 1.9 %collective-permute-start.4 = (f32[192,384]{1,0:T(8,128)S(1)}, f32[192,384]{1,0:T(8,128)S(1)}, u32[]{:S(2)}, u32[]{:S(2)}) collective-permute-start(f32[192,384]{1,0:T(8,128)S(1)} %get-tuple-element.14.outer_rows), channel_id=1, source_target_pairs={{1,2},{3,4},{5,6},{7,8},{9,10},{11,12},{13,14},{15,16},{17,18},{19... | collective-permute-start | bytes 884744 | tf_op jit(solution)/shard_map/ppermute | solution.py:368
  29.7 1.9 %collective-permute-start.5 = (f32[192,384]{1,0:T(8,128)S(1)}, f32[192,384]{1,0:T(8,128)S(1)}, u32[]{:S(2)}, u32[]{:S(2)}) collective-permute-start(f32[192,384]{1,0:T(8,128)S(1)} %get-tuple-element.15.inner_rows), channel_id=1, source_target_pairs={{0,1},{2,3},{4,5},{6,7},{8,9},{10,11},{12,13},{14,15},{16,17},{18,... | collective-permute-start | bytes 884744 | tf_op jit(solution)/shard_map/ppermute | solution.py:368
  31.6 4.2 %collective-permute-done.4.b_outer = f32[192,384]{1,0:T(8,128)S(1)} collective-permute-done((f32[192,384]{1,0:T(8,128)S(1)}, f32[192,384]{1,0:T(8,128)S(1)}, u32[]{:S(2)}, u32[]{:S(2)}) %collective-permute-start.4) | collective-permute-done | bytes 294944 | tf_op jit(solution)/shard_map/ppermute | solution.py:368
  35.8 0.0 collective-permute-done.5.b_inner
  35.8 2.0 %shard_map.73 = (f32[384,384]{1,0:T(8,128)S(1)}, f32[48,2,4,384]{3,2,1,0:T(4,128)}) custom-call(f32[1]{0:T(128)} %bitcast.side, f32[392,384]{1,0:T(8,128)S(1)} %copy-done, f32[392,384]{1,0:T(8,128)S(1)} %collective-permute-done.inner, f32[392,384]{1,0:T(8,128)S(1)} %collective-permute-done.1.outer, f32[960,384]{1,0:T(8,128)S(1)} %get-tuple-element.11.x1, ...), custom_call_target="tpu_custom_call" | custom-call | bytes 6291456 | tf_op jit(solution)/shard_map/pallas_call | solution.py:425
  37.8 27.3 %all_to_all.20 = f32[16,24,384]{2,1,0:T(8,128)S(1)} all-to-all(f32[16,24,384]{2,1,0:T(8,128)S(1)} %bitcast.11), channel_id=1, replica_groups=mesh['group'=16,'tile'=32] {'group'}, dimensions={0} | all-to-all | bytes 1179648 | tf_op jit(solution)/shard_map/all_to_all | solution.py:434
  65.1 0.9 fusion
  66.0 10.1 %all_to_all.21 = f32[16,1,16]{2,1,0:T(1,128)S(1)} all-to-all(f32[16,1,16]{2,1,0:T(1,128)S(1)} %bitcast.12), channel_id=1, replica_groups=mesh['group'=16,'tile'=32] {'group'}, dimensions={0} | all-to-all | bytes 2048 | tf_op jit(solution)/shard_map/all_to_all | solution.py:444
  76.2 21.0 %all_to_all.22 = f32[32,1,16]{2,1,0:T(1,128)S(1)} all-to-all(f32[32,1,16]{2,1,0:T(1,128)S(1)} %broadcast_in_dim.15), channel_id=1, replica_groups=mesh['group'=16,'tile'=32] {'tile'}, dimensions={0} | all-to-all | bytes 4096 | tf_op jit(solution)/shard_map/all_to_all | solution.py:446
  97.1 0.1 reduce_sum.19
  97.2 0.5 multiply_bitcast_fusion
  (2 shorter events, 0.0 us)
Async XLA Ops:
  0.6 11.8 %copy-start.1 = (f32[1,48,2,4,384]{4,3,2,1,0:T(4,128)S(1)}, f32[1,48,2,4,384]{4,3,2,1,0:T(4,128)}, u32[]{:S(2)}) copy-start(f32[1,48,2,4,384]{4,3,2,1,0:T(4,128)} %param.6) | copy-start | bytes 1769476
  0.6 16.1 %copy-start.2 = (f32[48]{0:T(128)S(1)}, f32[48]{0:T(128)}, u32[]{:S(2)}) copy-start(f32[48]{0:T(128)} %mix.1) | copy-start | bytes 580
  2.8 15.3 %copy-start = (f32[392,384]{1,0:T(8,128)S(1)}, f32[392,384]{1,0:T(8,128)}, u32[]{:S(2)}) copy-start(f32[392,384]{1,0:T(8,128)} %shard_map.68.own) | copy-start | bytes 1806340
  2.8 15.2 %collective-permute-start.1 = (f32[392,384]{1,0:T(8,128)}, f32[392,384]{1,0:T(8,128)S(1)}, u32[]{:S(2)}, u32[]{:S(2)}) collective-permute-start(f32[392,384]{1,0:T(8,128)} %shard_map.68.own), channel_id=1, source_target_pairs={{1,2},{3,4},{5,6},{7,8},{9,10},{11,12},{13,14},{15,16},{17,18},{19... | collective-permute-start | bytes 1806344 | tf_op jit(solution)/shard_map/ppermute | solution.py:368
  7.5 10.5 %collective-permute-start = (f32[392,384]{1,0:T(8,128)}, f32[392,384]{1,0:T(8,128)S(1)}, u32[]{:S(2)}, u32[]{:S(2)}) collective-permute-start(f32[392,384]{1,0:T(8,128)} %shard_map.68.own), channel_id=1, source_target_pairs={{0,1},{2,3},{4,5},{6,7},{8,9},{10,11},{12,13},{14,15},{16,17},{18,... | collective-permute-start | bytes 1806344 | tf_op jit(solution)/shard_map/ppermute | solution.py:368
  12.9 11.2 %collective-permute-start.3 = (f32[384,384]{1,0:T(8,128)S(1)}, f32[384,384]{1,0:T(8,128)S(1)}, u32[]{:S(2)}, u32[]{:S(2)}) collective-permute-start(f32[384,384]{1,0:T(8,128)S(1)} %shard_map.71.p_own), channel_id=1, source_target_pairs={{1,2},{3,4},{5,6},{7,8},{9,10},{11,12},{13,14},{15,16},{17,18},{19... | collective-permute-start | bytes 1769480 | tf_op jit(solution)/shard_map/ppermute | solution.py:368
  14.9 9.3 %collective-permute-start.2 = (f32[384,384]{1,0:T(8,128)S(1)}, f32[384,384]{1,0:T(8,128)S(1)}, u32[]{:S(2)}, u32[]{:S(2)}) collective-permute-start(f32[384,384]{1,0:T(8,128)S(1)} %shard_map.71.p_own), channel_id=1, source_target_pairs={{0,1},{2,3},{4,5},{6,7},{8,9},{10,11},{12,13},{14,15},{16,17},{18,... | collective-permute-start | bytes 1769480 | tf_op jit(solution)/shard_map/ppermute | solution.py:368
  27.7 8.0 %collective-permute-start.4 = (f32[192,384]{1,0:T(8,128)S(1)}, f32[192,384]{1,0:T(8,128)S(1)}, u32[]{:S(2)}, u32[]{:S(2)}) collective-permute-start(f32[192,384]{1,0:T(8,128)S(1)} %get-tuple-element.14.outer_rows), channel_id=1, source_target_pairs={{1,2},{3,4},{5,6},{7,8},{9,10},{11,12},{13,14},{15,16},{17,18},{19... | collective-permute-start | bytes 884744 | tf_op jit(solution)/shard_map/ppermute | solution.py:368
  29.7 6.1 %collective-permute-start.5 = (f32[192,384]{1,0:T(8,128)S(1)}, f32[192,384]{1,0:T(8,128)S(1)}, u32[]{:S(2)}, u32[]{:S(2)}) collective-permute-start(f32[192,384]{1,0:T(8,128)S(1)} %get-tuple-element.15.inner_rows), channel_id=1, source_target_pairs={{0,1},{2,3},{4,5},{6,7},{8,9},{10,11},{12,13},{14,15},{16,17},{18,... | collective-permute-start | bytes 884744 | tf_op jit(solution)/shard_map/ppermute | solution.py:368

commit v3 on v2

--- a/solution.py
+++ b/solution.py
@@ -43,25 +43,25 @@
         copy.wait()
 
 
-def pack_rows(src, dst, sems, flipped):
+def place_of(f, r, rows, flipped):
+    return f * rows + jnp.where(flipped, rows - 1 - r, r)
+
+
+def pack_rows(src, dst, sems, flipped, base):
     lev, fields, rows, _ = src.shape
-    copies = []
-    for f in range(fields):
-        for r in range(rows):
-            place = f * rows + jnp.where(flipped, rows - 1 - r, r)
-            copies.append(
-                pltpu.make_async_copy(
-                    src.at[:, f, r, :],
-                    dst.at[pl.ds(pl.multiple_of(place * lev, 8), lev), :],
-                    sems.at[f * rows + r],
-                )
-            )
-    return copies
-
-
-def fill_lines(ints, out, flipped):
+    return [
+        pltpu.make_async_copy(
+            src.at[:, f, r, :],
+            dst.at[pl.ds(pl.multiple_of(base + place_of(f, r, rows, flipped) * lev, 8), lev), :],
+            sems.at[f * rows + r],
+        )
+        for f in range(fields)
+        for r in range(rows)
+    ]
+
+
+def fill_lines(ints, out, flipped, end):
     rows = ints.shape[1]
-    end = out.shape[0] - 2 * rows
     keep = 1.0 - relaxation * ints[0].astype(jnp.float32)
     drag = drag_rate * ints[1].astype(jnp.float32)
     for k, values in enumerate((keep, drag)):
@@ -71,25 +71,27 @@
             out[end + k * rows + r : end + k * rows + r + 1, :] = line
 
 
-def pack_state_kernel(side, x, land, relax, out, sems, ints, more_sems, staged, out_sems):
+def pack_kernel(side, x, p, land, relax, out, sems, ints, more_sems, staged, out_sems):
     flipped = side[0] < 0.0
+    lev, fields, rows, _ = x.shape
+    high = fields * rows * lev
     loads = [
         pltpu.make_async_copy(src, ints.at[k], more_sems.at[k])
         for k, src in enumerate((relax, land))
     ]
-    copies = pack_rows(x, staged, sems, flipped)
+    copies = pack_rows(x, staged, sems.at[0], flipped, 0)
+    copies += pack_rows(p, staged, sems.at[1], flipped, high + 2 * rows)
     start_all(loads)
     start_all(copies)
     wait_all(loads)
-    fill_lines(ints, staged, flipped)
-    lev, fields, rows, _ = x.shape
-    places = [
-        (f * rows + jnp.where(flipped, rows - 1 - r, r)) * lev
+    fill_lines(ints, staged, flipped, high)
+    pieces = [
+        pl.ds(pl.multiple_of(base + place_of(f, r, rows, flipped) * lev, 8), lev)
+        for base in (0, high + 2 * rows)
         for f in range(fields)
         for r in range(rows)
     ]
-    pieces = [pl.ds(pl.multiple_of(place, 8), lev) for place in places]
-    pieces.append(pl.ds(fields * rows * lev, 2 * rows))
+    pieces.append(pl.ds(high, 2 * rows))
     outs = [
         pltpu.make_async_copy(staged.at[piece], out.at[piece], out_sems.at[k])
         for k, piece in enumerate(pieces)
@@ -101,8 +103,12 @@
     wait_all(outs)
 
 
-def pack_field_kernel(side, x, out, sems):
-    copies = pack_rows(x, out, sems, side[0] < 0.0)
+def split_kernel(both, state, start, sems):
+    size = state.shape[0]
+    copies = [
+        pltpu.make_async_copy(both.at[pl.ds(0, size)], state, sems.at[0]),
+        pltpu.make_async_copy(both.at[pl.ds(size, start.shape[0])], start, sems.at[1]),
+    ]
     start_all(copies)
     wait_all(copies)
 
@@ -167,9 +173,14 @@
 INNER = (7, 6, 5, 4)
 
 
+def known(own, outer, inner):
+    pieces = ((own, OWN), (outer, OUTER), (inner, INNER))
+    return [piece for piece in pieces if piece[0] is not None]
+
+
 def state_rows(own, outer, inner):
     lev = (own.shape[0] - 8) // 8
-    return Rows(lev, (own, OWN), (outer, OUTER), (inner, INNER))
+    return Rows(lev, *known(own, outer, inner))
 
 
 class Factors:
@@ -177,7 +188,7 @@
         self.end = own.shape[0] - 8
         self.lev = self.end // 8
         self.where = {}
-        for buf, rows in ((own, OWN), (outer, OUTER), (inner, INNER)):
+        for buf, rows in known(own, outer, inner):
             for k, i in enumerate(rows):
                 self.where[i] = (buf, k)
 
@@ -285,73 +296,105 @@
     return tuple(range(first, last))
 
 
-def trajectory_kernel(side, own, inner, outer, once, x1, x2):
-    sign = side[0]
-    first = state_rows(own, outer, inner)
-    factors = Factors(own, outer, inner)
-    lev = first.lev
-    second = Rows(lev, (x1, span(-3, 7)))
-    third = Rows(lev, (x2, span(-2, 6)))
-    for i in span(-3, 7):
-        state_row(i, sign, first, factors, once[...], second)
-    for i in span(-2, 6):
-        state_row(i, sign, second, factors, once[...], third)
+def forward(side, state, start, factors, xs, moved, once, twice, ranges):
+    for i in ranges[0]:
+        state_row(i, side, state, factors, once, xs[0])
+    for i in ranges[1]:
+        state_row(i, side, xs[0], factors, once, xs[1])
+    for i in ranges[2]:
+        tangent_row(i, side, start, state, factors, once, moved[0], False)
+    for i in ranges[3]:
+        tangent_row(i, side, moved[0], xs[0], factors, once, moved[1], False)
+    for i in ranges[4]:
+        tangent_row(i, side, moved[1], xs[1], factors, twice, moved[2], True)
+
+
+def inner_forward_kernel(
+    side, own, inner, p_own, p_inner, once, twice,
+    x1, x2, t1, t2, b2,
+):
+    state = state_rows(own, None, inner)
+    lev = state.lev
+    forward(
+        side[0],
+        state,
+        Rows(lev, (p_own, OWN), (p_inner, INNER)),
+        Factors(own, None, inner),
+        (Rows(lev, (x1, span(1, 7))), Rows(lev, (x2, span(2, 6)))),
+        (Rows(lev, (t1, span(1, 7))), Rows(lev, (t2, span(2, 6))), Rows(lev, (b2, span(3, 5)))),
+        once[...],
+        twice[...],
+        (span(1, 7), span(2, 6), span(1, 7), span(2, 6), span(3, 5)),
+    )
 
 
 def forward_kernel(
-    side, own, inner, outer, p_own, p_inner, p_outer, x1, x2, once, twice,
-    outer_rows, inner_rows,
-    t1, t2, b2,
+    side, own, p_own, both_outer, x1_in, x2_in, t1_in, t2_in, b2_in, once, twice,
+    outer_rows, inner_rows, x1,
+    x2, t1, t2, b2,
 ):
     sign = side[0]
-    first = state_rows(own, outer, inner)
-    factors = Factors(own, outer, inner)
-    lev = first.lev
-    second = Rows(lev, (x1, span(-3, 7)))
-    third = Rows(lev, (x2, span(-2, 6)))
-    start = Rows(lev, (p_own, OWN), (p_outer, OUTER), (p_inner, INNER))
-    once_moved = Rows(lev, (t1, span(-3, 7)))
-    twice_moved = Rows(lev, (t2, span(-2, 6)))
-    back = Rows(lev, (b2, span(-1, 5)))
+    size = own.shape[0]
+    outer = both_outer.at[pl.ds(0, size)]
+    p_outer = both_outer.at[pl.ds(size, p_own.shape[0])]
+    state = state_rows(own, outer, None)
+    factors = Factors(own, outer, None)
+    lev = state.lev
+    xs = (
+        Rows(lev, (x1, span(-3, 1)), (x1_in, span(1, 7))),
+        Rows(lev, (x2, span(-2, 2)), (x2_in, span(2, 6))),
+    )
+    moved = (
+        Rows(lev, (t1, span(-3, 1)), (t1_in, span(1, 7))),
+        Rows(lev, (t2, span(-2, 2)), (t2_in, span(2, 6))),
+        Rows(lev, (b2, span(-1, 3)), (b2_in, span(3, 5))),
+    )
+    forward(
+        sign,
+        state,
+        Rows(lev, (p_own, OWN), (p_outer, OUTER)),
+        factors,
+        xs,
+        moved,
+        once[...],
+        twice[...],
+        (span(-3, 1), span(-2, 2), span(-3, 1), span(-2, 2), span(-1, 3)),
+    )
     out = Rows(lev, (outer_rows, (0, 1)), (inner_rows, (3, 2)))
-    for i in span(-3, 7):
-        tangent_row(i, sign, start, first, factors, once[...], once_moved, False)
-    for i in span(-2, 6):
-        tangent_row(i, sign, once_moved, second, factors, once[...], twice_moved, False)
-    for i in span(-1, 5):
-        tangent_row(i, sign, twice_moved, third, factors, twice[...], back, True)
     for i in OWN:
-        adjoint_solved(i, sign, back, third, factors, once[...], out)
+        adjoint_solved(i, sign, moved[2], xs[1], factors, once[...], out)
 
 
 def backward_kernel(
-    side, own, inner, outer, x1, outer_rows, inner_rows, b_outer, b_inner, once,
+    side, own, inner, both_outer, x1, x1_in, outer_rows, inner_rows, b_outer, b_inner, once,
     packed, field,
     b0, sems,
 ):
     sign = side[0]
-    first = state_rows(own, outer, inner)
+    outer = both_outer.at[pl.ds(0, own.shape[0])]
+    state = state_rows(own, outer, inner)
     factors = Factors(own, outer, inner)
-    lev = first.lev
-    second = Rows(lev, (x1, span(-3, 7)))
+    lev = state.lev
+    second = Rows(lev, (x1, span(-3, 1)), (x1_in, span(1, 7)))
     back = Rows(
         lev, (outer_rows, (0, 1)), (inner_rows, (3, 2)), (b_outer, (-1, -2)), (b_inner, (4, 5))
     )
     last = Rows(lev, (b0, span(-1, 5)))
     for i in span(-1, 5):
         adjoint_solved(i, sign, back, second, factors, once[...], last)
-    outs = []
+    copies = []
     for i in OWN:
         row = jnp.where(sign < 0.0, 3 - i, i)
-        for f, value in enumerate(adjoint_row(i, sign, last, first, factors)):
+        for f, value in enumerate(adjoint_row(i, sign, last, state, factors)):
             k = 4 * f + i
             packed[k * lev : (k + 1) * lev, :] = value
-            copy = pltpu.make_async_copy(
-                packed.at[pl.ds(k * lev, lev), :], field.at[:, f, row, :], sems.at[k]
+            copies.append(
+                pltpu.make_async_copy(
+                    packed.at[pl.ds(k * lev, lev), :], field.at[:, f, row, :], sems.at[k]
+                )
             )
-            copy.start()
-            outs.append(copy)
-    wait_all(outs)
+            copies[-1].start()
+    wait_all(copies)
 
 
 def per_device(initial_state, perturbation, land_sea, relax_level, vertical_mix):
@@ -370,28 +413,35 @@
     def buffer(n):
         return pltpu.VMEM((fields * n * lev, width), jnp.float32)
 
-    state = run(
-        pack_state_kernel,
-        f32(high + 2 * rows, width),
-        [SMEM, ANY, ANY, ANY],
+    def rows_of(n):
+        return f32(fields * n * lev, width)
+
+    both = run(
+        pack_kernel,
+        f32(2 * high + 2 * rows, width),
+        [SMEM] + [ANY] * 4,
         ANY,
         [
-            dma((fields * rows,)),
+            dma((2, fields * rows)),
             pltpu.VMEM((2, rows, width), jnp.int32),
             dma((2,)),
-            pltpu.VMEM((high + 2 * rows, width), jnp.float32),
-            dma((fields * rows + 1,)),
+            pltpu.VMEM((2 * high + 2 * rows, width), jnp.float32),
+            dma((2 * fields * rows + 1,)),
         ],
         2**20,
         60 * 2**20,
-    )(side, initial_state, land_sea, relax_level)
+    )(side, initial_state, perturbation[0], land_sea, relax_level)
+    both_outer = swap(both, across)
+    state, start = run(
+        split_kernel,
+        (f32(high + 2 * rows, width), f32(high, width)),
+        [ANY],
+        (VMEM, VMEM),
+        [dma((2,))],
+        nbytes=2**18,
+    )(both)
     state_inner = swap(state, within)
-    state_outer = swap(state, across)
-    start = run(
-        pack_field_kernel, f32(high, width), [SMEM, ANY], VMEM, [dma((fields * rows,))], nbytes=2**20
-    )(side, perturbation[0])
     start_inner = swap(start, within)
-    start_outer = swap(start, across)
 
     weights = jax.ShapeDtypeStruct((lev, 3 * lev), jnp.bfloat16)
     once, twice = run(
@@ -400,36 +450,35 @@
         [SMEM],
         (VMEM, VMEM),
         [pltpu.VMEM((lev, 3 * lev), jnp.float32)],
+        nbytes=2**18,
+    )(vertical_mix)
+
+    x1_in, x2_in, t1, t2, b2 = run(
+        inner_forward_kernel,
+        (rows_of(6), rows_of(4), rows_of(6), rows_of(4), rows_of(2)),
+        [SMEM] + [VMEM] * 6,
+        (VMEM,) * 5,
+        [],
+        nbytes=2**18,
+    )(side, state, state_inner, start, start_inner, once, twice)
+    outer_rows, inner_rows, x1 = run(
+        forward_kernel,
+        (rows_of(2), rows_of(2), rows_of(4)),
+        [SMEM] + [VMEM] * 10,
+        (VMEM,) * 3,
+        [buffer(4)] * 4,
         nbytes=2**20,
-    )(vertical_mix)
-
-    x1, x2 = run(
-        trajectory_kernel,
-        (f32(fields * 10 * lev, width), f32(fields * 8 * lev, width)),
-        [SMEM] + [VMEM] * 4,
-        (VMEM, VMEM),
-        [],
-        nbytes=6 * 2**20,
-    )(side, state, state_inner, state_outer, once)
-
-    outer_rows, inner_rows = run(
-        forward_kernel,
-        (f32(fields * 2 * lev, width), f32(fields * 2 * lev, width)),
-        [SMEM] + [VMEM] * 10,
-        (VMEM, VMEM),
-        [buffer(10), buffer(8), buffer(6)],
-        nbytes=10 * 2**20,
-    )(side, state, state_inner, state_outer, start, start_inner, start_outer, x1, x2, once, twice)
+    )(side, state, start, both_outer, x1_in, x2_in, t1, t2, b2, once, twice)
 
     b_outer, b_inner = swap(outer_rows, across), swap(inner_rows, within)
     packed, field = run(
         backward_kernel,
         (f32(high, width), f32(lev, fields, rows, width)),
-        [SMEM] + [VMEM] * 9,
+        [SMEM] + [VMEM] * 10,
         (VMEM, ANY),
         [buffer(6), dma((fields * rows,))],
-        nbytes=6 * 2**20,
-    )(side, state, state_inner, state_outer, x1, outer_rows, inner_rows, b_outer, b_inner, once)
+        nbytes=2**20,
+    )(side, state, state_inner, both_outer, x1, x1_in, outer_rows, inner_rows, b_outer, b_inner, once)
 
     share = lax.all_to_all(
         packed.reshape(members, high // members, width), "group", 0, 0, tiled=True

time: 98.1 us -> 97.9 us (level)
  waiting for transfers between devices: 8.09 us -> 4.04 us
  blocking collectives: 58.4 us -> 60.8 us
  local copies, waits for them, and re-layouts: 0.03 us -> 1.3 us
    ppermute x6 -> x5, waiting for transfers between devices: 8.09 us -> 4.04 us  [swap(): return lax.ppermute(value, 'tile', pairs + [(j, i) for i, j in pairs])]
    all_to_all x1, blocking collectives: 27.3 us -> 29.7 us  [per_device(): lax.all_to_all(packed.reshape(members, high // members, width), 'group',...]
    unnamed x6 -> x4, local copies, waits for them, and re-layouts: 0.01 us -> 1.28 us
    ppermute x6 -> x5, starting transfers between devices: 17.3 us -> 17 us  [swap(): return lax.ppermute(value, 'tile', pairs + [(j, i) for i, j in pairs])]
  transfers between devices with their start and end apart: 6 -> 5, of which waited for: 2 -> 3; matrix products, arithmetic and copies ran while one was open for 0% -> 0% of each run, Pallas kernels for 4% -> 5%
where the time goes in v3:
time: 97.9 us; the launch traced here: 97.4 us
  blocking collectives  60.8 us (62%)
  starting transfers between devices  17 us (17%)
  Pallas kernels  12.1 us (12%)
  waiting for transfers between devices  4.04 us (4%)
  local copies, waits for them, and re-layouts  1.3 us (1%)
    all_to_all x1, blocking collectives, per_device(): lax.all_to_all(packed.reshape(members, high // members, width), 'group',...  29.7 us
    all_to_all x1, blocking collectives, per_device(): row = jnp.sum(lax.all_to_all(spread, 'tile', 0, 0, tiled=True), axis=0)  20.9 us
    ppermute x5, starting transfers between devices, swap(): return lax.ppermute(value, 'tile', pairs + [(j, i) for i, j in pairs])  17 us
    all_to_all x1, blocking collectives, per_device(): row = jnp.sum(lax.all_to_all(products, 'group', 0, 0, tiled=True), axis=0)  10.2 us
    ppermute x5, waiting for transfers between devices, swap(): return lax.ppermute(value, 'tile', pairs + [(j, i) for i, j in pairs])  4.04 us
    pallas_call x1, Pallas kernels, per_device(): run(forward_kernel, (rows_of(2), rows_of(2), rows_of(4)), [SMEM] + [VMEM]...  3.18 us
    pallas_call x1, Pallas kernels, per_device(): run(inner_forward_kernel, (rows_of(6), rows_of(4), rows_of(6), rows_of(4)...  2.98 us
    pallas_call x1, Pallas kernels, per_device(): run(pack_kernel, f32(2 * high + 2 * rows, width), [SMEM] + [ANY] * 4, ANY...  2.47 us
  transfers between devices with their start and end apart: 5, of which 3 were waited for; matrix products, arithmetic and copies ran while one was open for 0% of the time, Pallas kernels for 5%

profile of v3, /device:TPU:1, one launch (start us, length us, event | category | flops | bytes accessed | tf_op | source)
XLA Modules:
  0.0 97.4 jit_solution(9597829974887308943)
XLA Ops:
  0.6 2.5 %shard_map.68.both = f32[776,384]{1,0:T(8,128)} custom-call(f32[1]{0:T(128)} %bitcast.side, f32[48,2,4,384]{3,2,1,0:T(4,128)} %x.1, f32[48,2,4,384]{3,2,1,0:T(4,128)} %bitcast.11, s32[4,384]{1,0:T(4,128)} %land.1, s32[4,384]{1,0:T(4,128)} %relax.1), custom_call_target="tpu_custom_call" | custom-call | bytes 1048576 | tf_op jit(solution)/shard_map/pallas_call | solution.py:419
  3.1 4.6 %collective-permute-start.1 = (f32[776,384]{1,0:T(8,128)}, f32[776,384]{1,0:T(8,128)S(1)}, u32[]{:S(2)}, u32[]{:S(2)}) collective-permute-start(f32[776,384]{1,0:T(8,128)} %shard_map.68.both), channel_id=1, source_target_pairs={{1,2},{3,4},{5,6},{7,8},{9,10},{11,12},{13,14},{15,16},{17,18},{19... | collective-permute-start | bytes 3575816 | tf_op jit(solution)/shard_map/ppermute | solution.py:411
  7.7 0.0 copy-start
  7.7 1.3 %copy-done = f32[776,384]{1,0:T(8,128)S(1)} copy-done((f32[776,384]{1,0:T(8,128)S(1)}, f32[776,384]{1,0:T(8,128)}, u32[]{:S(2)}) %copy-start) | copy-done | bytes 1191960
  9.0 0.0 copy-start.1
  9.0 0.3 shard_map.69
  9.3 4.9 %collective-permute-start = (f32[392,384]{1,0:T(8,128)S(1)}, f32[392,384]{1,0:T(8,128)S(1)}, u32[]{:S(2)}, u32[]{:S(2)}) collective-permute-start(f32[392,384]{1,0:T(8,128)S(1)} %get-tuple-element.16.own), channel_id=1, source_target_pairs={{0,1},{2,3},{4,5},{6,7},{8,9},{10,11},{12,13},{14,15},{16,17},{18,... | collective-permute-start | bytes 1806344 | tf_op jit(solution)/shard_map/ppermute | solution.py:411
  14.2 1.9 %collective-permute-start.2 = (f32[384,384]{1,0:T(8,128)S(1)}, f32[384,384]{1,0:T(8,128)S(1)}, u32[]{:S(2)}, u32[]{:S(2)}) collective-permute-start(f32[384,384]{1,0:T(8,128)S(1)} %get-tuple-element.17.p_own), channel_id=1, source_target_pairs={{0,1},{2,3},{4,5},{6,7},{8,9},{10,11},{12,13},{14,15},{16,17},{18,... | collective-permute-start | bytes 1769480 | tf_op jit(solution)/shard_map/ppermute | solution.py:411
  16.1 0.0 copy-done.1
  16.1 1.2 %shard_map.70 = (bf16[48,144]{1,0:T(8,128)(2,1)S(1)}, bf16[48,144]{1,0:T(8,128)(2,1)S(1)}) custom-call(f32[48]{0:T(128)S(1)} %copy-done.1), custom_call_target="tpu_custom_call" | custom-call | bytes 262144 | tf_op jit(solution)/shard_map/pallas_call | solution.py:447
  17.4 0.7 collective-permute-done.2.p_inner
  18.1 0.0 collective-permute-done.inner
  18.1 3.0 %shard_map.71 = (f32[576,384]{1,0:T(8,128)S(1)}, f32[384,384]{1,0:T(8,128)S(1)}, f32[576,384]{1,0:T(8,128)S(1)}, f32[384,384]{1,0:T(8,128)S(1)}, f32[192,384]{1,0:T(8,128)S(1)}) custom-call(f32[1]{0:T(128)} %bitcast.side, f32[392,384]{1,0:T(8,128)S(1)} %get-tuple-element.16.own, f32[392,384]{1,0:T(8,128)S(1)} %collective-permute-done.inner, ...), custom_call_target="tpu_custom_call" | custom-call | bytes 262144 | tf_op jit(solution)/shard_map/pallas_call | solution.py:456
  21.1 0.8 collective-permute-done.1.both_outer
  21.9 3.2 %shard_map.72 = (f32[192,384]{1,0:T(8,128)S(1)}, f32[192,384]{1,0:T(8,128)S(1)}, f32[384,384]{1,0:T(8,128)S(1)}) custom-call(f32[1]{0:T(128)} %bitcast.side, f32[392,384]{1,0:T(8,128)S(1)} %get-tuple-element.16.own, f32[384,384]{1,0:T(8,128)S(1)} %get-tuple-element.17.p_own, f32[776,384]{1,0:T(8,128)S(1)} %collective-permute-done.1.both_outer, ...), custom_call_target="tpu_custom_call" | custom-call | bytes 1048576 | tf_op jit(solution)/shard_map/pallas_call | solution.py:464
  25.1 3.6 %collective-permute-start.3 = (f32[192,384]{1,0:T(8,128)S(1)}, f32[192,384]{1,0:T(8,128)S(1)}, u32[]{:S(2)}, u32[]{:S(2)}) collective-permute-start(f32[192,384]{1,0:T(8,128)S(1)} %get-tuple-element.26.outer_rows), channel_id=1, source_target_pairs={{1,2},{3,4},{5,6},{7,8},{9,10},{11,12},{13,14},{15,16},{17,18},{19... | collective-permute-start | bytes 884744 | tf_op jit(solution)/shard_map/ppermute | solution.py:411
  28.8 1.9 %collective-permute-start.4 = (f32[192,384]{1,0:T(8,128)S(1)}, f32[192,384]{1,0:T(8,128)S(1)}, u32[]{:S(2)}, u32[]{:S(2)}) collective-permute-start(f32[192,384]{1,0:T(8,128)S(1)} %get-tuple-element.27.inner_rows), channel_id=1, source_target_pairs={{0,1},{2,3},{4,5},{6,7},{8,9},{10,11},{12,13},{14,15},{16,17},{18,... | collective-permute-start | bytes 884744 | tf_op jit(solution)/shard_map/ppermute | solution.py:411
  30.7 2.5 %collective-permute-done.3.b_outer = f32[192,384]{1,0:T(8,128)S(1)} collective-permute-done((f32[192,384]{1,0:T(8,128)S(1)}, f32[192,384]{1,0:T(8,128)S(1)}, u32[]{:S(2)}, u32[]{:S(2)}) %collective-permute-start.3) | collective-permute-done | bytes 294944 | tf_op jit(solution)/shard_map/ppermute | solution.py:411
  33.2 0.0 collective-permute-done.4.b_inner
  33.2 2.0 %shard_map.73 = (f32[384,384]{1,0:T(8,128)S(1)}, f32[48,2,4,384]{3,2,1,0:T(4,128)}) custom-call(f32[1]{0:T(128)} %bitcast.side, f32[392,384]{1,0:T(8,128)S(1)} %get-tuple-element.16.own, f32[392,384]{1,0:T(8,128)S(1)} %collective-permute-done.inner, f32[776,384]{1,0:T(8,128)S(1)} %collective-permute-done.1.both_outer, f32[384,384]{1,0:T(8,128)S(1)} %get-tuple-element.25.x1, ...), custom_call_target="tpu_custom_call" | custom-call | bytes 1048576 | tf_op jit(solution)/shard_map/pallas_call | solution.py:474
  35.2 29.7 %all_to_all.20 = f32[16,24,384]{2,1,0:T(8,128)S(1)} all-to-all(f32[16,24,384]{2,1,0:T(8,128)S(1)} %bitcast.10), channel_id=1, replica_groups=mesh['group'=16,'tile'=32] {'group'}, dimensions={0} | all-to-all | bytes 1179648 | tf_op jit(solution)/shard_map/all_to_all | solution.py:483
  64.9 0.8 fusion
  65.7 10.2 %all_to_all.21 = f32[16,1,16]{2,1,0:T(1,128)S(1)} all-to-all(f32[16,1,16]{2,1,0:T(1,128)S(1)} %bitcast.12), channel_id=1, replica_groups=mesh['group'=16,'tile'=32] {'group'}, dimensions={0} | all-to-all | bytes 2048 | tf_op jit(solution)/shard_map/all_to_all | solution.py:493
  75.9 20.9 %all_to_all.22 = f32[32,1,16]{2,1,0:T(1,128)S(1)} all-to-all(f32[32,1,16]{2,1,0:T(1,128)S(1)} %broadcast_in_dim.15), channel_id=1, replica_groups=mesh['group'=16,'tile'=32] {'tile'}, dimensions={0} | all-to-all | bytes 4096 | tf_op jit(solution)/shard_map/all_to_all | solution.py:495
  96.9 0.1 reduce_sum.19
  96.9 0.5 multiply_bitcast_fusion
  (2 shorter events, 0.0 us)
Async XLA Ops:
  3.1 18.8 %collective-permute-start.1 = (f32[776,384]{1,0:T(8,128)}, f32[776,384]{1,0:T(8,128)S(1)}, u32[]{:S(2)}, u32[]{:S(2)}) collective-permute-start(f32[776,384]{1,0:T(8,128)} %shard_map.68.both), channel_id=1, source_target_pairs={{1,2},{3,4},{5,6},{7,8},{9,10},{11,12},{13,14},{15,16},{17,18},{19... | collective-permute-start | bytes 3575816 | tf_op jit(solution)/shard_map/ppermute | solution.py:411
  7.7 1.3 %copy-start = (f32[776,384]{1,0:T(8,128)S(1)}, f32[776,384]{1,0:T(8,128)}, u32[]{:S(2)}) copy-start(f32[776,384]{1,0:T(8,128)} %shard_map.68.both) | copy-start | bytes 3575812
  9.0 7.1 %copy-start.1 = (f32[48]{0:T(128)S(1)}, f32[48]{0:T(128)}, u32[]{:S(2)}) copy-start(f32[48]{0:T(128)} %mix.1) | copy-start | bytes 580
  9.3 8.8 %collective-permute-start = (f32[392,384]{1,0:T(8,128)S(1)}, f32[392,384]{1,0:T(8,128)S(1)}, u32[]{:S(2)}, u32[]{:S(2)}) collective-permute-start(f32[392,384]{1,0:T(8,128)S(1)} %get-tuple-element.16.own), channel_id=1, source_target_pairs={{0,1},{2,3},{4,5},{6,7},{8,9},{10,11},{12,13},{14,15},{16,17},{18,... | collective-permute-start | bytes 1806344 | tf_op jit(solution)/shard_map/ppermute | solution.py:411
  14.2 3.9 %collective-permute-start.2 = (f32[384,384]{1,0:T(8,128)S(1)}, f32[384,384]{1,0:T(8,128)S(1)}, u32[]{:S(2)}, u32[]{:S(2)}) collective-permute-start(f32[384,384]{1,0:T(8,128)S(1)} %get-tuple-element.17.p_own), channel_id=1, source_target_pairs={{0,1},{2,3},{4,5},{6,7},{8,9},{10,11},{12,13},{14,15},{16,17},{18,... | collective-permute-start | bytes 1769480 | tf_op jit(solution)/shard_map/ppermute | solution.py:411
  25.1 8.0 %collective-permute-start.3 = (f32[192,384]{1,0:T(8,128)S(1)}, f32[192,384]{1,0:T(8,128)S(1)}, u32[]{:S(2)}, u32[]{:S(2)}) collective-permute-start(f32[192,384]{1,0:T(8,128)S(1)} %get-tuple-element.26.outer_rows), channel_id=1, source_target_pairs={{1,2},{3,4},{5,6},{7,8},{9,10},{11,12},{13,14},{15,16},{17,18},{19... | collective-permute-start | bytes 884744 | tf_op jit(solution)/shard_map/ppermute | solution.py:411
  28.8 4.4 %collective-permute-start.4 = (f32[192,384]{1,0:T(8,128)S(1)}, f32[192,384]{1,0:T(8,128)S(1)}, u32[]{:S(2)}, u32[]{:S(2)}) collective-permute-start(f32[192,384]{1,0:T(8,128)S(1)} %get-tuple-element.27.inner_rows), channel_id=1, source_target_pairs={{0,1},{2,3},{4,5},{6,7},{8,9},{10,11},{12,13},{14,15},{16,17},{18,... | collective-permute-start | bytes 884744 | tf_op jit(solution)/shard_map/ppermute | solution.py:411

commit v4 on v3

--- a/solution.py
+++ b/solution.py
@@ -71,7 +71,7 @@
             out[end + k * rows + r : end + k * rows + r + 1, :] = line
 
 
-def pack_kernel(side, x, p, land, relax, out, sems, ints, more_sems, staged, out_sems):
+def pack_kernel(side, x, p, land, relax, out, deep, sems, ints, more_sems, staged, out_sems):
     flipped = side[0] < 0.0
     lev, fields, rows, _ = x.shape
     high = fields * rows * lev
@@ -100,7 +100,34 @@
     for copy, onward in zip(copies, outs):
         copy.wait()
         onward.start()
+    two, four = 2 * lev, 4 * lev
+    shift = 2 * rows + fields * two
+    inner = [(f * four + two, f * two, two) for f in range(fields)]
+    inner += [(high, fields * two, 2 * rows)]
+    inner += [(high + 2 * rows + f * four + two, shift + f * two, two) for f in range(fields)]
+    for k, (at, to, size) in enumerate(inner):
+        outs.append(
+            pltpu.make_async_copy(
+                staged.at[pl.ds(at, size)], deep.at[pl.ds(to, size)], out_sems.at[len(pieces) + k]
+            )
+        )
+        outs[-1].start()
     wait_all(outs)
+
+
+def relay_kernel(both, after, state_part, start_part, sems):
+    two = start_part.shape[0] // 2
+    ends = state_part.shape[0] - 2 * two
+    high = (both.shape[0] - ends) // 2
+    moves = [(0, state_part, 0, two), (2 * two, state_part, two, two)]
+    moves += [(high, state_part, 2 * two, ends)]
+    moves += [(high + ends, start_part, 0, two), (high + ends + 2 * two, start_part, two, two)]
+    copies = [
+        pltpu.make_async_copy(both.at[pl.ds(at, size)], dst.at[pl.ds(to, size)], sems.at[k])
+        for k, (at, dst, to, size) in enumerate(moves)
+    ]
+    start_all(copies)
+    wait_all(copies)
 
 
 def split_kernel(both, state, start, sems):
@@ -171,30 +198,24 @@
 OWN = (0, 1, 2, 3)
 OUTER = (-1, -2, -3, -4)
 INNER = (7, 6, 5, 4)
-
-
-def known(own, outer, inner):
-    pieces = ((own, OWN), (outer, OUTER), (inner, INNER))
-    return [piece for piece in pieces if piece[0] is not None]
-
-
-def state_rows(own, outer, inner):
-    lev = (own.shape[0] - 8) // 8
-    return Rows(lev, *known(own, outer, inner))
+DEEP = (-6, -5)
+FAR = (8, 9)
+
+
+def span(first, last):
+    return tuple(range(first, last))
 
 
 class Factors:
-    def __init__(self, own, outer, inner):
-        self.end = own.shape[0] - 8
-        self.lev = self.end // 8
+    def __init__(self, *pieces):
         self.where = {}
-        for buf, rows in known(own, outer, inner):
+        for buf, rows, first in pieces:
             for k, i in enumerate(rows):
-                self.where[i] = (buf, k)
+                self.where[i] = (buf, first + k)
 
     def line(self, i, kind):
         buf, k = self.where[i]
-        at = self.end + 4 * kind + k
+        at = buf.shape[0] - 8 + 4 * kind + k
         return jnp.broadcast_to(buf[at : at + 1, :], (8, buf.shape[1]))
 
     def keep(self, i):
@@ -292,100 +313,150 @@
         out.write(f, i, value * keep)
 
 
-def span(first, last):
-    return tuple(range(first, last))
-
-
-def forward(side, state, start, factors, xs, moved, once, twice, ranges):
+class Fields:
+    def __init__(self, lev, **pieces):
+        self.rows = {name: Rows(lev, *piece) for name, piece in pieces.items()}
+
+    def __getattr__(self, name):
+        return self.rows[name]
+
+
+def forward(side, rows, factors, once, twice, ranges):
     for i in ranges[0]:
-        state_row(i, side, state, factors, once, xs[0])
+        state_row(i, side, rows.x0, factors, once, rows.x1)
     for i in ranges[1]:
-        state_row(i, side, xs[0], factors, once, xs[1])
+        state_row(i, side, rows.x1, factors, once, rows.x2)
     for i in ranges[2]:
-        tangent_row(i, side, start, state, factors, once, moved[0], False)
+        tangent_row(i, side, rows.p, rows.x0, factors, once, rows.t1, False)
     for i in ranges[3]:
-        tangent_row(i, side, moved[0], xs[0], factors, once, moved[1], False)
+        tangent_row(i, side, rows.t1, rows.x1, factors, once, rows.t2, False)
     for i in ranges[4]:
-        tangent_row(i, side, moved[1], xs[1], factors, twice, moved[2], True)
-
-
-def inner_forward_kernel(
+        tangent_row(i, side, rows.t2, rows.x2, factors, twice, rows.b2, True)
+    for i in ranges[5]:
+        adjoint_solved(i, side, rows.b2, rows.x2, factors, once, rows.b1)
+
+
+def own_kernel(
     side, own, inner, p_own, p_inner, once, twice,
     x1, x2, t1, t2, b2,
 ):
-    state = state_rows(own, None, inner)
-    lev = state.lev
+    lev = p_own.shape[0] // 8
+    rows = Fields(
+        lev,
+        x0=((own, OWN), (inner, INNER)),
+        p=((p_own, OWN), (p_inner, INNER)),
+        x1=((x1, span(1, 7)),),
+        x2=((x2, span(2, 6)),),
+        t1=((t1, span(1, 7)),),
+        t2=((t2, span(2, 6)),),
+        b2=((b2, span(3, 5)),),
+    )
     forward(
         side[0],
-        state,
-        Rows(lev, (p_own, OWN), (p_inner, INNER)),
-        Factors(own, None, inner),
-        (Rows(lev, (x1, span(1, 7))), Rows(lev, (x2, span(2, 6)))),
-        (Rows(lev, (t1, span(1, 7))), Rows(lev, (t2, span(2, 6))), Rows(lev, (b2, span(3, 5)))),
+        rows,
+        Factors((own, OWN, 0), (inner, INNER, 0)),
         once[...],
         twice[...],
-        (span(1, 7), span(2, 6), span(1, 7), span(2, 6), span(3, 5)),
-    )
-
-
-def forward_kernel(
-    side, own, p_own, both_outer, x1_in, x2_in, t1_in, t2_in, b2_in, once, twice,
-    outer_rows, inner_rows, x1,
-    x2, t1, t2, b2,
+        (span(1, 7), span(2, 6), span(1, 7), span(2, 6), span(3, 5), ()),
+    )
+
+
+def outer_kernel(
+    side, own, p_own, both_outer, x1_own, x2_own, t1_own, t2_own, b2_own, once, twice,
+    x1, x2, t1, t2, b2, b1,
 ):
-    sign = side[0]
     size = own.shape[0]
     outer = both_outer.at[pl.ds(0, size)]
     p_outer = both_outer.at[pl.ds(size, p_own.shape[0])]
-    state = state_rows(own, outer, None)
-    factors = Factors(own, outer, None)
-    lev = state.lev
-    xs = (
-        Rows(lev, (x1, span(-3, 1)), (x1_in, span(1, 7))),
-        Rows(lev, (x2, span(-2, 2)), (x2_in, span(2, 6))),
-    )
-    moved = (
-        Rows(lev, (t1, span(-3, 1)), (t1_in, span(1, 7))),
-        Rows(lev, (t2, span(-2, 2)), (t2_in, span(2, 6))),
-        Rows(lev, (b2, span(-1, 3)), (b2_in, span(3, 5))),
-    )
+    rows = Fields(
+        p_own.shape[0] // 8,
+        x0=((own, OWN), (outer, OUTER)),
+        p=((p_own, OWN), (p_outer, OUTER)),
+        x1=((x1, span(-3, 1)), (x1_own, span(1, 7))),
+        x2=((x2, span(-2, 2)), (x2_own, span(2, 6))),
+        t1=((t1, span(-3, 1)), (t1_own, span(1, 7))),
+        t2=((t2, span(-2, 2)), (t2_own, span(2, 6))),
+        b2=((b2, span(-1, 3)), (b2_own, span(3, 5))),
+        b1=((b1, OWN),),
+    )
+    forward(
+        side[0],
+        rows,
+        Factors((own, OWN, 0), (outer, OUTER, 0)),
+        once[...],
+        twice[...],
+        (span(-3, 1), span(-2, 2), span(-3, 1), span(-2, 2), span(-1, 3), OWN),
+    )
+
+
+def far_kernel(
+    side, inner, p_inner, far, p_far, x1_own, x2_own, t1_own, t2_own, b2_own, once, twice,
+    b1,
+    x1, x2, t1, t2, b2,
+):
+    rows = Fields(
+        p_inner.shape[0] // 8,
+        x0=((inner, INNER), (far, FAR)),
+        p=((p_inner, INNER), (p_far, FAR)),
+        x1=((x1_own, span(1, 7)), (x1, (7, 8))),
+        x2=((x2_own, span(2, 6)), (x2, (6, 7))),
+        t1=((t1_own, span(1, 7)), (t1, (7, 8))),
+        t2=((t2_own, span(2, 6)), (t2, (6, 7))),
+        b2=((b2_own, span(3, 5)), (b2, (5, 6))),
+        b1=((b1, (4, 5)),),
+    )
+    forward(
+        side[0],
+        rows,
+        Factors((inner, INNER, 0), (far, FAR, 0)),
+        once[...],
+        twice[...],
+        ((7, 8), (6, 7), (7, 8), (6, 7), (5, 6), (4, 5)),
+    )
+
+
+def last_kernel(
+    side, own, inner, both_outer, deep, x1_own, x1_outer, x2_outer, t1_outer, t2_outer,
+    b2_outer, b1_own, b1_far, once, twice,
+    packed, field,
+    x1, x2, t1, t2, b2, b1, b0, sems,
+):
+    sign = side[0]
+    high = packed.shape[0]
+    lev = high // 8
+    size = own.shape[0]
+    outer = both_outer.at[pl.ds(0, size)]
+    p_outer = both_outer.at[pl.ds(size, high)]
+    part = high // 2 + size - high
+    deeper = deep.at[pl.ds(0, part)]
+    p_deeper = deep.at[pl.ds(part, high // 2)]
+    rows = Fields(
+        lev,
+        x0=((own, OWN), (inner, INNER), (outer, OUTER), (deeper, DEEP)),
+        p=((p_outer, OUTER), (p_deeper, DEEP)),
+        x1=((x1, (-5, -4)), (x1_outer, span(-3, 1)), (x1_own, span(1, 7))),
+        x2=((x2, (-4, -3)), (x2_outer, span(-2, 2))),
+        t1=((t1, (-5, -4)), (t1_outer, span(-3, 1))),
+        t2=((t2, (-4, -3)), (t2_outer, span(-2, 2))),
+        b2=((b2, (-3, -2)), (b2_outer, span(-1, 3))),
+        b1=((b1, (-2, -1)), (b1_own, OWN), (b1_far, (4, 5))),
+        b0=((b0, span(-1, 5)),),
+    )
+    factors = Factors((own, OWN, 0), (inner, INNER, 0), (outer, OUTER, 0), (deeper, DEEP, 2))
     forward(
         sign,
-        state,
-        Rows(lev, (p_own, OWN), (p_outer, OUTER)),
+        rows,
         factors,
-        xs,
-        moved,
         once[...],
         twice[...],
-        (span(-3, 1), span(-2, 2), span(-3, 1), span(-2, 2), span(-1, 3)),
-    )
-    out = Rows(lev, (outer_rows, (0, 1)), (inner_rows, (3, 2)))
-    for i in OWN:
-        adjoint_solved(i, sign, moved[2], xs[1], factors, once[...], out)
-
-
-def backward_kernel(
-    side, own, inner, both_outer, x1, x1_in, outer_rows, inner_rows, b_outer, b_inner, once,
-    packed, field,
-    b0, sems,
-):
-    sign = side[0]
-    outer = both_outer.at[pl.ds(0, own.shape[0])]
-    state = state_rows(own, outer, inner)
-    factors = Factors(own, outer, inner)
-    lev = state.lev
-    second = Rows(lev, (x1, span(-3, 1)), (x1_in, span(1, 7)))
-    back = Rows(
-        lev, (outer_rows, (0, 1)), (inner_rows, (3, 2)), (b_outer, (-1, -2)), (b_inner, (4, 5))
-    )
-    last = Rows(lev, (b0, span(-1, 5)))
+        ((-5, -4), (-4, -3), (-5, -4), (-4, -3), (-3, -2), (-2, -1)),
+    )
     for i in span(-1, 5):
-        adjoint_solved(i, sign, back, second, factors, once[...], last)
+        adjoint_solved(i, sign, rows.b1, rows.x1, factors, once[...], rows.b0)
     copies = []
     for i in OWN:
         row = jnp.where(sign < 0.0, 3 - i, i)
-        for f, value in enumerate(adjoint_row(i, sign, last, state, factors)):
+        for f, value in enumerate(adjoint_row(i, sign, rows.b0, rows.x0, factors)):
             k = 4 * f + i
             packed[k * lev : (k + 1) * lev, :] = value
             copies.append(
@@ -405,6 +476,8 @@
     dma = pltpu.SemaphoreType.DMA
     side = (1 - 2 * (lax.axis_index("tile") & 1)).astype(jnp.float32)[None]
     across = [(i, i + 1) for i in range(1, tiles - 1, 2)]
+    beyond = [(i, i + 2) for i in range(0, tiles - 2, 2)]
+    beyond += [(i + 2, i) for i in range(1, tiles - 2, 2)]
     within = [(i, i + 1) for i in range(0, tiles, 2)]
 
     def swap(value, pairs):
@@ -416,22 +489,23 @@
     def rows_of(n):
         return f32(fields * n * lev, width)
 
-    both = run(
+    both, deep = run(
         pack_kernel,
-        f32(2 * high + 2 * rows, width),
+        (f32(2 * high + 2 * rows, width), f32(high + 2 * rows, width)),
         [SMEM] + [ANY] * 4,
-        ANY,
+        (ANY, ANY),
         [
             dma((2, fields * rows)),
             pltpu.VMEM((2, rows, width), jnp.int32),
             dma((2,)),
             pltpu.VMEM((2 * high + 2 * rows, width), jnp.float32),
-            dma((2 * fields * rows + 1,)),
+            dma((2 * fields * rows + 6,)),
         ],
         2**20,
         60 * 2**20,
     )(side, initial_state, perturbation[0], land_sea, relax_level)
     both_outer = swap(both, across)
+    deep = lax.ppermute(deep, "tile", beyond)
     state, start = run(
         split_kernel,
         (f32(high + 2 * rows, width), f32(high, width)),
@@ -453,32 +527,55 @@
         nbytes=2**18,
     )(vertical_mix)
 
-    x1_in, x2_in, t1, t2, b2 = run(
-        inner_forward_kernel,
+    x1_own, x2_own, t1_own, t2_own, b2_own = run(
+        own_kernel,
         (rows_of(6), rows_of(4), rows_of(6), rows_of(4), rows_of(2)),
         [SMEM] + [VMEM] * 6,
         (VMEM,) * 5,
         [],
-        nbytes=2**18,
+        nbytes=0,
     )(side, state, state_inner, start, start_inner, once, twice)
-    outer_rows, inner_rows, x1 = run(
-        forward_kernel,
-        (rows_of(2), rows_of(2), rows_of(4)),
+
+    far, p_far = run(
+        relay_kernel,
+        (f32(high // 2 + 2 * rows, width), f32(high // 2, width)),
+        [ANY, ANY],
+        (VMEM, VMEM),
+        [dma((5,))],
+        nbytes=0,
+    )(both_outer, b2_own)
+    far, p_far = swap(far, within), swap(p_far, within)
+
+    x1_outer, x2_outer, t1_outer, t2_outer, b2_outer, b1_own = run(
+        outer_kernel,
+        (rows_of(4),) * 6,
         [SMEM] + [VMEM] * 10,
-        (VMEM,) * 3,
-        [buffer(4)] * 4,
-        nbytes=2**20,
-    )(side, state, start, both_outer, x1_in, x2_in, t1, t2, b2, once, twice)
-
-    b_outer, b_inner = swap(outer_rows, across), swap(inner_rows, within)
+        (VMEM,) * 6,
+        [],
+        nbytes=0,
+    )(side, state, start, both_outer, x1_own, x2_own, t1_own, t2_own, b2_own, once, twice)
+    b1_far = run(
+        far_kernel,
+        rows_of(2),
+        [SMEM] + [VMEM] * 11,
+        VMEM,
+        [buffer(2)] * 5,
+        nbytes=0,
+    )(
+        side, state_inner, start_inner, far, p_far, x1_own, x2_own, t1_own, t2_own, b2_own,
+        once, twice,
+    )
     packed, field = run(
-        backward_kernel,
+        last_kernel,
         (f32(high, width), f32(lev, fields, rows, width)),
-        [SMEM] + [VMEM] * 10,
+        [SMEM] + [VMEM] * 14,
         (VMEM, ANY),
-        [buffer(6), dma((fields * rows,))],
-        nbytes=2**20,
-    )(side, state, state_inner, both_outer, x1, x1_in, outer_rows, inner_rows, b_outer, b_inner, once)
+        [buffer(2)] * 6 + [buffer(6), dma((fields * rows,))],
+        nbytes=0,
+    )(
+        side, state, state_inner, both_outer, deep, x1_own, x1_outer, x2_outer, t1_outer,
+        t2_outer, b2_outer, b1_own, b1_far, once, twice,
+    )
 
     share = lax.all_to_all(
         packed.reshape(members, high // members, width), "group", 0, 0, tiled=True

time: 97.9 us -> 104 us (1.062)
  Pallas kernels: 12.1 us -> 16.7 us
  blocking collectives: 60.8 us -> 64.2 us
  waiting for transfers between devices: 4.04 us -> 2.2 us
    pallas_call x4 -> x6, Pallas kernels: 10.6 us -> 15.2 us  [the longest x1 3.96 us: per_device(): run(last_kernel, (f32(high, width), f32(lev, fields, rows, width)), [SMEM...]
    ppermute x5, waiting for transfers between devices: 4.04 us -> 2.2 us  [swap(): return lax.ppermute(value, 'tile', pairs + [(j, i) for i, j in pairs])]
    all_to_all x1, blocking collectives: 20.9 us -> 22.4 us  [per_device(): row = jnp.sum(lax.all_to_all(spread, 'tile', 0, 0, tiled=True), axis=0)]
    ppermute x0 -> x1, starting transfers between devices: none -> 1.29 us  [per_device(): deep = lax.ppermute(deep, 'tile', beyond)]
    ppermute x5, starting transfers between devices: 17 us -> 15.8 us  [swap(): return lax.ppermute(value, 'tile', pairs + [(j, i) for i, j in pairs])]
    all_to_all x1, blocking collectives: 29.7 us -> 30.8 us  [per_device(): lax.all_to_all(packed.reshape(members, high // members, width), 'group',...]
  transfers between devices with their start and end apart: 5 -> 6, of which waited for: 3 -> 1; matrix products, arithmetic and copies ran while one was open for 0% -> 0% of each run, Pallas kernels for 5% -> 10%
where the time goes in v4:
time: 104 us
  blocking collectives  64.2 us (62%)
  starting transfers between devices  17.1 us (16%)
  Pallas kernels  16.7 us (16%)
  waiting for transfers between devices  2.2 us (2%)
  local copies, waits for them, and re-layouts  1.3 us (1%)
    all_to_all x1, blocking collectives, per_device(): lax.all_to_all(packed.reshape(members, high // members, width), 'group',...  30.8 us
    all_to_all x1, blocking collectives, per_device(): row = jnp.sum(lax.all_to_all(spread, 'tile', 0, 0, tiled=True), axis=0)  22.4 us
    ppermute x5, starting transfers between devices, swap(): return lax.ppermute(value, 'tile', pairs + [(j, i) for i, j in pairs])  15.8 us
    all_to_all x1, blocking collectives, per_device(): row = jnp.sum(lax.all_to_all(products, 'group', 0, 0, tiled=True), axis=0)  11 us
    pallas_call x1, Pallas kernels, per_device(): run(last_kernel, (f32(high, width), f32(lev, fields, rows, width)), [SMEM...  3.96 us
    pallas_call x1, Pallas kernels, per_device(): run(outer_kernel, (rows_of(4),) * 6, [SMEM] + [VMEM] * 10, (VMEM,) * 6, [...  3.21 us
    pallas_call x1, Pallas kernels, per_device(): run(own_kernel, (rows_of(6), rows_of(4), rows_of(6), rows_of(4), rows_of(...  2.89 us
    pallas_call x1, Pallas kernels, per_device(): run(pack_kernel, (f32(2 * high + 2 * rows, width), f32(high + 2 * rows, w...  2.74 us
  transfers between devices with their start and end apart: 6, of which 1 were waited for; matrix products, arithmetic and copies ran while one was open for 0% of the time, Pallas kernels for 10%

profile of v4, /device:TPU:1, one launch (start us, length us, event | category | flops | bytes accessed | tf_op | source)
XLA Modules:
  0.0 103.8 jit_solution(9327641831018889223)
XLA Ops:
  0.6 0.0 copy-start.1
  0.6 2.7 %shard_map.68 = (f32[776,384]{1,0:T(8,128)}, f32[392,384]{1,0:T(8,128)}) custom-call(f32[1]{0:T(128)} %bitcast.side, f32[48,2,4,384]{3,2,1,0:T(4,128)} %x.1, f32[48,2,4,384]{3,2,1,0:T(4,128)} %bitcast.11, s32[4,384]{1,0:T(4,128)} %land.1, s32[4,384]{1,0:T(4,128)} %relax.1), custom_call_target="tpu_custom_call" | custom-call | bytes 1048576 | tf_op jit(solution)/shard_map/pallas_call | solution.py:492
  3.4 4.6 %collective-permute-start.1 = (f32[776,384]{1,0:T(8,128)}, f32[776,384]{1,0:T(8,128)S(1)}, u32[]{:S(2)}, u32[]{:S(2)}) collective-permute-start(f32[776,384]{1,0:T(8,128)} %get-tuple-element.23.both), channel_id=1, source_target_pairs={{1,2},{3,4},{5,6},{7,8},{9,10},{11,12},{13,14},{15,16},{17,18},{19... | collective-permute-start | bytes 3575816 | tf_op jit(solution)/shard_map/ppermute | solution.py:484
  8.0 0.0 copy-start
  8.0 1.3 %copy-done = f32[776,384]{1,0:T(8,128)S(1)} copy-done((f32[776,384]{1,0:T(8,128)S(1)}, f32[776,384]{1,0:T(8,128)}, u32[]{:S(2)}) %copy-start) | copy-done | bytes 1191960
  9.3 0.0 copy-start.2
  9.3 0.3 shard_map.69
  9.6 4.9 %collective-permute-start = (f32[392,384]{1,0:T(8,128)S(1)}, f32[392,384]{1,0:T(8,128)S(1)}, u32[]{:S(2)}, u32[]{:S(2)}) collective-permute-start(f32[392,384]{1,0:T(8,128)S(1)} %get-tuple-element.24.own), channel_id=1, source_target_pairs={{0,1},{2,3},{4,5},{6,7},{8,9},{10,11},{12,13},{14,15},{16,17},{18,... | collective-permute-start | bytes 1806344 | tf_op jit(solution)/shard_map/ppermute | solution.py:484
  14.5 1.9 %collective-permute-start.3 = (f32[384,384]{1,0:T(8,128)S(1)}, f32[384,384]{1,0:T(8,128)S(1)}, u32[]{:S(2)}, u32[]{:S(2)}) collective-permute-start(f32[384,384]{1,0:T(8,128)S(1)} %get-tuple-element.26.p_own), channel_id=1, source_target_pairs={{0,1},{2,3},{4,5},{6,7},{8,9},{10,11},{12,13},{14,15},{16,17},{18,... | collective-permute-start | bytes 1769480 | tf_op jit(solution)/shard_map/ppermute | solution.py:484
  16.4 0.0 copy-done.2
  16.4 1.3 %collective-permute-start.2 = (f32[392,384]{1,0:T(8,128)S(1)}, f32[392,384]{1,0:T(8,128)S(1)}, u32[]{:S(2)}, u32[]{:S(2)}) collective-permute-start(f32[392,384]{1,0:T(8,128)S(1)} %copy-done.2), channel_id=1, source_target_pairs={{0,2},{2,4},{4,6},{6,8},{8,10},{10,12},{12,14},{14,16},{16,18},{18... | collective-permute-start | bytes 1806344 | tf_op jit(solution)/shard_map/ppermute | solution.py:508
  17.8 0.0 copy-done.1
  17.8 1.2 %shard_map.70 = (bf16[48,144]{1,0:T(8,128)(2,1)S(1)}, bf16[48,144]{1,0:T(8,128)(2,1)S(1)}) custom-call(f32[48]{0:T(128)S(1)} %copy-done.1), custom_call_target="tpu_custom_call" | custom-call | bytes 262144 | tf_op jit(solution)/shard_map/pallas_call | solution.py:521
  19.0 0.0 collective-permute-done.3.p_inner
  19.0 0.0 collective-permute-done.inner
  19.0 2.9 %shard_map.71 = (f32[576,384]{1,0:T(8,128)S(1)}, f32[384,384]{1,0:T(8,128)S(1)}, f32[576,384]{1,0:T(8,128)S(1)}, f32[384,384]{1,0:T(8,128)S(1)}, f32[192,384]{1,0:T(8,128)S(1)}) custom-call(f32[1]{0:T(128)} %bitcast.side, f32[392,384]{1,0:T(8,128)S(1)} %get-tuple-element.24.own, f32[392,384]{1,0:T(8,128)S(1)} %collective-permute-done.inner, ...), custom_call_target="tpu_custom_call" | custom-call | tf_op jit(solution)/shard_map/pallas_call | solution.py:530
  21.9 2.2 %collective-permute-done.1.both_outer.both = f32[776,384]{1,0:T(8,128)S(1)} collective-permute-done((f32[776,384]{1,0:T(8,128)}, f32[776,384]{1,0:T(8,128)S(1)}, u32[]{:S(2)}, u32[]{:S(2)}) %collective-permute-start.1) | collective-permute-done | bytes 1191968 | tf_op jit(solution)/shard_map/ppermute | solution.py:484
  24.1 0.8 shard_map.73
  24.9 1.9 %collective-permute-start.4 = (f32[200,384]{1,0:T(8,128)S(1)}, f32[200,384]{1,0:T(8,128)S(1)}, u32[]{:S(2)}, u32[]{:S(2)}) collective-permute-start(f32[200,384]{1,0:T(8,128)S(1)} %get-tuple-element.40), channel_id=1, source_target_pairs={{0,1},{2,3},{4,5},{6,7},{8,9},{10,11},{12,13},{14,15},{16,17},{18,... | collective-permute-start | bytes 921608 | tf_op jit(solution)/shard_map/ppermute | solution.py:484
  26.8 2.4 %collective-permute-start.5 = (f32[192,384]{1,0:T(8,128)S(1)}, f32[192,384]{1,0:T(8,128)S(1)}, u32[]{:S(2)}, u32[]{:S(2)}) collective-permute-start(f32[192,384]{1,0:T(8,128)S(1)} %get-tuple-element.41), channel_id=1, source_target_pairs={{0,1},{2,3},{4,5},{6,7},{8,9},{10,11},{12,13},{14,15},{16,17},{18,... | collective-permute-start | bytes 884744 | tf_op jit(solution)/shard_map/ppermute | solution.py:484
  29.2 3.2 %shard_map.72 = (f32[384,384]{1,0:T(8,128)S(1)}, f32[384,384]{1,0:T(8,128)S(1)}, f32[384,384]{1,0:T(8,128)S(1)}, f32[384,384]{1,0:T(8,128)S(1)}, f32[384,384]{1,0:T(8,128)S(1)}, /*index=5*/f32[384,384]{1,0:T(8,128)S(1)}) custom-call(f32[1]{0:T(128)} %bitcast.side, f32[392,384]{1,0:T(8,128)S(1)} %get-tuple-element.24.own, ...), custom_call_target="tpu_custom_call" | custom-call | tf_op jit(solution)/shard_map/pallas_call | solution.py:549
  32.5 0.0 collective-permute-done.5.p_far
  32.5 0.0 collective-permute-done.4.far
  32.5 1.6 %shard_map.74.b1_far = f32[192,384]{1,0:T(8,128)S(1)} custom-call(f32[1]{0:T(128)} %bitcast.side, f32[392,384]{1,0:T(8,128)S(1)} %collective-permute-done.inner, f32[384,384]{1,0:T(8,128)S(1)} %collective-permute-done.3.p_inner, f32[200,384]{1,0:T(8,128)S(1)} %collective-permute-done.4.far, f32[192,384]{1,0:T(8,128)S(1)} %collective-permute-done.5.p_far, ...), custom_call_target="tpu_custom_call" | custom-call | tf_op jit(solution)/shard_map/pallas_call | solution.py:557
  34.1 0.0 collective-permute-done.2.deep
  34.1 4.0 %shard_map.75 = (f32[384,384]{1,0:T(8,128)S(1)}, f32[48,2,4,384]{3,2,1,0:T(4,128)}) custom-call(f32[1]{0:T(128)} %bitcast.side, f32[392,384]{1,0:T(8,128)S(1)} %get-tuple-element.24.own, f32[392,384]{1,0:T(8,128)S(1)} %collective-permute-done.inner, f32[776,384]{1,0:T(8,128)S(1)} %collective-permute-done.1.both_outer.both, ...), custom_call_target="tpu_custom_call" | custom-call | tf_op jit(solution)/shard_map/pallas_call | solution.py:568
  38.1 30.8 %all_to_all.20 = f32[16,24,384]{2,1,0:T(8,128)S(1)} all-to-all(f32[16,24,384]{2,1,0:T(8,128)S(1)} %bitcast.10), channel_id=1, replica_groups=mesh['group'=16,'tile'=32] {'group'}, dimensions={0} | all-to-all | bytes 1179648 | tf_op jit(solution)/shard_map/all_to_all | solution.py:580
  68.8 0.9 fusion
  69.7 11.0 %all_to_all.21 = f32[16,1,16]{2,1,0:T(1,128)S(1)} all-to-all(f32[16,1,16]{2,1,0:T(1,128)S(1)} %bitcast.12), channel_id=1, replica_groups=mesh['group'=16,'tile'=32] {'group'}, dimensions={0} | all-to-all | bytes 2048 | tf_op jit(solution)/shard_map/all_to_all | solution.py:590
  80.8 22.4 %all_to_all.22 = f32[32,1,16]{2,1,0:T(1,128)S(1)} all-to-all(f32[32,1,16]{2,1,0:T(1,128)S(1)} %broadcast_in_dim.15), channel_id=1, replica_groups=mesh['group'=16,'tile'=32] {'tile'}, dimensions={0} | all-to-all | bytes 4096 | tf_op jit(solution)/shard_map/all_to_all | solution.py:592
  103.2 0.1 reduce_sum.19
  103.2 0.5 multiply_bitcast_fusion
  (2 shorter events, 0.0 us)
Async XLA Ops:
  0.6 17.1 %copy-start.1 = (f32[48]{0:T(128)S(1)}, f32[48]{0:T(128)}, u32[]{:S(2)}) copy-start(f32[48]{0:T(128)} %mix.1) | copy-start | bytes 580
  3.4 20.7 %collective-permute-start.1 = (f32[776,384]{1,0:T(8,128)}, f32[776,384]{1,0:T(8,128)S(1)}, u32[]{:S(2)}, u32[]{:S(2)}) collective-permute-start(f32[776,384]{1,0:T(8,128)} %get-tuple-element.23.both), channel_id=1, source_target_pairs={{1,2},{3,4},{5,6},{7,8},{9,10},{11,12},{13,14},{15,16},{17,18},{19... | collective-permute-start | bytes 3575816 | tf_op jit(solution)/shard_map/ppermute | solution.py:484
  8.0 1.3 %copy-start = (f32[776,384]{1,0:T(8,128)S(1)}, f32[776,384]{1,0:T(8,128)}, u32[]{:S(2)}) copy-start(f32[776,384]{1,0:T(8,128)} %get-tuple-element.23.both) | copy-start | bytes 3575812
  9.3 7.1 %copy-start.2 = (f32[392,384]{1,0:T(8,128)S(1)}, f32[392,384]{1,0:T(8,128)}, u32[]{:S(2)}) copy-start(f32[392,384]{1,0:T(8,128)} %get-tuple-element.25) | copy-start | bytes 1806340
  9.6 9.4 %collective-permute-start = (f32[392,384]{1,0:T(8,128)S(1)}, f32[392,384]{1,0:T(8,128)S(1)}, u32[]{:S(2)}, u32[]{:S(2)}) collective-permute-start(f32[392,384]{1,0:T(8,128)S(1)} %get-tuple-element.24.own), channel_id=1, source_target_pairs={{0,1},{2,3},{4,5},{6,7},{8,9},{10,11},{12,13},{14,15},{16,17},{18,... | collective-permute-start | bytes 1806344 | tf_op jit(solution)/shard_map/ppermute | solution.py:484
  14.5 4.5 %collective-permute-start.3 = (f32[384,384]{1,0:T(8,128)S(1)}, f32[384,384]{1,0:T(8,128)S(1)}, u32[]{:S(2)}, u32[]{:S(2)}) collective-permute-start(f32[384,384]{1,0:T(8,128)S(1)} %get-tuple-element.26.p_own), channel_id=1, source_target_pairs={{0,1},{2,3},{4,5},{6,7},{8,9},{10,11},{12,13},{14,15},{16,17},{18,... | collective-permute-start | bytes 1769480 | tf_op jit(solution)/shard_map/ppermute | solution.py:484
  16.4 17.6 %collective-permute-start.2 = (f32[392,384]{1,0:T(8,128)S(1)}, f32[392,384]{1,0:T(8,128)S(1)}, u32[]{:S(2)}, u32[]{:S(2)}) collective-permute-start(f32[392,384]{1,0:T(8,128)S(1)} %copy-done.2), channel_id=1, source_target_pairs={{0,2},{2,4},{4,6},{6,8},{8,10},{10,12},{12,14},{14,16},{16,18},{18... | collective-permute-start | bytes 1806344 | tf_op jit(solution)/shard_map/ppermute | solution.py:508
  24.9 7.6 %collective-permute-start.4 = (f32[200,384]{1,0:T(8,128)S(1)}, f32[200,384]{1,0:T(8,128)S(1)}, u32[]{:S(2)}, u32[]{:S(2)}) collective-permute-start(f32[200,384]{1,0:T(8,128)S(1)} %get-tuple-element.40), channel_id=1, source_target_pairs={{0,1},{2,3},{4,5},{6,7},{8,9},{10,11},{12,13},{14,15},{16,17},{18,... | collective-permute-start | bytes 921608 | tf_op jit(solution)/shard_map/ppermute | solution.py:484
  26.8 5.6 %collective-permute-start.5 = (f32[192,384]{1,0:T(8,128)S(1)}, f32[192,384]{1,0:T(8,128)S(1)}, u32[]{:S(2)}, u32[]{:S(2)}) collective-permute-start(f32[192,384]{1,0:T(8,128)S(1)} %get-tuple-element.41), channel_id=1, source_target_pairs={{0,1},{2,3},{4,5},{6,7},{8,9},{10,11},{12,13},{14,15},{16,17},{18,... | collective-permute-start | bytes 884744 | tf_op jit(solution)/shard_map/ppermute | solution.py:484

commit v5 on v3

--- a/solution.py
+++ b/solution.py
@@ -157,7 +157,10 @@
         for buf, rows in pieces:
             for k, i in enumerate(rows):
                 for f in range(2):
-                    self.where[f, i] = (buf, (f * len(rows) + k) * lev)
+                    if isinstance(buf, tuple):
+                        self.where[f, i] = (buf[f], k * lev)
+                    else:
+                        self.where[f, i] = (buf, (f * len(rows) + k) * lev)
 
     def read(self, f, i):
         buf, at = self.where[f, i]
@@ -330,8 +333,8 @@
 
 def forward_kernel(
     side, own, p_own, both_outer, x1_in, x2_in, t1_in, t2_in, b2_in, once, twice,
-    outer_rows, inner_rows, x1,
-    x2, t1, t2, b2,
+    outer_rows, x1, x2, b2,
+    t1, t2,
 ):
     sign = side[0]
     size = own.shape[0]
@@ -360,40 +363,81 @@
         twice[...],
         (span(-3, 1), span(-2, 2), span(-3, 1), span(-2, 2), span(-1, 3)),
     )
-    out = Rows(lev, (outer_rows, (0, 1)), (inner_rows, (3, 2)))
-    for i in OWN:
+    out = Rows(lev, (outer_rows, (0, 1)))
+    for i in (0, 1):
         adjoint_solved(i, sign, moved[2], xs[1], factors, once[...], out)
 
 
+def inner_rows_kernel(side, own, x2, x2_in, b2, b2_in, once, inner_u, inner_t):
+    factors = Factors(own, None, None)
+    lev = factors.lev
+    third = Rows(lev, (x2, span(-2, 2)), (x2_in, span(2, 6)))
+    back = Rows(lev, (b2, span(-1, 3)), (b2_in, span(3, 5)))
+    out = Rows(lev, ((inner_u, inner_t), (3, 2)))
+    for i in (2, 3):
+        adjoint_solved(i, side[0], back, third, factors, once[...], out)
+
+
+def inner_backward_kernel(
+    side, own, inner, x1, x1_in, outer_rows, inner_u, inner_t, b_u, b_t, once,
+    b0, done,
+):
+    sign = side[0]
+    state = state_rows(own, None, inner)
+    factors = Factors(own, None, inner)
+    lev = state.lev
+    second = Rows(lev, (x1, span(-3, 1)), (x1_in, span(1, 7)))
+    back = Rows(
+        lev, (outer_rows, (0, 1)), ((inner_u, inner_t), (3, 2)), ((b_u, b_t), (4, 5))
+    )
+    last = Rows(lev, (b0, span(1, 5)))
+    for i in span(1, 5):
+        adjoint_solved(i, sign, back, second, factors, once[...], last)
+    out = Rows(lev, (done, (2, 3)))
+    for i in (2, 3):
+        for f, value in enumerate(adjoint_row(i, sign, last, state, factors)):
+            out.write(f, i, value)
+
+
 def backward_kernel(
-    side, own, inner, both_outer, x1, x1_in, outer_rows, inner_rows, b_outer, b_inner, once,
+    side, own, both_outer, x1, x1_in, outer_rows, inner_u, inner_t, b_outer, b0_in, done, once,
     packed, field,
     b0, sems,
 ):
     sign = side[0]
     outer = both_outer.at[pl.ds(0, own.shape[0])]
-    state = state_rows(own, outer, inner)
-    factors = Factors(own, outer, inner)
+    state = state_rows(own, outer, None)
+    factors = Factors(own, outer, None)
     lev = state.lev
     second = Rows(lev, (x1, span(-3, 1)), (x1_in, span(1, 7)))
     back = Rows(
-        lev, (outer_rows, (0, 1)), (inner_rows, (3, 2)), (b_outer, (-1, -2)), (b_inner, (4, 5))
-    )
-    last = Rows(lev, (b0, span(-1, 5)))
-    for i in span(-1, 5):
+        lev, (outer_rows, (0, 1)), ((inner_u, inner_t), (3, 2)), (b_outer, (-1, -2))
+    )
+    last = Rows(lev, (b0, (-1, 0)), (b0_in, span(1, 5)))
+    ready = Rows(lev, (done, (2, 3)))
+    results = Rows(lev, (packed, OWN))
+    copies = []
+
+    def send(f, i):
+        k = 4 * f + i
+        row = jnp.where(sign < 0.0, 3 - i, i)
+        copies.append(
+            pltpu.make_async_copy(
+                packed.at[pl.ds(k * lev, lev), :], field.at[:, f, row, :], sems.at[k]
+            )
+        )
+        copies[-1].start()
+
+    for i in (2, 3):
+        for f in range(2):
+            results.write(f, i, ready.read(f, i))
+            send(f, i)
+    for i in (-1, 0):
         adjoint_solved(i, sign, back, second, factors, once[...], last)
-    copies = []
-    for i in OWN:
-        row = jnp.where(sign < 0.0, 3 - i, i)
+    for i in (0, 1):
         for f, value in enumerate(adjoint_row(i, sign, last, state, factors)):
-            k = 4 * f + i
-            packed[k * lev : (k + 1) * lev, :] = value
-            copies.append(
-                pltpu.make_async_copy(
-                    packed.at[pl.ds(k * lev, lev), :], field.at[:, f, row, :], sems.at[k]
-                )
-            )
-            copies[-1].start()
+            results.write(f, i, value)
+            send(f, i)
     wait_all(copies)
 
 
@@ -461,24 +505,44 @@
         [],
         nbytes=2**18,
     )(side, state, state_inner, start, start_inner, once, twice)
-    outer_rows, inner_rows, x1 = run(
+    outer_rows, x1, x2, b2_outer = run(
         forward_kernel,
-        (rows_of(2), rows_of(2), rows_of(4)),
+        (rows_of(2), rows_of(4), rows_of(4), rows_of(4)),
         [SMEM] + [VMEM] * 10,
-        (VMEM,) * 3,
-        [buffer(4)] * 4,
+        (VMEM,) * 4,
+        [buffer(4), buffer(4)],
         nbytes=2**20,
     )(side, state, start, both_outer, x1_in, x2_in, t1, t2, b2, once, twice)
 
-    b_outer, b_inner = swap(outer_rows, across), swap(inner_rows, within)
+    b_outer = swap(outer_rows, across)
+    half = f32(2 * lev, width)
+    inner_u, inner_t = run(
+        inner_rows_kernel,
+        (half, half),
+        [SMEM] + [VMEM] * 6,
+        (VMEM, VMEM),
+        [],
+        nbytes=0,
+    )(side, state, x2, x2_in, b2_outer, b2, once)
+    b_u, b_t = swap(inner_u, within), swap(inner_t, within)
+    b0, done = run(
+        inner_backward_kernel,
+        (rows_of(4), rows_of(2)),
+        [SMEM] + [VMEM] * 10,
+        (VMEM, VMEM),
+        [],
+        nbytes=0,
+    )(side, state, state_inner, x1, x1_in, outer_rows, inner_u, inner_t, b_u, b_t, once)
     packed, field = run(
         backward_kernel,
         (f32(high, width), f32(lev, fields, rows, width)),
-        [SMEM] + [VMEM] * 10,
+        [SMEM] + [VMEM] * 11,
         (VMEM, ANY),
-        [buffer(6), dma((fields * rows,))],
+        [buffer(2), dma((fields * rows,))],
         nbytes=2**20,
-    )(side, state, state_inner, both_outer, x1, x1_in, outer_rows, inner_rows, b_outer, b_inner, once)
+    )(
+        side, state, both_outer, x1, x1_in, outer_rows, inner_u, inner_t, b_outer, b0, done, once
+    )
 
     share = lax.all_to_all(
         packed.reshape(members, high // members, width), "group", 0, 0, tiled=True

time: 97.9 us -> 99.7 us (1.018)
  starting transfers between devices: 17 us -> 19.4 us
  waiting for transfers between devices: 4.04 us -> 2.57 us
    ppermute x5 -> x6, starting transfers between devices: 17 us -> 19.4 us  [swap(): return lax.ppermute(value, 'tile', pairs + [(j, i) for i, j in pairs])]
    all_to_all x1, blocking collectives: 29.7 us -> 28.2 us  [per_device(): lax.all_to_all(packed.reshape(members, high // members, width), 'group',...]
    ppermute x5 -> x6, waiting for transfers between devices: 4.04 us -> 2.57 us  [swap(): return lax.ppermute(value, 'tile', pairs + [(j, i) for i, j in pairs])]
    all_to_all x1, blocking collectives: 10.2 us -> 11.5 us  [per_device(): row = jnp.sum(lax.all_to_all(products, 'group', 0, 0, tiled=True), axis=0)]
    pallas_call x1 -> x3, Pallas kernels: 3.18 us -> 4.19 us  [the longest x1 2.93 us: per_device(): run(forward_kernel, (rows_of(2), rows_of(4), rows_of(4), rows_of(4)), [SM...]
  transfers between devices with their start and end apart: 5 -> 6, of which waited for: 3 -> 3; matrix products, arithmetic and copies ran while one was open for 0% -> 0% of each run, Pallas kernels for 5% -> 6%
where the time goes in v5:
time: 99.7 us; the launch traced here: 99.3 us
  blocking collectives  61.2 us (61%)
  starting transfers between devices  19.4 us (19%)
  Pallas kernels  12.6 us (13%)
  waiting for transfers between devices  2.57 us (3%)
  local copies, waits for them, and re-layouts  1.3 us (1%)
    all_to_all x1, blocking collectives, per_device(): lax.all_to_all(packed.reshape(members, high // members, width), 'group',...  28.2 us
    all_to_all x1, blocking collectives, per_device(): row = jnp.sum(lax.all_to_all(spread, 'tile', 0, 0, tiled=True), axis=0)  21.5 us
    ppermute x6, starting transfers between devices, swap(): return lax.ppermute(value, 'tile', pairs + [(j, i) for i, j in pairs])  19.4 us
    all_to_all x1, blocking collectives, per_device(): row = jnp.sum(lax.all_to_all(products, 'group', 0, 0, tiled=True), axis=0)  11.5 us
    pallas_call x1, Pallas kernels, per_device(): run(inner_forward_kernel, (rows_of(6), rows_of(4), rows_of(6), rows_of(4)...  2.97 us
    pallas_call x1, Pallas kernels, per_device(): run(forward_kernel, (rows_of(2), rows_of(4), rows_of(4), rows_of(4)), [SM...  2.93 us
    ppermute x6, waiting for transfers between devices, swap(): return lax.ppermute(value, 'tile', pairs + [(j, i) for i, j in pairs])  2.57 us
    pallas_call x1, Pallas kernels, per_device(): run(pack_kernel, f32(2 * high + 2 * rows, width), [SMEM] + [ANY] * 4, ANY...  2.47 us
  transfers between devices with their start and end apart: 6, of which 3 were waited for; matrix products, arithmetic and copies ran while one was open for 0% of the time, Pallas kernels for 6%

profile of v5, /device:TPU:1, one launch (start us, length us, event | category | flops | bytes accessed | tf_op | source)
XLA Modules:
  0.0 99.3 jit_solution(17749948829477376335)
XLA Ops:
  0.6 2.5 %shard_map.68.both = f32[776,384]{1,0:T(8,128)} custom-call(f32[1]{0:T(128)} %bitcast.side, f32[48,2,4,384]{3,2,1,0:T(4,128)} %x.1, f32[48,2,4,384]{3,2,1,0:T(4,128)} %bitcast.11, s32[4,384]{1,0:T(4,128)} %land.1, s32[4,384]{1,0:T(4,128)} %relax.1), custom_call_target="tpu_custom_call" | custom-call | bytes 1048576 | tf_op jit(solution)/shard_map/pallas_call | solution.py:463
  3.1 4.6 %collective-permute-start = (f32[776,384]{1,0:T(8,128)}, f32[776,384]{1,0:T(8,128)S(1)}, u32[]{:S(2)}, u32[]{:S(2)}) collective-permute-start(f32[776,384]{1,0:T(8,128)} %shard_map.68.both), channel_id=1, source_target_pairs={{1,2},{3,4},{5,6},{7,8},{9,10},{11,12},{13,14},{15,16},{17,18},{19... | collective-permute-start | bytes 3575816 | tf_op jit(solution)/shard_map/ppermute | solution.py:455
  7.7 0.0 copy-start
  7.7 1.3 %copy-done = f32[776,384]{1,0:T(8,128)S(1)} copy-done((f32[776,384]{1,0:T(8,128)S(1)}, f32[776,384]{1,0:T(8,128)}, u32[]{:S(2)}) %copy-start) | copy-done | bytes 1191960
  9.0 0.0 copy-start.1
  9.0 0.3 shard_map.69
  9.3 4.9 %collective-permute-start.1 = (f32[392,384]{1,0:T(8,128)S(1)}, f32[392,384]{1,0:T(8,128)S(1)}, u32[]{:S(2)}, u32[]{:S(2)}) collective-permute-start(f32[392,384]{1,0:T(8,128)S(1)} %get-tuple-element.21.own), channel_id=1, source_target_pairs={{0,1},{2,3},{4,5},{6,7},{8,9},{10,11},{12,13},{14,15},{16,17},{18,... | collective-permute-start | bytes 1806344 | tf_op jit(solution)/shard_map/ppermute | solution.py:455
  14.2 1.9 %collective-permute-start.2 = (f32[384,384]{1,0:T(8,128)S(1)}, f32[384,384]{1,0:T(8,128)S(1)}, u32[]{:S(2)}, u32[]{:S(2)}) collective-permute-start(f32[384,384]{1,0:T(8,128)S(1)} %get-tuple-element.22.p_own), channel_id=1, source_target_pairs={{0,1},{2,3},{4,5},{6,7},{8,9},{10,11},{12,13},{14,15},{16,17},{18,... | collective-permute-start | bytes 1769480 | tf_op jit(solution)/shard_map/ppermute | solution.py:455
  16.1 0.0 copy-done.1
  16.1 1.2 %shard_map.70 = (bf16[48,144]{1,0:T(8,128)(2,1)S(1)}, bf16[48,144]{1,0:T(8,128)(2,1)S(1)}) custom-call(f32[48]{0:T(128)S(1)} %copy-done.1), custom_call_target="tpu_custom_call" | custom-call | bytes 262144 | tf_op jit(solution)/shard_map/pallas_call | solution.py:491
  17.4 0.7 collective-permute-done.2.p_inner
  18.1 0.0 collective-permute-done.1.inner
  18.1 3.0 %shard_map.71 = (f32[576,384]{1,0:T(8,128)S(1)}, f32[384,384]{1,0:T(8,128)S(1)}, f32[576,384]{1,0:T(8,128)S(1)}, f32[384,384]{1,0:T(8,128)S(1)}, f32[192,384]{1,0:T(8,128)S(1)}) custom-call(f32[1]{0:T(128)} %bitcast.side, f32[392,384]{1,0:T(8,128)S(1)} %get-tuple-element.21.own, f32[392,384]{1,0:T(8,128)S(1)} %collective-permute-done.1.inner, ...), custom_call_target="tpu_custom_call" | custom-call | bytes 262144 | tf_op jit(solution)/shard_map/pallas_call | solution.py:500
  21.1 0.8 collective-permute-done.both_outer
  21.9 2.9 %shard_map.72 = (f32[192,384]{1,0:T(8,128)S(1)}, f32[384,384]{1,0:T(8,128)S(1)}, f32[384,384]{1,0:T(8,128)S(1)}, f32[384,384]{1,0:T(8,128)S(1)}) custom-call(f32[1]{0:T(128)} %bitcast.side, f32[392,384]{1,0:T(8,128)S(1)} %get-tuple-element.21.own, f32[384,384]{1,0:T(8,128)S(1)} %get-tuple-element.22.p_own, f32[776,384]{1,0:T(8,128)S(1)} %collective-permute-done.both_outer, ...), custom_call_target="tpu_custom_call" | custom-call | bytes 1048576 | tf_op jit(solution)/shard_map/pallas_call | solution.py:508
  24.9 3.6 %collective-permute-start.3 = (f32[192,384]{1,0:T(8,128)S(1)}, f32[192,384]{1,0:T(8,128)S(1)}, u32[]{:S(2)}, u32[]{:S(2)}) collective-permute-start(f32[192,384]{1,0:T(8,128)S(1)} %get-tuple-element.31.outer_rows), channel_id=1, source_target_pairs={{1,2},{3,4},{5,6},{7,8},{9,10},{11,12},{13,14},{15,16},{17,18},{19... | collective-permute-start | bytes 884744 | tf_op jit(solution)/shard_map/ppermute | solution.py:455
  28.5 0.4 shard_map.73
  28.9 1.9 %collective-permute-start.4 = (f32[96,384]{1,0:T(8,128)S(1)}, f32[96,384]{1,0:T(8,128)S(1)}, u32[]{:S(2)}, u32[]{:S(2)}) collective-permute-start(f32[96,384]{1,0:T(8,128)S(1)} %get-tuple-element.34.inner_u), channel_id=1, source_target_pairs={{0,1},{2,3},{4,5},{6,7},{8,9},{10,11},{12,13},{14,15},{16,17},{18,... | collective-permute-start | bytes 442376 | tf_op jit(solution)/shard_map/ppermute | solution.py:455
  30.9 2.4 %collective-permute-start.5 = (f32[96,384]{1,0:T(8,128)S(1)}, f32[96,384]{1,0:T(8,128)S(1)}, u32[]{:S(2)}, u32[]{:S(2)}) collective-permute-start(f32[96,384]{1,0:T(8,128)S(1)} %get-tuple-element.35.inner_t), channel_id=1, source_target_pairs={{0,1},{2,3},{4,5},{6,7},{8,9},{10,11},{12,13},{14,15},{16,17},{18,... | collective-permute-start | bytes 442376 | tf_op jit(solution)/shard_map/ppermute | solution.py:455
  33.3 0.0 collective-permute-done.4.b_u
  33.3 1.0 collective-permute-done.5.b_t
  34.3 0.8 shard_map.74
  35.1 0.0 collective-permute-done.3.b_outer
  35.1 1.4 %shard_map.75 = (f32[384,384]{1,0:T(8,128)S(1)}, f32[48,2,4,384]{3,2,1,0:T(4,128)}) custom-call(f32[1]{0:T(128)} %bitcast.side, f32[392,384]{1,0:T(8,128)S(1)} %get-tuple-element.21.own, f32[776,384]{1,0:T(8,128)S(1)} %collective-permute-done.both_outer, f32[384,384]{1,0:T(8,128)S(1)} %get-tuple-element.30.x1, f32[576,384]{1,0:T(8,128)S(1)} %get-tuple-element.25.x1_in, ...), custom_call_target="tpu_custom_call" | custom-call | bytes 1048576 | tf_op jit(solution)/shard_map/pallas_call | solution.py:536
  36.6 28.2 %all_to_all.20 = f32[16,24,384]{2,1,0:T(8,128)S(1)} all-to-all(f32[16,24,384]{2,1,0:T(8,128)S(1)} %bitcast.10), channel_id=1, replica_groups=mesh['group'=16,'tile'=32] {'group'}, dimensions={0} | all-to-all | bytes 1179648 | tf_op jit(solution)/shard_map/all_to_all | solution.py:547
  64.8 0.9 fusion
  65.7 11.5 %all_to_all.21 = f32[16,1,16]{2,1,0:T(1,128)S(1)} all-to-all(f32[16,1,16]{2,1,0:T(1,128)S(1)} %bitcast.12), channel_id=1, replica_groups=mesh['group'=16,'tile'=32] {'group'}, dimensions={0} | all-to-all | bytes 2048 | tf_op jit(solution)/shard_map/all_to_all | solution.py:557
  77.2 21.5 %all_to_all.22 = f32[32,1,16]{2,1,0:T(1,128)S(1)} all-to-all(f32[32,1,16]{2,1,0:T(1,128)S(1)} %broadcast_in_dim.15), channel_id=1, replica_groups=mesh['group'=16,'tile'=32] {'tile'}, dimensions={0} | all-to-all | bytes 4096 | tf_op jit(solution)/shard_map/all_to_all | solution.py:559
  98.7 0.1 reduce_sum.19
  98.8 0.5 multiply_bitcast_fusion
  (2 shorter events, 0.0 us)
Async XLA Ops:
  3.1 18.8 %collective-permute-start = (f32[776,384]{1,0:T(8,128)}, f32[776,384]{1,0:T(8,128)S(1)}, u32[]{:S(2)}, u32[]{:S(2)}) collective-permute-start(f32[776,384]{1,0:T(8,128)} %shard_map.68.both), channel_id=1, source_target_pairs={{1,2},{3,4},{5,6},{7,8},{9,10},{11,12},{13,14},{15,16},{17,18},{19... | collective-permute-start | bytes 3575816 | tf_op jit(solution)/shard_map/ppermute | solution.py:455
  7.7 1.3 %copy-start = (f32[776,384]{1,0:T(8,128)S(1)}, f32[776,384]{1,0:T(8,128)}, u32[]{:S(2)}) copy-start(f32[776,384]{1,0:T(8,128)} %shard_map.68.both) | copy-start | bytes 3575812
  9.0 7.1 %copy-start.1 = (f32[48]{0:T(128)S(1)}, f32[48]{0:T(128)}, u32[]{:S(2)}) copy-start(f32[48]{0:T(128)} %mix.1) | copy-start | bytes 580
  9.3 8.8 %collective-permute-start.1 = (f32[392,384]{1,0:T(8,128)S(1)}, f32[392,384]{1,0:T(8,128)S(1)}, u32[]{:S(2)}, u32[]{:S(2)}) collective-permute-start(f32[392,384]{1,0:T(8,128)S(1)} %get-tuple-element.21.own), channel_id=1, source_target_pairs={{0,1},{2,3},{4,5},{6,7},{8,9},{10,11},{12,13},{14,15},{16,17},{18,... | collective-permute-start | bytes 1806344 | tf_op jit(solution)/shard_map/ppermute | solution.py:455
  14.2 3.9 %collective-permute-start.2 = (f32[384,384]{1,0:T(8,128)S(1)}, f32[384,384]{1,0:T(8,128)S(1)}, u32[]{:S(2)}, u32[]{:S(2)}) collective-permute-start(f32[384,384]{1,0:T(8,128)S(1)} %get-tuple-element.22.p_own), channel_id=1, source_target_pairs={{0,1},{2,3},{4,5},{6,7},{8,9},{10,11},{12,13},{14,15},{16,17},{18,... | collective-permute-start | bytes 1769480 | tf_op jit(solution)/shard_map/ppermute | solution.py:455
  24.9 10.3 %collective-permute-start.3 = (f32[192,384]{1,0:T(8,128)S(1)}, f32[192,384]{1,0:T(8,128)S(1)}, u32[]{:S(2)}, u32[]{:S(2)}) collective-permute-start(f32[192,384]{1,0:T(8,128)S(1)} %get-tuple-element.31.outer_rows), channel_id=1, source_target_pairs={{1,2},{3,4},{5,6},{7,8},{9,10},{11,12},{13,14},{15,16},{17,18},{19... | collective-permute-start | bytes 884744 | tf_op jit(solution)/shard_map/ppermute | solution.py:455
  28.9 4.3 %collective-permute-start.4 = (f32[96,384]{1,0:T(8,128)S(1)}, f32[96,384]{1,0:T(8,128)S(1)}, u32[]{:S(2)}, u32[]{:S(2)}) collective-permute-start(f32[96,384]{1,0:T(8,128)S(1)} %get-tuple-element.34.inner_u), channel_id=1, source_target_pairs={{0,1},{2,3},{4,5},{6,7},{8,9},{10,11},{12,13},{14,15},{16,17},{18,... | collective-permute-start | bytes 442376 | tf_op jit(solution)/shard_map/ppermute | solution.py:455
  30.9 3.4 %collective-permute-start.5 = (f32[96,384]{1,0:T(8,128)S(1)}, f32[96,384]{1,0:T(8,128)S(1)}, u32[]{:S(2)}, u32[]{:S(2)}) collective-permute-start(f32[96,384]{1,0:T(8,128)S(1)} %get-tuple-element.35.inner_t), channel_id=1, source_target_pairs={{0,1},{2,3},{4,5},{6,7},{8,9},{10,11},{12,13},{14,15},{16,17},{18,... | collective-permute-start | bytes 442376 | tf_op jit(solution)/shard_map/ppermute | solution.py:455

commit v6 on v5

--- a/solution.py
+++ b/solution.py
@@ -11,6 +11,7 @@
 relaxation = 0.125
 
 VMEM_LIMIT = 24 * 2**20
+PAD = 16
 
 ANY = pl.BlockSpec(memory_space=pl.ANY)
 VMEM = pl.BlockSpec(memory_space=pltpu.VMEM)
@@ -157,10 +158,7 @@
         for buf, rows in pieces:
             for k, i in enumerate(rows):
                 for f in range(2):
-                    if isinstance(buf, tuple):
-                        self.where[f, i] = (buf[f], k * lev)
-                    else:
-                        self.where[f, i] = (buf, (f * len(rows) + k) * lev)
+                    self.where[f, i] = (buf, (f * len(rows) + k) * lev)
 
     def read(self, f, i):
         buf, at = self.where[f, i]
@@ -364,22 +362,23 @@
         (span(-3, 1), span(-2, 2), span(-3, 1), span(-2, 2), span(-1, 3)),
     )
     out = Rows(lev, (outer_rows, (0, 1)))
+    outer_rows[outer_rows.shape[0] - PAD :, :] = jnp.zeros((PAD, own.shape[1]), jnp.float32)
     for i in (0, 1):
         adjoint_solved(i, sign, moved[2], xs[1], factors, once[...], out)
 
 
-def inner_rows_kernel(side, own, x2, x2_in, b2, b2_in, once, inner_u, inner_t):
+def inner_rows_kernel(side, own, x2, x2_in, b2, b2_in, once, inner_rows):
     factors = Factors(own, None, None)
     lev = factors.lev
     third = Rows(lev, (x2, span(-2, 2)), (x2_in, span(2, 6)))
     back = Rows(lev, (b2, span(-1, 3)), (b2_in, span(3, 5)))
-    out = Rows(lev, ((inner_u, inner_t), (3, 2)))
+    out = Rows(lev, (inner_rows, (3, 2)))
     for i in (2, 3):
         adjoint_solved(i, side[0], back, third, factors, once[...], out)
 
 
 def inner_backward_kernel(
-    side, own, inner, x1, x1_in, outer_rows, inner_u, inner_t, b_u, b_t, once,
+    side, own, inner, x1, x1_in, outer_rows, inner_rows, b_inner, once,
     b0, done,
 ):
     sign = side[0]
@@ -387,9 +386,7 @@
     factors = Factors(own, None, inner)
     lev = state.lev
     second = Rows(lev, (x1, span(-3, 1)), (x1_in, span(1, 7)))
-    back = Rows(
-        lev, (outer_rows, (0, 1)), ((inner_u, inner_t), (3, 2)), ((b_u, b_t), (4, 5))
-    )
+    back = Rows(lev, (outer_rows, (0, 1)), (inner_rows, (3, 2)), (b_inner, (4, 5)))
     last = Rows(lev, (b0, span(1, 5)))
     for i in span(1, 5):
         adjoint_solved(i, sign, back, second, factors, once[...], last)
@@ -400,7 +397,7 @@
 
 
 def backward_kernel(
-    side, own, both_outer, x1, x1_in, outer_rows, inner_u, inner_t, b_outer, b0_in, done, once,
+    side, own, both_outer, x1, x1_in, outer_rows, inner_rows, b_outer, b0_in, done, once,
     packed, field,
     b0, sems,
 ):
@@ -410,9 +407,7 @@
     factors = Factors(own, outer, None)
     lev = state.lev
     second = Rows(lev, (x1, span(-3, 1)), (x1_in, span(1, 7)))
-    back = Rows(
-        lev, (outer_rows, (0, 1)), ((inner_u, inner_t), (3, 2)), (b_outer, (-1, -2))
-    )
+    back = Rows(lev, (outer_rows, (0, 1)), (inner_rows, (3, 2)), (b_outer, (-1, -2)))
     last = Rows(lev, (b0, (-1, 0)), (b0_in, span(1, 5)))
     ready = Rows(lev, (done, (2, 3)))
     results = Rows(lev, (packed, OWN))
@@ -505,9 +500,10 @@
         [],
         nbytes=2**18,
     )(side, state, state_inner, start, start_inner, once, twice)
+    outer_shape = f32(fields * 2 * lev + PAD, width)
     outer_rows, x1, x2, b2_outer = run(
         forward_kernel,
-        (rows_of(2), rows_of(4), rows_of(4), rows_of(4)),
+        (outer_shape, rows_of(4), rows_of(4), rows_of(4)),
         [SMEM] + [VMEM] * 10,
         (VMEM,) * 4,
         [buffer(4), buffer(4)],
@@ -515,33 +511,32 @@
     )(side, state, start, both_outer, x1_in, x2_in, t1, t2, b2, once, twice)
 
     b_outer = swap(outer_rows, across)
-    half = f32(2 * lev, width)
-    inner_u, inner_t = run(
+    inner_rows = run(
         inner_rows_kernel,
-        (half, half),
+        rows_of(2),
         [SMEM] + [VMEM] * 6,
+        VMEM,
+        [],
+        nbytes=0,
+    )(side, state, x2, x2_in, b2_outer, b2, once)
+    b_inner = swap(inner_rows, within)
+    b0, done = run(
+        inner_backward_kernel,
+        (rows_of(4), rows_of(2)),
+        [SMEM] + [VMEM] * 8,
         (VMEM, VMEM),
         [],
         nbytes=0,
-    )(side, state, x2, x2_in, b2_outer, b2, once)
-    b_u, b_t = swap(inner_u, within), swap(inner_t, within)
-    b0, done = run(
-        inner_backward_kernel,
-        (rows_of(4), rows_of(2)),
-        [SMEM] + [VMEM] * 10,
-        (VMEM, VMEM),
-        [],
-        nbytes=0,
-    )(side, state, state_inner, x1, x1_in, outer_rows, inner_u, inner_t, b_u, b_t, once)
+    )(side, state, state_inner, x1, x1_in, outer_rows, inner_rows, b_inner, once)
     packed, field = run(
         backward_kernel,
         (f32(high, width), f32(lev, fields, rows, width)),
-        [SMEM] + [VMEM] * 11,
+        [SMEM] + [VMEM] * 10,
         (VMEM, ANY),
         [buffer(2), dma((fields * rows,))],
         nbytes=2**20,
     )(
-        side, state, both_outer, x1, x1_in, outer_rows, inner_u, inner_t, b_outer, b0, done, once
+        side, state, both_outer, x1, x1_in, outer_rows, inner_rows, b_outer, b0, done, once
     )
 
     share = lax.all_to_all(
@@ -551,14 +546,13 @@
         share,
         share,
         (((1, 2), (1, 2)), ((), ())),
-        precision=lax.Precision.HIGHEST,
+        precision=lax.Precision.HIGH,
         preferred_element_type=jnp.float32,
-    )
+    ) * (1.0 / (high * width * tiles))
     row = jnp.sum(lax.all_to_all(products, "group", 0, 0, tiled=True), axis=0)
     spread = jnp.broadcast_to(row[None], (tiles, members))
     row = jnp.sum(lax.all_to_all(spread, "tile", 0, 0, tiled=True), axis=0)
-    gram = row[None] / (high * width * tiles)
-    return (field[None], gram)
+    return (field[None], row[None])
 
 
 def solution(mesh):

time: 99.7 us -> 97.2 us (0.975)
  starting transfers between devices: 19.4 us -> 17 us
    ppermute x6 -> x5, starting transfers between devices: 19.4 us -> 17 us  [swap(): return lax.ppermute(value, 'tile', pairs + [(j, i) for i, j in pairs])]
    ppermute x6 -> x5, waiting for transfers between devices: 2.57 us -> 3.14 us  [swap(): return lax.ppermute(value, 'tile', pairs + [(j, i) for i, j in pairs])]
  transfers between devices with their start and end apart: 6 -> 5, of which waited for: 3 -> 3; matrix products, arithmetic and copies ran while one was open for 0% -> 0% of each run, Pallas kernels for 6% -> 6%
where the time goes in v6:
time: 97.2 us; the launch traced here: 96.8 us
  blocking collectives  60.9 us (63%)
  starting transfers between devices  17 us (17%)
  Pallas kernels  12.5 us (13%)
  waiting for transfers between devices  3.14 us (3%)
  local copies, waits for them, and re-layouts  1.3 us (1%)
    all_to_all x1, blocking collectives, per_device(): lax.all_to_all(packed.reshape(members, high // members, width), 'group',...  28.5 us
    all_to_all x1, blocking collectives, per_device(): row = jnp.sum(lax.all_to_all(spread, 'tile', 0, 0, tiled=True), axis=0)  21.2 us
    ppermute x5, starting transfers between devices, swap(): return lax.ppermute(value, 'tile', pairs + [(j, i) for i, j in pairs])  17 us
    all_to_all x1, blocking collectives, per_device(): row = jnp.sum(lax.all_to_all(products, 'group', 0, 0, tiled=True), axis=0)  11.3 us
    ppermute x5, waiting for transfers between devices, swap(): return lax.ppermute(value, 'tile', pairs + [(j, i) for i, j in pairs])  3.14 us
    pallas_call x1, Pallas kernels, per_device(): run(inner_forward_kernel, (rows_of(6), rows_of(4), rows_of(6), rows_of(4)...  2.96 us
    pallas_call x1, Pallas kernels, per_device(): run(forward_kernel, (outer_shape, rows_of(4), rows_of(4), rows_of(4)), [S...  2.9 us
    pallas_call x1, Pallas kernels, per_device(): run(pack_kernel, f32(2 * high + 2 * rows, width), [SMEM] + [ANY] * 4, ANY...  2.46 us
  transfers between devices with their start and end apart: 5, of which 3 were waited for; matrix products, arithmetic and copies ran while one was open for 0% of the time, Pallas kernels for 6%

profile of v6, /device:TPU:1, one launch (start us, length us, event | category | flops | bytes accessed | tf_op | source)
XLA Modules:
  0.0 96.8 jit_solution(13813024048721365937)
XLA Ops:
  0.6 2.5 %shard_map.68.both = f32[776,384]{1,0:T(8,128)} custom-call(f32[1]{0:T(128)} %bitcast.side, f32[48,2,4,384]{3,2,1,0:T(4,128)} %x.1, f32[48,2,4,384]{3,2,1,0:T(4,128)} %bitcast.13, s32[4,384]{1,0:T(4,128)} %land.1, s32[4,384]{1,0:T(4,128)} %relax.1), custom_call_target="tpu_custom_call" | custom-call | bytes 1048576 | tf_op jit(solution)/shard_map/pallas_call | solution.py:458
  3.1 4.6 %collective-permute-start = (f32[776,384]{1,0:T(8,128)}, f32[776,384]{1,0:T(8,128)S(1)}, u32[]{:S(2)}, u32[]{:S(2)}) collective-permute-start(f32[776,384]{1,0:T(8,128)} %shard_map.68.both), channel_id=1, source_target_pairs={{1,2},{3,4},{5,6},{7,8},{9,10},{11,12},{13,14},{15,16},{17,18},{19... | collective-permute-start | bytes 3575816 | tf_op jit(solution)/shard_map/ppermute | solution.py:450
  7.7 0.0 copy-start
  7.7 1.3 %copy-done = f32[776,384]{1,0:T(8,128)S(1)} copy-done((f32[776,384]{1,0:T(8,128)S(1)}, f32[776,384]{1,0:T(8,128)}, u32[]{:S(2)}) %copy-start) | copy-done | bytes 1191960
  9.0 0.0 copy-start.1
  9.0 0.3 shard_map.69
  9.3 4.9 %collective-permute-start.1 = (f32[392,384]{1,0:T(8,128)S(1)}, f32[392,384]{1,0:T(8,128)S(1)}, u32[]{:S(2)}, u32[]{:S(2)}) collective-permute-start(f32[392,384]{1,0:T(8,128)S(1)} %get-tuple-element.19.own), channel_id=1, source_target_pairs={{0,1},{2,3},{4,5},{6,7},{8,9},{10,11},{12,13},{14,15},{16,17},{18,... | collective-permute-start | bytes 1806344 | tf_op jit(solution)/shard_map/ppermute | solution.py:450
  14.2 1.9 %collective-permute-start.2 = (f32[384,384]{1,0:T(8,128)S(1)}, f32[384,384]{1,0:T(8,128)S(1)}, u32[]{:S(2)}, u32[]{:S(2)}) collective-permute-start(f32[384,384]{1,0:T(8,128)S(1)} %get-tuple-element.20.p_own), channel_id=1, source_target_pairs={{0,1},{2,3},{4,5},{6,7},{8,9},{10,11},{12,13},{14,15},{16,17},{18,... | collective-permute-start | bytes 1769480 | tf_op jit(solution)/shard_map/ppermute | solution.py:450
  16.1 0.0 copy-done.1
  16.1 1.2 %shard_map.70 = (bf16[48,144]{1,0:T(8,128)(2,1)S(1)}, bf16[48,144]{1,0:T(8,128)(2,1)S(1)}) custom-call(f32[48]{0:T(128)S(1)} %copy-done.1), custom_call_target="tpu_custom_call" | custom-call | bytes 262144 | tf_op jit(solution)/shard_map/pallas_call | solution.py:486
  17.4 0.7 collective-permute-done.2.p_inner
  18.1 0.0 collective-permute-done.1.inner
  18.1 3.0 %shard_map.71 = (f32[576,384]{1,0:T(8,128)S(1)}, f32[384,384]{1,0:T(8,128)S(1)}, f32[576,384]{1,0:T(8,128)S(1)}, f32[384,384]{1,0:T(8,128)S(1)}, f32[192,384]{1,0:T(8,128)S(1)}) custom-call(f32[1]{0:T(128)} %bitcast.side, f32[392,384]{1,0:T(8,128)S(1)} %get-tuple-element.19.own, f32[392,384]{1,0:T(8,128)S(1)} %collective-permute-done.1.inner, ...), custom_call_target="tpu_custom_call" | custom-call | bytes 262144 | tf_op jit(solution)/shard_map/pallas_call | solution.py:495
  21.1 0.8 collective-permute-done.both_outer
  21.9 2.9 %shard_map.72 = (f32[208,384]{1,0:T(8,128)S(1)}, f32[384,384]{1,0:T(8,128)S(1)}, f32[384,384]{1,0:T(8,128)S(1)}, f32[384,384]{1,0:T(8,128)S(1)}) custom-call(f32[1]{0:T(128)} %bitcast.side, f32[392,384]{1,0:T(8,128)S(1)} %get-tuple-element.19.own, f32[384,384]{1,0:T(8,128)S(1)} %get-tuple-element.20.p_own, f32[776,384]{1,0:T(8,128)S(1)} %collective-permute-done.both_outer, ...), custom_call_target="tpu_custom_call" | custom-call | bytes 1048576 | tf_op jit(solution)/shard_map/pallas_call | solution.py:504
  24.8 3.6 %collective-permute-start.3 = (f32[208,384]{1,0:T(8,128)S(1)}, f32[208,384]{1,0:T(8,128)S(1)}, u32[]{:S(2)}, u32[]{:S(2)}) collective-permute-start(f32[208,384]{1,0:T(8,128)S(1)} %get-tuple-element.29.outer_rows), channel_id=1, source_target_pairs={{1,2},{3,4},{5,6},{7,8},{9,10},{11,12},{13,14},{15,16},{17,18},{19... | collective-permute-start | bytes 958472 | tf_op jit(solution)/shard_map/ppermute | solution.py:450
  28.5 0.4 shard_map.73.inner_rows
  28.9 1.9 %collective-permute-start.4 = (f32[192,384]{1,0:T(8,128)S(1)}, f32[192,384]{1,0:T(8,128)S(1)}, u32[]{:S(2)}, u32[]{:S(2)}) collective-permute-start(f32[192,384]{1,0:T(8,128)S(1)} %shard_map.73.inner_rows), channel_id=1, source_target_pairs={{0,1},{2,3},{4,5},{6,7},{8,9},{10,11},{12,13},{14,15},{16,17},{18,... | collective-permute-start | bytes 884744 | tf_op jit(solution)/shard_map/ppermute | solution.py:450
  30.8 1.5 %collective-permute-done.4.b_inner = f32[192,384]{1,0:T(8,128)S(1)} collective-permute-done((f32[192,384]{1,0:T(8,128)S(1)}, f32[192,384]{1,0:T(8,128)S(1)}, u32[]{:S(2)}, u32[]{:S(2)}) %collective-permute-start.4) | collective-permute-done | bytes 294944 | tf_op jit(solution)/shard_map/ppermute | solution.py:450
  32.4 0.8 shard_map.74
  33.2 0.0 collective-permute-done.3.b_outer
  33.2 1.4 %shard_map.75 = (f32[384,384]{1,0:T(8,128)S(1)}, f32[48,2,4,384]{3,2,1,0:T(4,128)}) custom-call(f32[1]{0:T(128)} %bitcast.side, f32[392,384]{1,0:T(8,128)S(1)} %get-tuple-element.19.own, f32[776,384]{1,0:T(8,128)S(1)} %collective-permute-done.both_outer, f32[384,384]{1,0:T(8,128)S(1)} %get-tuple-element.28.x1, f32[576,384]{1,0:T(8,128)S(1)} %get-tuple-element.23.x1_in, ...), custom_call_target="tpu_custom_call" | custom-call | bytes 1048576 | tf_op jit(solution)/shard_map/pallas_call | solution.py:531
  34.7 28.5 %all_to_all.20 = f32[16,24,384]{2,1,0:T(8,128)S(1)} all-to-all(f32[16,24,384]{2,1,0:T(8,128)S(1)} %bitcast.12), channel_id=1, replica_groups=mesh['group'=16,'tile'=32] {'group'}, dimensions={0} | all-to-all | bytes 1179648 | tf_op jit(solution)/shard_map/all_to_all | solution.py:542
  63.2 0.5 fusion
  63.8 11.3 %all_to_all.21 = f32[16,1,16]{2,1,0:T(1,128)S(1)} all-to-all(f32[16,1,16]{2,1,0:T(1,128)S(1)} %bitcast.14), channel_id=1, replica_groups=mesh['group'=16,'tile'=32] {'group'}, dimensions={0} | all-to-all | bytes 2048 | tf_op jit(solution)/shard_map/all_to_all | solution.py:552
  75.1 21.2 %all_to_all.22 = f32[32,1,16]{2,1,0:T(1,128)S(1)} all-to-all(f32[32,1,16]{2,1,0:T(1,128)S(1)} %broadcast_in_dim.17), channel_id=1, replica_groups=mesh['group'=16,'tile'=32] {'tile'}, dimensions={0} | all-to-all | bytes 4096 | tf_op jit(solution)/shard_map/all_to_all | solution.py:554
  96.2 0.6 reduce_sum.19
  (2 shorter events, 0.0 us)
Async XLA Ops:
  3.1 18.8 %collective-permute-start = (f32[776,384]{1,0:T(8,128)}, f32[776,384]{1,0:T(8,128)S(1)}, u32[]{:S(2)}, u32[]{:S(2)}) collective-permute-start(f32[776,384]{1,0:T(8,128)} %shard_map.68.both), channel_id=1, source_target_pairs={{1,2},{3,4},{5,6},{7,8},{9,10},{11,12},{13,14},{15,16},{17,18},{19... | collective-permute-start | bytes 3575816 | tf_op jit(solution)/shard_map/ppermute | solution.py:450
  7.7 1.3 %copy-start = (f32[776,384]{1,0:T(8,128)S(1)}, f32[776,384]{1,0:T(8,128)}, u32[]{:S(2)}) copy-start(f32[776,384]{1,0:T(8,128)} %shard_map.68.both) | copy-start | bytes 3575812
  9.0 7.1 %copy-start.1 = (f32[48]{0:T(128)S(1)}, f32[48]{0:T(128)}, u32[]{:S(2)}) copy-start(f32[48]{0:T(128)} %mix.1) | copy-start | bytes 580
  9.3 8.8 %collective-permute-start.1 = (f32[392,384]{1,0:T(8,128)S(1)}, f32[392,384]{1,0:T(8,128)S(1)}, u32[]{:S(2)}, u32[]{:S(2)}) collective-permute-start(f32[392,384]{1,0:T(8,128)S(1)} %get-tuple-element.19.own), channel_id=1, source_target_pairs={{0,1},{2,3},{4,5},{6,7},{8,9},{10,11},{12,13},{14,15},{16,17},{18,... | collective-permute-start | bytes 1806344 | tf_op jit(solution)/shard_map/ppermute | solution.py:450
  14.2 3.9 %collective-permute-start.2 = (f32[384,384]{1,0:T(8,128)S(1)}, f32[384,384]{1,0:T(8,128)S(1)}, u32[]{:S(2)}, u32[]{:S(2)}) collective-permute-start(f32[384,384]{1,0:T(8,128)S(1)} %get-tuple-element.20.p_own), channel_id=1, source_target_pairs={{0,1},{2,3},{4,5},{6,7},{8,9},{10,11},{12,13},{14,15},{16,17},{18,... | collective-permute-start | bytes 1769480 | tf_op jit(solution)/shard_map/ppermute | solution.py:450
  24.8 8.4 %collective-permute-start.3 = (f32[208,384]{1,0:T(8,128)S(1)}, f32[208,384]{1,0:T(8,128)S(1)}, u32[]{:S(2)}, u32[]{:S(2)}) collective-permute-start(f32[208,384]{1,0:T(8,128)S(1)} %get-tuple-element.29.outer_rows), channel_id=1, source_target_pairs={{1,2},{3,4},{5,6},{7,8},{9,10},{11,12},{13,14},{15,16},{17,18},{19... | collective-permute-start | bytes 958472 | tf_op jit(solution)/shard_map/ppermute | solution.py:450
  28.9 3.5 %collective-permute-start.4 = (f32[192,384]{1,0:T(8,128)S(1)}, f32[192,384]{1,0:T(8,128)S(1)}, u32[]{:S(2)}, u32[]{:S(2)}) collective-permute-start(f32[192,384]{1,0:T(8,128)S(1)} %shard_map.73.inner_rows), channel_id=1, source_target_pairs={{0,1},{2,3},{4,5},{6,7},{8,9},{10,11},{12,13},{14,15},{16,17},{18,... | collective-permute-start | bytes 884744 | tf_op jit(solution)/shard_map/ppermute | solution.py:450

commit v7 on v6

--- a/solution.py
+++ b/solution.py
@@ -11,7 +11,7 @@
 relaxation = 0.125
 
 VMEM_LIMIT = 24 * 2**20
-PAD = 16
+PAD = 8
 
 ANY = pl.BlockSpec(memory_space=pl.ANY)
 VMEM = pl.BlockSpec(memory_space=pltpu.VMEM)
@@ -256,16 +256,17 @@
     lev = x.lev
     keep, drag = factors.keep(i), factors.drag(i)
     near = tiled(diffusion * keep, lev)
-    wind = side * x.read(0, i)
-    du = side * d.read(0, i)
+    wind = x.read(0, i)
+    du = d.read(0, i)
+    signed = tiled((diffusion * side) * keep, lev)
     parts = []
     for f in range(2):
         centre = d.read(f, i)
         up, down = d.read(f, i + 1), d.read(f, i - 1)
         slope = x.read(f, i + 1) - x.read(f, i - 1)
         own = tiled(keep * (0.6 - drag) if f == 0 else 0.6 * keep, lev)
-        around = (up + down) + beside(centre) - wind * (up - down) - du * slope
-        parts.append(own * centre + near * around)
+        moved = wind * (up - down) + du * slope
+        parts.append(own * centre + near * ((up + down) + beside(centre)) - signed * moved)
     for f, value in enumerate(solve(matrix, *parts)):
         out.write(f, i, value * tiled(keep, lev) if damp else value)
 
@@ -298,14 +299,12 @@
 
 
 def forward(side, state, start, factors, xs, moved, once, twice, ranges):
-    for i in ranges[0]:
+    for i, j in zip(ranges[0], ranges[2]):
         state_row(i, side, state, factors, once, xs[0])
-    for i in ranges[1]:
+        tangent_row(j, side, start, state, factors, once, moved[0], False)
+    for i, j in zip(ranges[1], ranges[3]):
         state_row(i, side, xs[0], factors, once, xs[1])
-    for i in ranges[2]:
-        tangent_row(i, side, start, state, factors, once, moved[0], False)
-    for i in ranges[3]:
-        tangent_row(i, side, moved[0], xs[0], factors, once, moved[1], False)
+        tangent_row(j, side, moved[0], xs[0], factors, once, moved[1], False)
     for i in ranges[4]:
         tangent_row(i, side, moved[1], xs[1], factors, twice, moved[2], True)
 

time: 97.2 us -> 97.3 us (level)
  no operation moved by 1% of the time
where the time goes in v7:
time: 97.3 us; the launch traced here: 96.9 us
  blocking collectives  61 us (63%)
  starting transfers between devices  17 us (17%)
  Pallas kernels  12.4 us (13%)
  waiting for transfers between devices  3.29 us (3%)
  local copies, waits for them, and re-layouts  1.3 us (1%)
    all_to_all x1, blocking collectives, per_device(): lax.all_to_all(packed.reshape(members, high // members, width), 'group',...  28.5 us
    all_to_all x1, blocking collectives, per_device(): row = jnp.sum(lax.all_to_all(spread, 'tile', 0, 0, tiled=True), axis=0)  21.2 us
    ppermute x5, starting transfers between devices, swap(): return lax.ppermute(value, 'tile', pairs + [(j, i) for i, j in pairs])  17 us
    all_to_all x1, blocking collectives, per_device(): row = jnp.sum(lax.all_to_all(products, 'group', 0, 0, tiled=True), axis=0)  11.3 us
    ppermute x5, waiting for transfers between devices, swap(): return lax.ppermute(value, 'tile', pairs + [(j, i) for i, j in pairs])  3.29 us
    pallas_call x1, Pallas kernels, per_device(): run(forward_kernel, (outer_shape, rows_of(4), rows_of(4), rows_of(4)), [S...  2.88 us
    pallas_call x1, Pallas kernels, per_device(): run(inner_forward_kernel, (rows_of(6), rows_of(4), rows_of(6), rows_of(4)...  2.81 us
    pallas_call x1, Pallas kernels, per_device(): run(pack_kernel, f32(2 * high + 2 * rows, width), [SMEM] + [ANY] * 4, ANY...  2.46 us
  transfers between devices with their start and end apart: 5, of which 3 were waited for; matrix products, arithmetic and copies ran while one was open for 0% of the time, Pallas kernels for 6%

profile of v7, /device:TPU:1, one launch (start us, length us, event | category | flops | bytes accessed | tf_op | source)
XLA Modules:
  0.0 96.9 jit_solution(608556883788005355)
XLA Ops:
  0.6 2.5 %shard_map.68.both = f32[776,384]{1,0:T(8,128)} custom-call(f32[1]{0:T(128)} %bitcast.side, f32[48,2,4,384]{3,2,1,0:T(4,128)} %x.1, f32[48,2,4,384]{3,2,1,0:T(4,128)} %bitcast.13, s32[4,384]{1,0:T(4,128)} %land.1, s32[4,384]{1,0:T(4,128)} %relax.1), custom_call_target="tpu_custom_call" | custom-call | bytes 1048576 | tf_op jit(solution)/shard_map/pallas_call | solution.py:457
  3.1 4.6 %collective-permute-start = (f32[776,384]{1,0:T(8,128)}, f32[776,384]{1,0:T(8,128)S(1)}, u32[]{:S(2)}, u32[]{:S(2)}) collective-permute-start(f32[776,384]{1,0:T(8,128)} %shard_map.68.both), channel_id=1, source_target_pairs={{1,2},{3,4},{5,6},{7,8},{9,10},{11,12},{13,14},{15,16},{17,18},{19... | collective-permute-start | bytes 3575816 | tf_op jit(solution)/shard_map/ppermute | solution.py:449
  7.7 0.0 copy-start
  7.7 1.3 %copy-done = f32[776,384]{1,0:T(8,128)S(1)} copy-done((f32[776,384]{1,0:T(8,128)S(1)}, f32[776,384]{1,0:T(8,128)}, u32[]{:S(2)}) %copy-start) | copy-done | bytes 1191960
  9.0 0.0 copy-start.1
  9.0 0.3 shard_map.69
  9.3 4.9 %collective-permute-start.1 = (f32[392,384]{1,0:T(8,128)S(1)}, f32[392,384]{1,0:T(8,128)S(1)}, u32[]{:S(2)}, u32[]{:S(2)}) collective-permute-start(f32[392,384]{1,0:T(8,128)S(1)} %get-tuple-element.19.own), channel_id=1, source_target_pairs={{0,1},{2,3},{4,5},{6,7},{8,9},{10,11},{12,13},{14,15},{16,17},{18,... | collective-permute-start | bytes 1806344 | tf_op jit(solution)/shard_map/ppermute | solution.py:449
  14.2 1.9 %collective-permute-start.2 = (f32[384,384]{1,0:T(8,128)S(1)}, f32[384,384]{1,0:T(8,128)S(1)}, u32[]{:S(2)}, u32[]{:S(2)}) collective-permute-start(f32[384,384]{1,0:T(8,128)S(1)} %get-tuple-element.20.p_own), channel_id=1, source_target_pairs={{0,1},{2,3},{4,5},{6,7},{8,9},{10,11},{12,13},{14,15},{16,17},{18,... | collective-permute-start | bytes 1769480 | tf_op jit(solution)/shard_map/ppermute | solution.py:449
  16.1 0.0 copy-done.1
  16.1 1.2 %shard_map.70 = (bf16[48,144]{1,0:T(8,128)(2,1)S(1)}, bf16[48,144]{1,0:T(8,128)(2,1)S(1)}) custom-call(f32[48]{0:T(128)S(1)} %copy-done.1), custom_call_target="tpu_custom_call" | custom-call | bytes 262144 | tf_op jit(solution)/shard_map/pallas_call | solution.py:485
  17.4 0.7 collective-permute-done.2.p_inner
  18.1 0.0 collective-permute-done.1.inner
  18.1 2.8 %shard_map.71 = (f32[576,384]{1,0:T(8,128)S(1)}, f32[384,384]{1,0:T(8,128)S(1)}, f32[576,384]{1,0:T(8,128)S(1)}, f32[384,384]{1,0:T(8,128)S(1)}, f32[192,384]{1,0:T(8,128)S(1)}) custom-call(f32[1]{0:T(128)} %bitcast.side, f32[392,384]{1,0:T(8,128)S(1)} %get-tuple-element.19.own, f32[392,384]{1,0:T(8,128)S(1)} %collective-permute-done.1.inner, ...), custom_call_target="tpu_custom_call" | custom-call | bytes 262144 | tf_op jit(solution)/shard_map/pallas_call | solution.py:494
  20.9 1.0 %collective-permute-done.both_outer = f32[776,384]{1,0:T(8,128)S(1)} collective-permute-done((f32[776,384]{1,0:T(8,128)}, f32[776,384]{1,0:T(8,128)S(1)}, u32[]{:S(2)}, u32[]{:S(2)}) %collective-permute-start) | collective-permute-done | bytes 1191968 | tf_op jit(solution)/shard_map/ppermute | solution.py:449
  21.9 2.9 %shard_map.72 = (f32[200,384]{1,0:T(8,128)S(1)}, f32[384,384]{1,0:T(8,128)S(1)}, f32[384,384]{1,0:T(8,128)S(1)}, f32[384,384]{1,0:T(8,128)S(1)}) custom-call(f32[1]{0:T(128)} %bitcast.side, f32[392,384]{1,0:T(8,128)S(1)} %get-tuple-element.19.own, f32[384,384]{1,0:T(8,128)S(1)} %get-tuple-element.20.p_own, f32[776,384]{1,0:T(8,128)S(1)} %collective-permute-done.both_outer, ...), custom_call_target="tpu_custom_call" | custom-call | bytes 1048576 | tf_op jit(solution)/shard_map/pallas_call | solution.py:503
  24.8 3.6 %collective-permute-start.3 = (f32[200,384]{1,0:T(8,128)S(1)}, f32[200,384]{1,0:T(8,128)S(1)}, u32[]{:S(2)}, u32[]{:S(2)}) collective-permute-start(f32[200,384]{1,0:T(8,128)S(1)} %get-tuple-element.29.outer_rows), channel_id=1, source_target_pairs={{1,2},{3,4},{5,6},{7,8},{9,10},{11,12},{13,14},{15,16},{17,18},{19... | collective-permute-start | bytes 921608 | tf_op jit(solution)/shard_map/ppermute | solution.py:449
  28.5 0.4 shard_map.73.inner_rows
  28.9 1.9 %collective-permute-start.4 = (f32[192,384]{1,0:T(8,128)S(1)}, f32[192,384]{1,0:T(8,128)S(1)}, u32[]{:S(2)}, u32[]{:S(2)}) collective-permute-start(f32[192,384]{1,0:T(8,128)S(1)} %shard_map.73.inner_rows), channel_id=1, source_target_pairs={{0,1},{2,3},{4,5},{6,7},{8,9},{10,11},{12,13},{14,15},{16,17},{18,... | collective-permute-start | bytes 884744 | tf_op jit(solution)/shard_map/ppermute | solution.py:449
  30.8 1.5 %collective-permute-done.4.b_inner = f32[192,384]{1,0:T(8,128)S(1)} collective-permute-done((f32[192,384]{1,0:T(8,128)S(1)}, f32[192,384]{1,0:T(8,128)S(1)}, u32[]{:S(2)}, u32[]{:S(2)}) %collective-permute-start.4) | collective-permute-done | bytes 294944 | tf_op jit(solution)/shard_map/ppermute | solution.py:449
  32.4 0.8 shard_map.74
  33.2 0.0 collective-permute-done.3.b_outer
  33.2 1.5 %shard_map.75 = (f32[384,384]{1,0:T(8,128)S(1)}, f32[48,2,4,384]{3,2,1,0:T(4,128)}) custom-call(f32[1]{0:T(128)} %bitcast.side, f32[392,384]{1,0:T(8,128)S(1)} %get-tuple-element.19.own, f32[776,384]{1,0:T(8,128)S(1)} %collective-permute-done.both_outer, f32[384,384]{1,0:T(8,128)S(1)} %get-tuple-element.28.x1, f32[576,384]{1,0:T(8,128)S(1)} %get-tuple-element.23.x1_in, ...), custom_call_target="tpu_custom_call" | custom-call | bytes 1048576 | tf_op jit(solution)/shard_map/pallas_call | solution.py:530
  34.7 28.5 %all_to_all.20 = f32[16,24,384]{2,1,0:T(8,128)S(1)} all-to-all(f32[16,24,384]{2,1,0:T(8,128)S(1)} %bitcast.12), channel_id=1, replica_groups=mesh['group'=16,'tile'=32] {'group'}, dimensions={0} | all-to-all | bytes 1179648 | tf_op jit(solution)/shard_map/all_to_all | solution.py:541
  63.3 0.5 fusion
  63.8 11.3 %all_to_all.21 = f32[16,1,16]{2,1,0:T(1,128)S(1)} all-to-all(f32[16,1,16]{2,1,0:T(1,128)S(1)} %bitcast.14), channel_id=1, replica_groups=mesh['group'=16,'tile'=32] {'group'}, dimensions={0} | all-to-all | bytes 2048 | tf_op jit(solution)/shard_map/all_to_all | solution.py:551
  75.1 21.2 %all_to_all.22 = f32[32,1,16]{2,1,0:T(1,128)S(1)} all-to-all(f32[32,1,16]{2,1,0:T(1,128)S(1)} %broadcast_in_dim.17), channel_id=1, replica_groups=mesh['group'=16,'tile'=32] {'tile'}, dimensions={0} | all-to-all | bytes 4096 | tf_op jit(solution)/shard_map/all_to_all | solution.py:553
  96.3 0.6 reduce_sum.19
  (2 shorter events, 0.0 us)
Async XLA Ops:
  3.1 18.8 %collective-permute-start = (f32[776,384]{1,0:T(8,128)}, f32[776,384]{1,0:T(8,128)S(1)}, u32[]{:S(2)}, u32[]{:S(2)}) collective-permute-start(f32[776,384]{1,0:T(8,128)} %shard_map.68.both), channel_id=1, source_target_pairs={{1,2},{3,4},{5,6},{7,8},{9,10},{11,12},{13,14},{15,16},{17,18},{19... | collective-permute-start | bytes 3575816 | tf_op jit(solution)/shard_map/ppermute | solution.py:449
  7.7 1.3 %copy-start = (f32[776,384]{1,0:T(8,128)S(1)}, f32[776,384]{1,0:T(8,128)}, u32[]{:S(2)}) copy-start(f32[776,384]{1,0:T(8,128)} %shard_map.68.both) | copy-start | bytes 3575812
  9.0 7.1 %copy-start.1 = (f32[48]{0:T(128)S(1)}, f32[48]{0:T(128)}, u32[]{:S(2)}) copy-start(f32[48]{0:T(128)} %mix.1) | copy-start | bytes 580
  9.3 8.8 %collective-permute-start.1 = (f32[392,384]{1,0:T(8,128)S(1)}, f32[392,384]{1,0:T(8,128)S(1)}, u32[]{:S(2)}, u32[]{:S(2)}) collective-permute-start(f32[392,384]{1,0:T(8,128)S(1)} %get-tuple-element.19.own), channel_id=1, source_target_pairs={{0,1},{2,3},{4,5},{6,7},{8,9},{10,11},{12,13},{14,15},{16,17},{18,... | collective-permute-start | bytes 1806344 | tf_op jit(solution)/shard_map/ppermute | solution.py:449
  14.2 3.9 %collective-permute-start.2 = (f32[384,384]{1,0:T(8,128)S(1)}, f32[384,384]{1,0:T(8,128)S(1)}, u32[]{:S(2)}, u32[]{:S(2)}) collective-permute-start(f32[384,384]{1,0:T(8,128)S(1)} %get-tuple-element.20.p_own), channel_id=1, source_target_pairs={{0,1},{2,3},{4,5},{6,7},{8,9},{10,11},{12,13},{14,15},{16,17},{18,... | collective-permute-start | bytes 1769480 | tf_op jit(solution)/shard_map/ppermute | solution.py:449
  24.8 8.4 %collective-permute-start.3 = (f32[200,384]{1,0:T(8,128)S(1)}, f32[200,384]{1,0:T(8,128)S(1)}, u32[]{:S(2)}, u32[]{:S(2)}) collective-permute-start(f32[200,384]{1,0:T(8,128)S(1)} %get-tuple-element.29.outer_rows), channel_id=1, source_target_pairs={{1,2},{3,4},{5,6},{7,8},{9,10},{11,12},{13,14},{15,16},{17,18},{19... | collective-permute-start | bytes 921608 | tf_op jit(solution)/shard_map/ppermute | solution.py:449
  28.9 3.5 %collective-permute-start.4 = (f32[192,384]{1,0:T(8,128)S(1)}, f32[192,384]{1,0:T(8,128)S(1)}, u32[]{:S(2)}, u32[]{:S(2)}) collective-permute-start(f32[192,384]{1,0:T(8,128)S(1)} %shard_map.73.inner_rows), channel_id=1, source_target_pairs={{0,1},{2,3},{4,5},{6,7},{8,9},{10,11},{12,13},{14,15},{16,17},{18,... | collective-permute-start | bytes 884744 | tf_op jit(solution)/shard_map/ppermute | solution.py:449
